TPU v7x, 32 devices: a whole 2x2x4 slice. The times are simulated.
32 devices in a mesh: rep: 2 (over y), fsdp: 16 (over z, x, core).
Axes of the slice: x: 2, y: 2, z: 4, core: 2. Of those that a mesh axis runs over, the one named last changes fastest.
Arguments:
- pixels_a: bfloat16 [32, 3, 160, 160], P(('rep', 'fsdp')), may hold values from -6 to 6
- pixels_b: bfloat16 [32, 3, 240, 240], P(('rep', 'fsdp')), may hold values from -6 to 6
- pixels_c: bfloat16 [32, 3, 384, 384], P(('rep', 'fsdp')), may hold values from -6 to 6
- resize_a: float32 [100, 1024], replicated, may hold values from -0.1875 to 0.1875
- resize_b: float32 [144, 1024], replicated, may hold values from -0.1875 to 0.1875
- resize_c: float32 [256, 1024], replicated, may hold values from -0.1875 to 0.1875
- posmap_a: float32 [256, 49], replicated, may hold values from 0 to 0.08
- posmap_b: float32 [400, 49], replicated, may hold values from 0 to 0.08
- posmap_c: float32 [576, 49], replicated, may hold values from 0 to 0.08
- base_kernel: bfloat16 [3, 1024, 768], P(None, None, 'fsdp'), may hold values from -0.21875 to 0.21875
- patch_bias: bfloat16 [768], P('fsdp'), may hold values from -3 to 3
- posemb: bfloat16 [49, 768], P(None, 'fsdp'), may hold values from -12 to 12
- ln1_gain: bfloat16 [768], P('fsdp'), may hold values from 0.099609375 to 1.8984375
- ln1_bias: bfloat16 [768], P('fsdp'), may hold values from -2 to 2
- qkv_weight: bfloat16 [768, 2304], P('fsdp'), may hold values from -0.21875 to 0.21875
- qv_bias: bfloat16 [2, 768], P(None, 'fsdp'), may hold values from -3 to 3
- out_weight: bfloat16 [768, 768], P('fsdp'), may hold values from -0.875 to 0.875
- out_bias: bfloat16 [768], P('fsdp'), may hold values from -2 to 2
- ln2_gain: bfloat16 [768], P('fsdp'), may hold values from 0.099609375 to 1.8984375
- ln2_bias: bfloat16 [768], P('fsdp'), may hold values from -2 to 2
- up_weight: bfloat16 [768, 3072], P('fsdp'), may hold values from -0.21875 to 0.21875
- up_bias: bfloat16 [3072], P('fsdp'), may hold values from -3 to 3
- down_weight: bfloat16 [3072, 768], P('fsdp'), may hold values from -0.109375 to 0.109375
- down_bias: bfloat16 [768], P('fsdp'), may hold values from -2 to 2
- cotangent_a: bfloat16 [32, 256, 768], P(('rep', 'fsdp')), may hold values from -6 to 6
- cotangent_b: bfloat16 [32, 400, 768], P(('rep', 'fsdp')), may hold values from -6 to 6
- cotangent_c: bfloat16 [32, 576, 768], P(('rep', 'fsdp')), may hold values from -6 to 6
Outputs:
- out_a: bfloat16 [32, 256, 768], P(('rep', 'fsdp'))
- out_b: bfloat16 [32, 400, 768], P(('rep', 'fsdp'))
- out_c: bfloat16 [32, 576, 768], P(('rep', 'fsdp'))
- pixel_grad_a: bfloat16 [32, 3, 160, 160], P(('rep', 'fsdp'))
- pixel_grad_b: bfloat16 [32, 3, 240, 240], P(('rep', 'fsdp'))
- pixel_grad_c: bfloat16 [32, 3, 384, 384], P(('rep', 'fsdp'))
- base_kernel_grad: float32 [3, 1024, 768], P(None, None, 'fsdp')
- patch_bias_grad: float32 [768], P('fsdp')
- posemb_grad: float32 [49, 768], P(None, 'fsdp')
- ln1_gain_grad: float32 [768], P('fsdp')
- ln1_bias_grad: float32 [768], P('fsdp')
- qkv_weight_grad: float32 [768, 2304], P('fsdp')
- qv_bias_grad: float32 [2, 768], P(None, 'fsdp')
- out_weight_grad: float32 [768, 768], P('fsdp')
- out_bias_grad: float32 [768], P('fsdp')
- ln2_gain_grad: float32 [768], P('fsdp')
- ln2_bias_grad: float32 [768], P('fsdp')
- up_weight_grad: float32 [768, 3072], P('fsdp')
- up_bias_grad: float32 [3072], P('fsdp')
- down_weight_grad: float32 [3072, 768], P('fsdp')
- down_bias_grad: float32 [768], P('fsdp')
All inputs are finite; a program needn't handle non-finite values.
Results may differ from a plain program's by a relative error of at most 0.013.
Values may be sent and summed in bfloat16 or wider, within the bound.
No kernel may reach another device: no remote copies, remote signals or barrier semaphores. Data moves between devices by JAX's collectives and lax.ppermute only.
A program may use at most 256 MiB of HBM per device.

v0:
```python
import functools
import math

import jax
import jax.numpy as jnp
from jax import lax
from jax.experimental import pallas as pl
from jax.experimental.pallas import tpu as pltpu
from jax.sharding import PartitionSpec as P

HEADS = 12
HEAD = 64
SIDES = (10, 12, 16)
SLOT = 16
F32 = jnp.float32
BF16 = jnp.bfloat16
BRIEF = pl.CostEstimate(flops=1, bytes_accessed=1, transcendentals=0)


def swap(value, axis, size, bit):
    return lax.ppermute(value, axis, [(i, i ^ bit) for i in range(size)])


def after(first, *rest):
    return lax.optimization_barrier((first, *rest))


class Gather:
    def __init__(self, shard, where, count, steps, split=False):
        self.count, self.split, self.columns = count, split, shard.shape[1]
        if split:
            width = shard.shape[1] // 2
            shard = lax.dynamic_slice_in_dim(shard, where[1] * width, width, 1)
        self.held = [(shard[None], [0])]
        self.steps = list(steps) + (["rep"] if split else []) + ["core"]
        self.step = None
        self.pieces = []
        self.ready = [shard[None]]

    def prepare(self):
        if not self.steps:
            self.ready = []
            return
        if len(self.held) > 1 and len(self.held[0]) == 2:
            offsets = [o for _, offsets in self.held for o in offsets]
            self.held = [(join([blocks for blocks, _ in self.held]), offsets)]
        self.ready = [blocks for blocks, *_ in self.held]

    def renew(self, ready):
        if ready:
            self.held = [(blocks, *h[1:]) for blocks, h in zip(ready, self.held)]
        self.ready = ready

    def send(self):
        self.step, self.steps = self.steps[0], self.steps[1:]
        if self.step in ("rep", "core"):
            axis, size = ("rep", 2) if self.step == "rep" else ("fsdp", self.count)
            self.sent = [swap(blocks, axis, size, 1) for blocks in self.ready]
        else:
            self.sent = [swap(self.ready[0], "fsdp", self.count, offset) for offset in self.step]
        return self

    def take(self, arrived):
        if self.step == "rep":
            self.held = [(*h, 0) for h in self.held] + [
                (blocks, h[1], 1) for blocks, h in zip(arrived, self.held)
            ]
        elif self.step == "core":
            held = [h if len(h) == 3 else (*h, None) for h in self.held]
            self.held = held + [
                (blocks, [o ^ 1 for o in h[1]], h[2]) for blocks, h in zip(arrived, held)
            ]
        else:
            offsets = self.held[0][1]
            self.held = self.held + [
                (blocks, [o ^ offset for o in offsets])
                for blocks, offset in zip(arrived, self.step)
            ]


def finish(anchor, *chains):
    sizes = [len(chain.sent) for chain in chains]
    anchor, *flat = after(anchor, *[part for chain in chains for part in chain.sent])
    for chain, size in zip(chains, sizes):
        chain.take(flat[:size])
        chain.prepare()
        flat = flat[size:]
    sizes = [len(chain.ready) for chain in chains]
    anchor, *flat = after(anchor, *[part for chain in chains for part in chain.ready])
    for chain, size in zip(chains, sizes):
        chain.renew(flat[:size])
        flat = flat[size:]
    return anchor


def together(anchor, *chains):
    anchor = finish(anchor, *chains)
    for chain in chains:
        if chain.steps:
            chain.send()
    return anchor


def go_on(anchor, *chains):
    for chain in chains:
        anchor = together(anchor, chain)
    return anchor


def complete(anchor, *chains):
    while chains:
        left = [chain for chain in chains if chain.steps]
        anchor = go_on(anchor, *chains)
        chains = left
    return anchor


def place_copies(pieces, parts, whole, where_ref, sems):
    me, other = where_ref[0], where_ref[1]
    copies = []
    for part, (offsets, half, first, columns) in zip(parts, pieces):
        rows = part.shape[1]
        for k, offset in enumerate(offsets):
            row = pl.ds(pl.multiple_of(lax.bitwise_xor(me, offset) * rows, rows), rows)
            if half is None:
                target = whole.at[row, pl.ds(first, columns)]
            else:
                width = columns // 2
                start = pl.multiple_of(first + lax.bitwise_xor(other, half) * width, 128)
                target = whole.at[row, pl.ds(start, width)]
            copies.append(pltpu.make_async_copy(part.at[k], target, sems.at[len(copies)]))
    return copies


def copies_of(pieces):
    return sum(len(offsets) for offsets, *_ in pieces)


def place_kernel(pieces, me_ref, *refs):
    parts, whole, sems = refs[: len(pieces)], refs[len(pieces)], refs[len(pieces) + 1]
    me, other = me_ref[0], me_ref[1]
    copies = []
    for part, (offsets, half, first, columns) in zip(parts, pieces):
        for k, offset in enumerate(offsets):
            row = lax.bitwise_xor(me, offset)
            if half is None:
                target = whole.at[row, :, pl.ds(first, columns)]
            else:
                width = columns // 2
                start = pl.multiple_of(first + lax.bitwise_xor(other, half) * width, 128)
                target = whole.at[row, :, pl.ds(start, width)]
            copies.append(pltpu.make_async_copy(part.at[k], target, sems.at[len(copies)]))
    for copy in copies:
        copy.start()
    for copy in copies:
        copy.wait()


def place(gathers, where, count):
    parts, pieces = parts_of(gathers)
    rows, kind = parts[0].shape[1], parts[0].dtype
    columns = sum(g.columns for g in gathers)
    whole = pl.pallas_call(
        functools.partial(place_kernel, pieces),
        out_shape=jax.ShapeDtypeStruct((count, rows, columns), kind),
        in_specs=[pl.BlockSpec(memory_space=pltpu.SMEM)]
        + [pl.BlockSpec(memory_space=pl.ANY)] * len(pieces),
        out_specs=pl.BlockSpec(memory_space=pltpu.VMEM),
        scratch_shapes=[pltpu.SemaphoreType.DMA((copies_of(pieces),))],
        compiler_params=pltpu.CompilerParams(vmem_limit_bytes=16 * 2**20),
        cost_estimate=BRIEF,
    )(where, *parts)
    return whole.reshape(count * rows, columns)


def parts_of(gathers):
    parts, pieces, first = [], [], 0
    for g in gathers:
        for blocks, offsets, half in g.held:
            parts.append(blocks)
            pieces.append((tuple(offsets), half, first, g.columns))
        first += g.columns
    return parts, pieces


def regroup(blocks, rows, count):
    parts, first = [], 0
    for size in rows:
        part = blocks[:, first : first + size]
        parts.append(part.reshape(count, -1, blocks.shape[2]))
        first += size
    return jnp.concatenate(parts, axis=1)


class Parts:
    def __init__(self, gathers, where, count, rows=None):
        self.columns = sum(g.columns for g in gathers)
        self.where = where
        if count == 16:
            self.parts, self.pieces = parts_of(gathers)
        else:
            whole = place(gathers, where, count).reshape(count, -1, self.columns)
            rows = rows or (whole.shape[1],)
            self.parts = [regroup(whole, rows, 16)]
            self.pieces = [(tuple(range(16)), None, 0, self.columns)]
            self.where = jnp.zeros_like(where)

    def pairs(self, halves):
        if len(self.parts) > 1:
            near = len(self.parts) // 2
            assert near == halves and all(piece[0] == ORDER for piece in self.pieces[:near])
            return self.parts
        size = self.columns // halves
        return [
            jnp.stack([self.parts[0][o + core, :, h * size : (h + 1) * size] for o in ORDER])
            for core in range(2)
            for h in range(halves)
        ]


def ordered(keep, give, where, count, rows=None, split=False):
    if count == 16:
        return keep, give
    if not split:
        keep, give = keep[None], give[None]
    whole = jnp.stack([keep, give], axis=2)
    halves, blocks, _, size, columns = whole.shape
    whole = whole.reshape(halves, 2 * blocks, size, columns)
    whole = jnp.concatenate([whole[h] for h in range(halves)], axis=2)
    columns = whole.shape[2]
    whole = regroup(whole, rows or (size,), count).reshape(-1, columns)
    found = take([whole], [(0, 0, columns)], where, count, split)
    if split:
        return jnp.stack(found[:2]), jnp.stack(found[2:])
    return found


def take_kernel(count, split, segments, me_ref, *refs):
    inputs = max(which for which, *_ in segments) + 1
    wholes, outs, sems = refs[:inputs], refs[inputs:-1], refs[-1]
    me, other = me_ref[0], me_ref[1]
    half = outs[0].shape[2]

    def copies(switch):
        found = []
        for which, start, columns, first in segments:
            for d in range(count):
                source = wholes[which].at[lax.bitwise_xor(me, d), :, pl.ds(start, columns)]
                side = (first // half) ^ switch
                target = outs[2 * (d % 2) + side] if split else outs[d % 2]
                target = target.at[d // 2, :, pl.ds(first % half, columns)]
                found.append(pltpu.make_async_copy(source, target, sems.at[len(found)]))
        return found

    def run(switch):
        found = copies(switch)
        for copy in found:
            copy.start()
        for copy in found:
            copy.wait()

    if split:
        for switch in range(2):
            pl.when(other == switch)(functools.partial(run, switch))
    else:
        run(0)


def take(wholes, segments, where, count, split):
    rows = wholes[0].shape[0] // count
    blocks = [w.reshape(count, rows, w.shape[1]) for w in wholes]
    columns = sum(segment[2] for segment in segments)
    half = columns // 2 if split else columns
    ends, first = [], 0
    for which, start, size in segments:
        while size:
            room = min(size, half - first % half)
            ends.append((which, start, room, first))
            first, start, size = first + room, start + room, size - room
    shape = jax.ShapeDtypeStruct((count // 2, rows, half), wholes[0].dtype)
    outs = 4 if split else 2
    return pl.pallas_call(
        functools.partial(take_kernel, count, split, ends),
        out_shape=(shape,) * outs,
        in_specs=[pl.BlockSpec(memory_space=pltpu.SMEM)]
        + [pl.BlockSpec(memory_space=pltpu.VMEM)] * len(blocks),
        out_specs=[pl.BlockSpec(memory_space=pl.ANY)] * outs,
        scratch_shapes=[pltpu.SemaphoreType.DMA((count * len(ends),))],
        compiler_params=pltpu.CompilerParams(vmem_limit_bytes=16 * 2**20),
        cost_estimate=BRIEF,
    )(where, *blocks)


def add(*values):
    return sum(value.astype(F32) for value in values).astype(BF16)


def join_kernel(*refs):
    *parts, whole = refs
    first = 0
    for part in parts:
        whole[first : first + part.shape[0]] = part[...]
        first += part.shape[0]


def join(parts):
    blocks = sum(part.shape[0] for part in parts)
    whole = pl.BlockSpec(memory_space=pltpu.VMEM)
    return pl.pallas_call(
        join_kernel,
        out_shape=jax.ShapeDtypeStruct((blocks, *parts[0].shape[1:]), parts[0].dtype),
        in_specs=[whole] * len(parts),
        out_specs=whole,
        compiler_params=pltpu.CompilerParams(vmem_limit_bytes=16 * 2**20),
        cost_estimate=BRIEF,
    )(*parts)


def merge_kernel(groups, parts, *refs):
    outs = refs[parts:]
    for group, out in zip(groups, outs):
        for j, index in enumerate(group):
            out[j] = sum(ref[index].astype(F32) for ref in refs[:parts]).astype(BF16)


def merge(parts, groups):
    rest = parts[0].shape[-2:]
    whole = pl.BlockSpec(memory_space=pltpu.VMEM)
    return pl.pallas_call(
        functools.partial(merge_kernel, groups, len(parts)),
        out_shape=[jax.ShapeDtypeStruct((len(group), *rest), BF16) for group in groups],
        in_specs=[whole] * len(parts),
        out_specs=[whole] * len(groups),
        compiler_params=pltpu.CompilerParams(vmem_limit_bytes=24 * 2**20),
        cost_estimate=BRIEF,
    )(*parts)


class Scatter:
    def __init__(self, keep, give, where, count, steps, split=False):
        self.where, self.count, self.split = where, count, split
        self.keep, self.give = keep, give
        self.steps = ["core"] + (["half"] if split else []) + list(steps) + ["rep"]
        self.offsets = list(range(0, count, 2))
        self.step = None

        self.ready = [give]

    def prepare(self):
        pass

    def renew(self, ready):
        self.ready = ready

    def send(self):
        self.step, self.steps = self.steps[0], self.steps[1:]
        if self.step in ("half", "rep"):
            self.sent = [swap(self.ready[0], "rep", 2, 1)]
        else:
            offsets = [1] if self.step == "core" else self.step
            self.sent = [
                swap(part, "fsdp", self.count, offset)
                for part, offset in zip(self.ready, offsets)
            ]
        return self

    def share_out(self, parts):
        step = self.steps[0]
        if step == "rep":
            self.held = merge(parts, [[0]])[0][0]
            self.ready = [self.held]
            return
        mask = 0
        for offset in step:
            mask |= offset
        stay = [o for o in self.offsets if o & mask == 0]
        groups = [[self.offsets.index(o | offset) for o in stay] for offset in (0, *step)]
        self.staying, *self.ready = merge(parts, groups)
        self.offsets = stay

    def take(self, arrived):
        if self.step == "core" and self.split:
            blocks = len(self.offsets)
            flat = [a.reshape(2 * blocks, *a.shape[2:]) for a in (self.keep, *arrived)]
            away, self.staying = merge(
                flat, [list(range(blocks, 2 * blocks)), list(range(blocks))]
            )
            self.ready = [away]
        elif self.step == "core":
            self.share_out([self.keep, *arrived])
        elif self.step == "rep":
            if self.split:
                low = self.where[1] == 0
                self.result = [
                    jnp.where(low, self.held, arrived[0]),
                    jnp.where(low, arrived[0], self.held),
                ]
            else:
                self.result = add(self.held, arrived[0])
            self.ready = []
        else:
            self.share_out([self.staying, *arrived])


def up_to(value, unit):
    return -(-value // unit) * unit

def swap_chunks(lines):
    chunk = lax.broadcasted_iota(jnp.int32, lines[0].shape, 1) // SLOT
    for step in (1, 2, 4):
        stays = (chunk & step) == 0
        for i in range(8):
            if i & step == 0:
                low, high = lines[i], lines[i + step]
                lines[i] = jnp.where(stays, low, pltpu.roll(high, step * SLOT, 1))
                lines[i + step] = jnp.where(stays, pltpu.roll(low, 128 - step * SLOT, 1), high)
    return lines

def spread(side, grid, columns):
    pixel = lax.broadcasted_iota(jnp.int32, (grid * side, columns), 0)
    column = lax.broadcasted_iota(jnp.int32, (grid * side, columns), 1)
    place = column % SLOT
    return ((pixel == column // SLOT * side + place) & (place < side)).astype(BF16)

def patch_kernel(*refs):
    pixels, outs, rows_ref, flat_ref = refs[:3], refs[3:6], refs[6], refs[7]
    for side, pixel_ref, out in zip(SIDES, pixels, outs):
        high = pixel_ref.shape[2]
        grid = high // side
        columns = up_to(grid * SLOT, 128)
        table = None if side == SLOT else spread(side, grid, columns)
        for c in range(3):
            picture = pixel_ref[0, c]
            if table is None:
                wide = picture.astype(F32)
            else:
                wide = jnp.dot(picture, table, preferred_element_type=F32)
            for block in range(columns // 128):
                rows_ref[3 * c + block, :high, :] = wide[:, 128 * block:128 * block + 128]
        slots = 3 * side
        for group in range(out.shape[1] // 128):
            for block in range(columns // 128):
                lines = []
                for q in range(8 * group, 8 * group + 8):
                    if q < slots:
                        lines.append(rows_ref[q // side * 3 + block, pl.ds(q % side, grid, stride=side), :])
                    else:
                        lines.append(jnp.zeros((grid, 128), F32))
                lines = swap_chunks(lines)
                for g in range(8):
                    if 8 * block + g < grid:
                        flat_ref[group, pl.ds(8 * block + g, grid, stride=grid), :] = lines[g]
        for group in range(out.shape[1] // 128):
            out[:, 128 * group:128 * group + 128] = flat_ref[group, :grid * grid, :].astype(BF16)

def patch_all(pixels):
    shapes = []
    for picture, side in zip(pixels, SIDES):
        grid = picture.shape[2] // side
        shapes.append(jax.ShapeDtypeStruct((grid * grid, up_to(3 * side * SLOT, 128)), BF16))
    high = max(p.shape[2] for p in pixels)
    return pl.pallas_call(
        patch_kernel,
        out_shape=shapes,
        in_specs=[pl.BlockSpec(memory_space=pltpu.VMEM)] * 3,
        out_specs=[pl.BlockSpec(memory_space=pltpu.VMEM)] * 3,
        scratch_shapes=[pltpu.VMEM((9, high, 128), F32), pltpu.VMEM((max(s.shape[1] for s in shapes) // 128, max(s.shape[0] for s in shapes), 128), F32)],
        compiler_params=pltpu.CompilerParams(vmem_limit_bytes=40 * 2**20),
        cost_estimate=BRIEF,
    )(*pixels)

def unpatch_kernel(pieces, starts, bounds, where_ref, grad_ref, *refs):
    parts, refs = refs[: len(pieces)], refs[len(pieces) :]
    outs, flat_ref, rows_ref, kernel_ref, sems = refs[:3], *refs[3:]
    copies = place_copies(pieces, parts, kernel_ref, where_ref, sems)
    for copy in copies:
        copy.start()
    for copy in copies:
        copy.wait()
    for i, side in enumerate(SIDES):
        out = outs[i]
        high = out.shape[2]
        grid = high // side
        columns = up_to(grid * SLOT, 128)
        width = bounds[i + 1] - bounds[i]
        grads = grad_ref[starts[i]:starts[i + 1], :]
        flat = jnp.dot(grads, kernel_ref[:, bounds[i]:bounds[i + 1]], preferred_element_type=F32)
        for group in range(width // 128):
            flat_ref[group, :grid * grid, :] = flat[:, 128 * group:128 * group + 128]
        slots = 3 * side
        for group in range(width // 128):
            for block in range(columns // 128):
                lines = []
                for g in range(8):
                    if 8 * block + g < grid:
                        lines.append(flat_ref[group, pl.ds(8 * block + g, grid, stride=grid), :])
                    else:
                        lines.append(jnp.zeros((grid, 128), F32))
                lines = swap_chunks(lines)
                for q in range(8 * group, min(8 * group + 8, slots)):
                    rows_ref[q // side * 3 + block, pl.ds(q % side, grid, stride=side), :] = lines[q % 8]
        table = None if side == SLOT else spread(side, grid, columns)
        for c in range(3):
            picture = jnp.concatenate([rows_ref[3 * c + block, :high, :] for block in range(columns // 128)], axis=1).astype(BF16)
            if table is not None:
                picture = lax.dot_general(picture, table, (((1,), (1,)), ((), ())), preferred_element_type=F32).astype(BF16)
            out[0, c] = picture

def unpatch_all(grads, embed_parts, starts, bounds, sides):
    high = max(sides)
    whole = pl.BlockSpec(memory_space=pltpu.VMEM)
    parts = embed_parts.parts
    return pl.pallas_call(
        functools.partial(unpatch_kernel, embed_parts.pieces, starts, bounds),
        out_shape=[jax.ShapeDtypeStruct((1, 3, s, s), BF16) for s in sides],
        in_specs=[pl.BlockSpec(memory_space=pltpu.SMEM), whole]
        + [pl.BlockSpec(memory_space=pl.ANY)] * len(parts),
        out_specs=[whole] * 3,
        scratch_shapes=[
            pltpu.VMEM(
                (
                    max(e - s for s, e in zip(bounds, bounds[1:])) // 128,
                    max(e - s for s, e in zip(starts, starts[1:])),
                    128,
                ),
                F32,
            ),
            pltpu.VMEM((9, high, 128), F32),
            pltpu.VMEM((grads.shape[1], embed_parts.columns), BF16),
            pltpu.SemaphoreType.DMA((copies_of(embed_parts.pieces),)),
        ],
        compiler_params=pltpu.CompilerParams(vmem_limit_bytes=32 * 2**20),
        cost_estimate=BRIEF,
    )(embed_parts.where, grads, *parts)


def unit(values):
    mean_row = jnp.mean(values, axis=-1, keepdims=True)
    centred = values - mean_row
    inverse = lax.rsqrt(jnp.mean(centred * centred, axis=-1, keepdims=True) + 1e-06)
    return centred * inverse, inverse


def norm_backward(grad_out, unit_rows, inverse, gain):
    grad_unit = grad_out * gain
    inner = jnp.mean(grad_unit * unit_rows, axis=-1, keepdims=True)
    grad_in = inverse * (
        grad_unit - jnp.mean(grad_unit, axis=-1, keepdims=True) - unit_rows * inner
    )
    return grad_in, jnp.sum(grad_out * unit_rows, axis=0), jnp.sum(grad_out, axis=0)


def chunks(total, most):
    pieces = -(-total // most)
    size = -(-total // pieces)
    size = -(-size // 16) * 16
    return [(s, min(size, total - s)) for s in range(0, total, size)]

def outer_t(first, second):
    return lax.dot_general(first, second, (((1,), (1,)), ((), ())), preferred_element_type=F32)

def attend_kernel(starts, chunk, q_ref, k_ref, v_ref, *refs):
    pair = pl.program_id(0)
    mixed_ref, total_ref = refs[-2:]
    if len(refs) > 2:
        mixed_ref[: starts[0], :] = refs[0][: starts[0], :]

    @pl.when(pair == 0)
    def _():
        total_ref[...] = refs[1][...] if len(refs) > 2 else jnp.zeros_like(total_ref)

    for begin, end in zip(starts, starts[1:]):
        keys, values = k_ref[begin:end, :], v_ref[begin:end, :]
        for offset, size in chunks(end - begin, chunk):
            rows = slice(begin + offset, begin + offset + size)
            queries = q_ref[rows, :] * (HEAD ** -0.5)
            lane = lax.broadcasted_iota(jnp.int32, (size, 128), 1)
            mixed, totals = [], []
            for head in range(2):
                own = (lane < HEAD) if head == 0 else (lane >= HEAD)
                scores = outer_t(jnp.where(own, queries, jnp.zeros_like(queries)), keys)
                top = jnp.max(scores, axis=1, keepdims=True)
                expo = jnp.exp(scores - top)
                total = jnp.sum(expo, axis=1, keepdims=True)
                out = jnp.dot(expo.astype(BF16), values, preferred_element_type=F32)
                mixed.append(out / total)
                totals.append(top + jnp.log(total))
            mixed_ref[rows, :] = jnp.where(lane < HEAD, mixed[0], mixed[1]).astype(BF16)
            held = total_ref[rows, :]
            held = jnp.where(lane == 2 * pair, totals[0], held)
            total_ref[rows, :] = jnp.where(lane == 2 * pair + 1, totals[1], held)

def attend_forward(qkv, starts, done=(), chunk=576):
    rows, width = qkv.shape[0], qkv.shape[1] // 3
    pairs = width // 128
    block = lambda first: pl.BlockSpec((rows, 128), lambda j: (0, first * pairs + j))
    return pl.pallas_call(
        functools.partial(attend_kernel, starts, chunk),
        grid=(pairs,),
        out_shape=(jax.ShapeDtypeStruct((rows, width), BF16), jax.ShapeDtypeStruct((rows, 128), F32)),
        in_specs=[block(0), block(1), block(2)]
        + [block(0), pl.BlockSpec((rows, 128), lambda j: (0, 0))][: len(done)],
        out_specs=[pl.BlockSpec((rows, 128), lambda j: (0, j)), pl.BlockSpec((rows, 128), lambda j: (0, 0))],
        compiler_params=pltpu.CompilerParams(vmem_limit_bytes=24 * 2**20),
        cost_estimate=BRIEF,
    )(qkv, qkv, qkv, *done)

def terms(value):
    first = value.astype(BF16)
    rest = value - first.astype(F32)
    second = rest.astype(BF16)
    return first, second, (rest - second.astype(F32)).astype(BF16)

def attend_back_kernel(starts, chunk, q_ref, k_ref, v_ref, mixed_ref, grad_ref, total_ref, *refs):
    pair = pl.program_id(0)
    *done, out_ref, left, right, acc = refs
    if done:
        out_ref[:, : starts[0], :] = done[0][:, : starts[0], :]
    scale = HEAD ** -0.5
    zero = jnp.zeros((), BF16)
    for begin, end in zip(starts, starts[1:]):
        size = end - begin
        for offset, part in chunks(size, chunk):
            rows = slice(begin + offset, begin + offset + part)
            lane = lax.broadcasted_iota(jnp.int32, (part, 128), 1)
            queries, grads = q_ref[rows, :] * scale, grad_ref[rows, :]
            product = grads.astype(F32) * mixed_ref[rows, :].astype(F32)
            total_all = total_ref[rows, :]
            for head in range(2):
                own = (lane < HEAD) if head == 0 else (lane >= HEAD)
                free = HEAD * (1 - head)
                inner = jnp.sum(jnp.where(own, product, 0.0), axis=1, keepdims=True)
                total = jnp.sum(jnp.where(lane == 2 * pair + head, total_all, 0.0), axis=1, keepdims=True)
                for target, value, line in ((left, queries, total), (right, grads, inner)):
                    wide = jnp.where(own, value, zero)
                    for i, term in enumerate(terms(line)):
                        wide = jnp.where(lane == free + i, term, wide)
                    target[head, offset:offset + part, :] = wide
        queries, grads = q_ref[begin:end, :], grad_ref[begin:end, :]
        acc[...] = jnp.zeros_like(acc)
        for offset, part in chunks(size, chunk):
            rows = slice(begin + offset, begin + offset + part)
            lane = lax.broadcasted_iota(jnp.int32, (part, 128), 1)
            keys, values = k_ref[rows, :], v_ref[rows, :]
            grad_key, grad_value = [], []
            for head in range(2):
                own = (lane < HEAD) if head == 0 else (lane >= HEAD)
                free = HEAD * (1 - head)
                minus = jnp.where((lane >= free) & (lane < free + 3), -jnp.ones((), BF16), zero)
                scores = outer_t(jnp.where(own, keys, minus), left[head, :size, :])
                probs = jnp.exp(scores)
                grad_scores = outer_t(jnp.where(own, values, minus), right[head, :size, :])
                grad_scores = (probs * grad_scores).astype(BF16)
                grad_value.append(jnp.dot(probs.astype(BF16), grads, preferred_element_type=F32))
                grad_key.append(jnp.dot(grad_scores, queries, preferred_element_type=F32))
                acc[head, :size, :] += lax.dot_general(grad_scores, keys, (((0,), (0,)), ((), ())), preferred_element_type=F32)
            out_ref[1, rows, :] = (jnp.where(lane < HEAD, *grad_key) * scale).astype(BF16)
            out_ref[2, rows, :] = jnp.where(lane < HEAD, *grad_value).astype(BF16)
        lane = lax.broadcasted_iota(jnp.int32, (size, 128), 1)
        out_ref[0, begin:end, :] = (jnp.where(lane < HEAD, acc[0, :size, :], acc[1, :size, :]) * scale).astype(BF16)

def attend_backward(qkv, mixed, totals, grad_mixed, starts, done=(), chunk=400):
    rows, width = mixed.shape
    pairs = width // 128
    longest = max(e - s for s, e in zip(starts, starts[1:]))
    block = lambda first: pl.BlockSpec((rows, 128), lambda j: (0, first * pairs + j))
    return pl.pallas_call(
        functools.partial(attend_back_kernel, starts, chunk),
        grid=(pairs,),
        out_shape=jax.ShapeDtypeStruct((3, rows, width), BF16),
        in_specs=[block(0), block(1), block(2), block(0), block(0), pl.BlockSpec((rows, 128), lambda j: (0, 0))]
        + [pl.BlockSpec((3, rows, 128), lambda j: (0, 0, j))][: len(done)],
        out_specs=pl.BlockSpec((3, rows, 128), lambda j: (0, 0, j)),
        scratch_shapes=[pltpu.VMEM((2, longest, 128), BF16), pltpu.VMEM((2, longest, 128), BF16), pltpu.VMEM((2, longest, 128), F32)],
        compiler_params=pltpu.CompilerParams(vmem_limit_bytes=24 * 2**20),
        cost_estimate=BRIEF,
    )(qkv, qkv, qkv, mixed, grad_mixed, totals, *done)


def slot_table(side, size, c):
    pixel = lax.broadcasted_iota(jnp.int32, (side * side, size), 0)
    column = lax.broadcasted_iota(jnp.int32, (side * side, size), 1)
    row, spot = column // SLOT - c * side, column % SLOT
    table = (row >= 0) & (row < side) & (spot < side) & (pixel == row * side + spot)
    return table.astype(BF16)


def two_terms(value):
    first = value.astype(BF16)
    return first, (value - first.astype(F32)).astype(BF16)


def resize_kernel(starts, inputs, *refs):
    sources, base_ref, pos_ref, vectors = refs[:3], refs[3], refs[4], refs[5 : 5 + inputs]
    low_ref, high_ref, *resizes, sems, out_ref, small = refs[5 + inputs :]
    copies = [
        pltpu.make_async_copy(source, target, sems.at[i])
        for i, (source, target) in enumerate(zip(sources, resizes))
    ]
    for copy in copies:
        copy.start()
    share = base_ref.shape[1]
    base = jnp.concatenate([base_ref[c] for c in range(3)])
    for start, side, resize_ref, copy in zip(starts, SIDES, resizes, copies):
        copy.wait()
        size = up_to(3 * side * SLOT, 128)
        own = sum(outer_t(base, term) for term in two_terms(resize_ref[...])[::-1]).astype(BF16)
        if side == SLOT:
            for c in range(3):
                first = start + c * side * SLOT
                out_ref[:, first : first + side * SLOT] = own[c * share : (c + 1) * share]
        else:
            out_ref[:, start : start + size] = sum(
                dot(own[c * share : (c + 1) * share], slot_table(side, size, c)) for c in range(3)
            ).astype(BF16)
    spots, width = pos_ref.shape[1], out_ref.shape[1] - starts[3]
    rise = vectors[-1].shape[1] // share
    for i, ref in enumerate(vectors):
        rows = [ref[:, k * share : (k + 1) * share] for k in range(ref.shape[1] // share)]
        for k, row in enumerate(rows):
            small[i + k : i + k + 1, :] = row.astype(F32)
    count = len(vectors) - 1 + rise

    def shift(rows, by):
        row = lax.broadcasted_iota(jnp.int32, (rows, width), 0)
        column = lax.broadcasted_iota(jnp.int32, (rows, width), 1)
        return ((row + by == column) & (row < count + 64 * (by == 0))).astype(BF16)

    small[count:, :] = jnp.zeros((16 - count, share), F32)
    out_ref[:, starts[3] :] = (
        dot(pos_ref[...], shift(spots, 0)) + inner_t(small[...].astype(BF16), shift(16, spots))
    ).astype(BF16)
    low_ref[...] = out_ref[:, : low_ref.shape[1]]
    high_ref[...] = out_ref[:, low_ref.shape[1] :]


def resize_all(resizes, base_kernel, posemb, vectors, starts, columns):
    whole = pl.BlockSpec(memory_space=pltpu.VMEM)
    share = base_kernel.shape[1]
    half = jax.ShapeDtypeStruct((share, columns // 2), BF16)
    return pl.pallas_call(
        functools.partial(resize_kernel, starts, len(vectors)),
        out_shape=(half, half),
        in_specs=[pl.BlockSpec(memory_space=pl.ANY)] * 3 + [whole] * (2 + len(vectors)),
        out_specs=(whole, whole),
        scratch_shapes=[pltpu.VMEM(r.shape, F32) for r in resizes]
        + [
            pltpu.SemaphoreType.DMA((3,)),
            pltpu.VMEM((share, columns), BF16),
            pltpu.VMEM((16, share), F32),
        ],
        compiler_params=pltpu.CompilerParams(vmem_limit_bytes=60 * 2**20),
        cost_estimate=BRIEF,
    )(*resizes, base_kernel, posemb, *vectors)


def enter_kernel(embed_pieces, qkv_pieces, starts, bounds, spots, where_ref, *refs):
    patches, map_ref, refs = refs[:3], refs[3], refs[4:]
    embed_parts, refs = refs[: len(embed_pieces)], refs[len(embed_pieces) :]
    qkv_parts, refs = refs[: len(qkv_pieces)], refs[len(qkv_pieces) :]
    embedded, units, qkv, lines_ref, inverse_ref, small_ref = refs[:6]
    normed, table, weight, embed_sems, qkv_sems = refs[6:]
    width = embedded.shape[1]
    embed_copies = place_copies(embed_pieces, embed_parts, table, where_ref, embed_sems)
    qkv_copies = place_copies(qkv_pieces, qkv_parts, weight, where_ref, qkv_sems)
    for copy in embed_copies + qkv_copies:
        copy.start()
    for copy in embed_copies:
        copy.wait()
    smalls = table[:, bounds[3] :]
    small_ref[...] = smalls
    row = lax.broadcasted_iota(jnp.int32, (16, 128), 0)
    lane = lax.broadcasted_iota(jnp.int32, (16, 128), 1)
    lines = outer_t(((lane == row + spots) & (row < 9)).astype(BF16), smalls)
    lines_ref[...] = lines
    for i, patch_ref in enumerate(patches):
        rows = slice(starts[i], starts[i + 1])
        value = outer_t(patch_ref[...], table[:, bounds[i] : bounds[i + 1]])
        for part in reversed(terms(map_ref[rows, :])):
            value = value + outer_t(part, smalls)
        embedded[rows, :] = value
        unit_rows, inverse = unit(value)
        inverse_ref[rows, :] = inverse
        units[rows, :] = unit_rows.astype(BF16)
        normed[rows, :] = (unit_rows * lines[1:2] + lines[2:3]).astype(BF16)
    for copy in qkv_copies:
        copy.wait()
    for i in range(3):
        columns = slice(i * width, (i + 1) * width)
        value = dot(normed[...], weight[:, columns])
        if i != 1:
            value = value + lines[3 + i // 2 : 4 + i // 2]
        qkv[:, columns] = value.astype(BF16)


def enter_all(embed_parts, qkv_parts, patches, maps, starts, bounds, spots):
    whole = pl.BlockSpec(memory_space=pltpu.VMEM)
    anywhere = pl.BlockSpec(memory_space=pl.ANY)
    parts = [*embed_parts.parts, *qkv_parts.parts]
    rows, width = maps.shape[0], 16 * parts[0].shape[1]
    return pl.pallas_call(
        functools.partial(
            enter_kernel, embed_parts.pieces, qkv_parts.pieces, starts, bounds, spots
        ),
        out_shape=(
            jax.ShapeDtypeStruct((rows, width), F32),
            jax.ShapeDtypeStruct((rows, width), BF16),
            jax.ShapeDtypeStruct((rows, 3 * width), BF16),
            jax.ShapeDtypeStruct((16, width), F32),
            jax.ShapeDtypeStruct((rows, 1), F32),
            jax.ShapeDtypeStruct((width, embed_parts.columns - bounds[3]), BF16),
        ),
        in_specs=[pl.BlockSpec(memory_space=pltpu.SMEM)]
        + [whole] * 4
        + [anywhere] * len(parts),
        out_specs=[whole] * 6,
        scratch_shapes=[
            pltpu.VMEM((rows, width), BF16),
            pltpu.VMEM((width, embed_parts.columns), BF16),
            pltpu.VMEM((width, 3 * width), BF16),
            pltpu.SemaphoreType.DMA((copies_of(embed_parts.pieces),)),
            pltpu.SemaphoreType.DMA((copies_of(qkv_parts.pieces),)),
        ],
        compiler_params=pltpu.CompilerParams(vmem_limit_bytes=40 * 2**20),
        cost_estimate=BRIEF,
    )(embed_parts.where, *patches, maps, *parts)


def base_gradient_kernel(starts, *refs):
    resizes, sum_ref, out_ref = refs[:3], refs[3], refs[4]
    share = sum_ref.shape[0]
    total = None
    for start, side, resize_ref in zip(starts, SIDES, resizes):
        size = up_to(3 * side * SLOT, 128)
        given = sum_ref[:, start : start + size]
        if side == SLOT:
            own = [given[:, c * side * SLOT : (c + 1) * side * SLOT] for c in range(3)]
        else:
            own = [outer_t(given, slot_table(side, size, c)).astype(BF16) for c in range(3)]
        own = jnp.concatenate(own)
        for term in two_terms(resize_ref[...])[::-1]:
            value = dot(own, term)
            total = value if total is None else total + value
    for c in range(3):
        out_ref[c] = total[c * share : (c + 1) * share]


def base_gradient(resizes, embed_sum, shape, starts):
    whole = pl.BlockSpec(memory_space=pltpu.VMEM)
    return pl.pallas_call(
        functools.partial(base_gradient_kernel, starts),
        out_shape=jax.ShapeDtypeStruct(shape, F32),
        in_specs=[whole] * 4,
        out_specs=whole,
        compiler_params=pltpu.CompilerParams(vmem_limit_bytes=24 * 2**20),
        cost_estimate=BRIEF,
    )(*resizes, embed_sum)


def gelu_pair(value):
    slope = math.sqrt(2 / math.pi)
    square = value * value
    curve = jnp.tanh(value * (slope + (slope * 0.044715) * square))
    half = 0.5 * value
    rise = 0.5 + 0.5 * curve
    bend = (half - half * (curve * curve)) * (slope + (3 * slope * 0.044715) * square)
    return value * rise, rise + bend


ORDER = (0, 8, 4, 12, 2, 10, 6, 14)


def feed_kernel(starts, chunk, where_ref, *refs):
    mixed_ref, embedded_ref, lines_ref, b_up_ref = refs[:4]
    up_parts, down_parts, cotangents = refs[4:8], refs[8:10], refs[10:13]
    finals = refs[13:16]
    up_keep, up_give, down_keep, down_give, g_bias_ref = refs[16:21]
    branch_ref, g_mixed_ref, sums_ref = refs[21:24]
    middle, normed, grads, act, grad_up, total, back = refs[24:31]
    w_up, w_down, w_out, g_up, g_down, g_out = refs[31:37]
    up_in, down_in, out_in, up_out, down_out, out_out, one, ends = refs[37:]
    step, steps = pl.program_id(0), pl.num_programs(0)
    rows = middle.shape[0]
    me, other = where_ref[0], where_ref[1]
    slot = lax.rem(step, 2)
    tile = w_up.shape[2]
    up_rows, down_rows = up_keep.shape[2], w_down.shape[1] // 4
    count = 16

    def at(index, size):
        return pl.ds(pl.multiple_of(index * size, size), size)

    def load_up(s, half):
        t = lax.bitwise_xor(s, me // 4)
        return [
            pltpu.make_async_copy(
                up_parts[2 * (d % 2) + half].at[ORDER.index(d - d % 2), :, at(lax.rem(t, 2), tile)],
                w_up.at[lax.rem(s, 2), at(lax.bitwise_xor(me, d), up_rows), :],
                up_in.at[lax.rem(s, 2), d],
            )
            for d in range(count)
        ]

    def load_down(s):
        copies = []
        for j in range(4):
            place_ = s // 2 + 2 * lax.rem(s, 2) + 4 * (j // 2)
            copies.append(
                pltpu.make_async_copy(
                    down_parts[j % 2].at[place_, pl.ds(0, down_rows), :],
                    w_down.at[lax.rem(s, 2), at(lax.bitwise_xor(lax.rem(me, 4), j), down_rows), :],
                    down_in.at[lax.rem(s, 2), j],
                )
            )
        return copies

    def load(s):
        t = lax.bitwise_xor(s, me // 4)
        side = lax.bitwise_xor(t // 2, other)
        for half in range(2):

            @pl.when(side == half)
            def _():
                for copy in load_up(s, half):
                    copy.start()

        for copy in load_down(s):
            copy.start()

    def load_out():
        return [
            pltpu.make_async_copy(
                down_parts[d % 2].at[ORDER.index(d - d % 2), pl.ds(down_rows, up_rows), :],
                w_out.at[at(lax.bitwise_xor(me, d), up_rows), :],
                out_in.at[d],
            )
            for d in range(count)
        ]

    def store(s):
        t = lax.bitwise_xor(s, me // 4)
        side = lax.bitwise_xor(t // 2, other)
        copies = []
        for d in range(count):
            copies.append(
                pltpu.make_async_copy(
                    g_up.at[lax.rem(s, 2), at(lax.bitwise_xor(me, d), up_rows), :],
                    (up_keep, up_give)[d % 2].at[side, d // 2, :, at(lax.rem(t, 2), tile)],
                    up_out.at[lax.rem(s, 2), d],
                )
            )
        for j in range(4):
            copies.append(
                pltpu.make_async_copy(
                    g_down.at[lax.rem(s, 2), at(lax.bitwise_xor(lax.rem(me, 4), j), down_rows), :],
                    (down_keep, down_give)[j % 2].at[2 * s + j // 2, pl.ds(0, down_rows), :],
                    down_out.at[lax.rem(s, 2), j],
                )
            )
        return copies

    def store_out():
        return [
            pltpu.make_async_copy(
                g_out.at[at(lax.bitwise_xor(me, d), up_rows), :],
                (down_keep, down_give)[d % 2].at[d // 2, pl.ds(down_rows, up_rows), :],
                out_out.at[d],
            )
            for d in range(count)
        ]

    @pl.when(step == 0)
    def _():
        copy = pltpu.make_async_copy(embedded_ref, middle, one.at[0])
        copy.start()
        for first in load_out():
            first.start()
        load(0)
        for i, ref in enumerate(cotangents):
            grads[starts[i] : starts[i + 1], :] = ref[0]
        copy.wait()
        for first in load_out():
            first.wait()
        for first, size in chunks(rows, 416):
            part = slice(first, first + size)
            value = middle[part, :] + dot(mixed_ref[part, :], w_out[...]) + lines_ref[5:6, :]
            middle[part, :] = value
            unit_rows, _ = unit(value)
            normed[part, :] = (unit_rows * lines_ref[6:7, :] + lines_ref[7:8, :]).astype(BF16)
            total[part, :] = value + lines_ref[8:9, :]
            back[part, :] = jnp.zeros((size, back.shape[1]), F32)

    @pl.when(step + 1 < steps)
    def _():
        load(step + 1)

    for copy in load_up(step, 0) + load_down(step):
        copy.wait()

    column = jnp.zeros((1, tile), F32)
    for first, size in chunks(rows, chunk):
        part = slice(first, first + size)
        up = dot(normed[part, :], w_up[slot]) + b_up_ref[...]
        value, slope = gelu_pair(up)
        value = value.astype(BF16)
        act[part, :] = value
        grad = (slope * outer_t(grads[part, :], w_down[slot])).astype(BF16)
        grad_up[part, :] = grad
        column += jnp.sum(grad.astype(F32), axis=0, keepdims=True)
        total[part, :] += dot(value, w_down[slot])
        back[part, :] += outer_t(grad, w_up[slot])
    g_bias_ref[...] = column

    @pl.when(step >= 2)
    def _():
        for copy in store(step - 2):
            copy.wait()

    g_down[slot] = inner_t(act[...], grads[...]).astype(BF16)
    g_up[slot] = inner_t(normed[...], grad_up[...]).astype(BF16)
    for copy in store(step):
        copy.start()

    @pl.when(step == steps - 1)
    def _():
        done = []

        def leave(source, target):
            done.append(pltpu.make_async_copy(source, target, ends.at[len(done)]))
            done[-1].start()

        for i, ref in enumerate(finals):
            part = pl.ds(starts[i], starts[i + 1] - starts[i])
            act[part, :] = total[part, :].astype(BF16)
            leave(act.at[part, :], ref.at[0])
        width = middle.shape[1]
        sums = [jnp.zeros((1, width), F32)] * 4
        for first, size in chunks(rows, 416):
            part = pl.ds(first, size)
            unit_rows, inverse = unit(middle[part, :])
            out = back[part, :]
            down = grads[part, :].astype(F32)
            grad, gain, bias = norm_backward(out, unit_rows, inverse, lines_ref[6:7, :])
            low = (grad + down).astype(BF16)
            normed[part, :] = low
            leave(normed.at[part, :], branch_ref.at[part, :])
            grad_up[part, :] = outer_t(low, w_out[...]).astype(BF16)
            leave(grad_up.at[part, :], g_mixed_ref.at[part, :])
            found = (
                gain[None],
                bias[None],
                jnp.sum(down, axis=0, keepdims=True),
                jnp.sum(low.astype(F32), axis=0, keepdims=True),
            )
            sums = [a + b for a, b in zip(sums, found)]
        g_out[...] = inner_t(mixed_ref[...], normed[...]).astype(BF16)
        for last in store_out():
            last.start()
        sums_ref[...] = jnp.concatenate(sums + [jnp.zeros((4, width), F32)])
        for last in store_out() + store(step - 1) + store(step) + done:
            last.wait()


def feed_all(where, mixed, embedded, lines, b_up, up_parts, down_parts, cotangents, starts, chunk=624):
    rows, width = mixed.shape
    tile = up_parts[0].shape[2] // 2
    hidden = 4 * tile
    up_rows = up_parts[0].shape[1]
    down_rows = down_parts[0].shape[1]
    fixed = lambda *shape: pl.BlockSpec(
        shape, lambda s, w: (0,) * len(shape), pipeline_mode=pl.Buffered(1)
    )
    whole = lambda *shape: pl.BlockSpec(shape, lambda s, w: (0,) * len(shape))
    mine = pl.BlockSpec((1, tile), lambda s, w: (0, lax.bitwise_xor(s, w[0] // 4)))
    anywhere = pl.BlockSpec(memory_space=pl.ANY)
    like = lambda shape, kind: jax.ShapeDtypeStruct(shape, kind)
    return pl.pallas_call(
        functools.partial(feed_kernel, starts, chunk),
        grid_spec=pltpu.PrefetchScalarGridSpec(
            num_scalar_prefetch=1,
            grid=(4,),
            in_specs=[fixed(rows, width), anywhere, fixed(16, width), mine]
            + [anywhere] * 6
            + [fixed(*c.shape) for c in cotangents],
            out_specs=[anywhere] * 7 + [mine, anywhere, anywhere, whole(8, width)],
            scratch_shapes=[
                pltpu.VMEM((rows, width), F32),
                pltpu.VMEM((rows, width), BF16),
                pltpu.VMEM((rows, width), BF16),
                pltpu.VMEM((rows, tile), BF16),
                pltpu.VMEM((rows, tile), BF16),
                pltpu.VMEM((rows, width), F32),
                pltpu.VMEM((rows, width), F32),
                pltpu.VMEM((2, width, tile), BF16),
                pltpu.VMEM((2, tile, width), BF16),
                pltpu.VMEM((width, width), BF16),
                pltpu.VMEM((2, width, tile), BF16),
                pltpu.VMEM((2, tile, width), BF16),
                pltpu.VMEM((width, width), BF16),
                pltpu.SemaphoreType.DMA((2, 16)),
                pltpu.SemaphoreType.DMA((2, 4)),
                pltpu.SemaphoreType.DMA((16,)),
                pltpu.SemaphoreType.DMA((2, 16)),
                pltpu.SemaphoreType.DMA((2, 4)),
                pltpu.SemaphoreType.DMA((16,)),
                pltpu.SemaphoreType.DMA((1,)),
                pltpu.SemaphoreType.DMA((3 + 2 * len(chunks(rows, 416)),)),
            ],
        ),
        out_shape=[like(c.shape, BF16) for c in cotangents]
        + [like((2, 8, up_rows, hidden // 2), BF16)] * 2
        + [like((8, down_rows, width), BF16)] * 2
        + [
            like((1, hidden), F32),
            like((rows, width), BF16),
            like((rows, width), BF16),
            like((8, width), F32),
        ],
        compiler_params=pltpu.CompilerParams(vmem_limit_bytes=56 * 2**20),
        cost_estimate=BRIEF,
    )(where, mixed, embedded, lines, b_up, *up_parts, *down_parts, *cotangents)


def spread_copies(source, segments, where_ref, sems, first=0):
    me, other = where_ref[0], where_ref[1]
    copies = []
    for start, columns, targets, half, there in segments:
        for d in range(16):
            rows = source.shape[0] // 16
            row = pl.ds(pl.multiple_of(lax.bitwise_xor(me, d) * rows, rows), rows)
            target = targets[d % 2]
            if half is not None:
                target = target.at[lax.bitwise_xor(other, half)]
            copies.append(
                pltpu.make_async_copy(
                    source.at[row, pl.ds(start, columns)],
                    target.at[d // 2, :, pl.ds(there, columns)],
                    sems.at[first + len(copies)],
                )
            )
    return copies


def leave_kernel(pieces, starts, bounds, spots, low_columns, chunk, where_ref, *refs):
    grads, units, branch, lines_ref, given_ref, bias_ref, inverse_ref, map_ref = refs[:8]
    patches, parts, refs = refs[8:11], refs[11 : 11 + len(pieces)], refs[11 + len(pieces) :]
    low_ref, low_outs, high_outs, refs = refs[0], refs[1:3], refs[3:5], refs[5:]
    normed, weight, embed_out, qkv_out, sums, weight_sems, out_sems = refs
    rows, width = low_ref.shape
    weights = place_copies(pieces, parts, weight, where_ref, weight_sems)
    half = embed_out.shape[1] // 2
    quarter = half // 2
    low = low_columns - half
    rest = (3 * width - low) // 2
    segments = [
        (qkv_out, (0, low, low_outs, None, half)),
        (qkv_out, (low, rest, high_outs, 0, quarter)),
        (qkv_out, (low + rest, rest, high_outs, 1, quarter)),
        (embed_out, (0, half, low_outs, None, 0)),
        (embed_out, (half, quarter, high_outs, 0, 0)),
        (embed_out, (half + quarter, quarter, high_outs, 1, 0)),
    ]
    copies = []
    for source, segment in segments:
        copies += spread_copies(source, [segment], where_ref, out_sems, len(copies))
    for copy in weights:
        copy.start()
    normed[...] = (units[...].astype(F32) * lines_ref[1:2, :] + lines_ref[2:3, :]).astype(BF16)
    for i in range(3):
        columns = slice(i * width, (i + 1) * width)
        qkv_out[:, columns] = inner_t(normed[...], grads[i]).astype(BF16)
        for copy in copies[16 * i - 16 : 16 * i] if i < 2 else copies[16:48]:
            copy.start()
    sums[...] = jnp.zeros_like(sums)
    sums[5:6, :] = given_ref[3:4, :]
    sums[6:9, :] = given_ref[:3, :]
    for copy in weights:
        copy.wait()
    totals = [jnp.zeros((1, width), F32)] * 4
    for first, size in chunks(rows, chunk):
        part = slice(first, first + size)
        found = sum(
            outer_t(grads[i, part, :], weight[:, i * width : (i + 1) * width]) for i in range(3)
        )
        grad, gain, bias = norm_backward(
            found, units[part, :].astype(F32), inverse_ref[part, :], lines_ref[1:2, :]
        )
        low_ref[part, :] = (grad + branch[part, :].astype(F32)).astype(BF16)
        found = [gain[None], bias[None]] + [
            jnp.sum(grads[i, part, :].astype(F32), axis=0, keepdims=True) for i in (0, 2)
        ]
        totals = [a + b for a, b in zip(totals, found)]
    for i, value in enumerate(totals):
        sums[i + 1 : i + 2, :] = value
    row = lax.broadcasted_iota(jnp.int32, (16, 128), 0)
    lane = lax.broadcasted_iota(jnp.int32, (16, 128), 1)
    smalls = inner_t(sums[...].astype(BF16), ((lane == row + spots) & (row < 9)).astype(BF16))
    rise = bias_ref.shape[1]
    smalls += dot(bias_ref[...], ((lane == row + spots + 9)[:rise]).astype(BF16))
    started = 48
    for i, patch_ref in enumerate(patches):
        part = slice(starts[i], starts[i + 1])
        size = bounds[i + 1] - bounds[i]
        above, below = two_terms(map_ref[part, :])
        found = inner_t(low_ref[part, :], jnp.concatenate([patch_ref[...], above, below], axis=1))
        embed_out[:, bounds[i] : bounds[i + 1]] = found[:, :size].astype(BF16)
        smalls += found[:, size : size + 128] + found[:, size + 128 :]
        if bounds[i + 1] >= half and started == 48:
            started = 64
            for copy in copies[48:64]:
                copy.start()
    embed_out[:, bounds[3] :] = smalls.astype(BF16)
    for copy in copies[started:]:
        copy.start()
    for copy in copies:
        copy.wait()


def leave_all(
    qkv_parts,
    grad_qkv,
    units,
    branch,
    lines,
    given,
    bias,
    inverse,
    maps,
    patches,
    starts,
    bounds,
    spots,
    low_columns,
    chunk=416,
):
    _, rows, width = grad_qkv.shape
    whole = pl.BlockSpec(memory_space=pltpu.VMEM)
    anywhere = pl.BlockSpec(memory_space=pl.ANY)
    parts = qkv_parts.parts
    columns = bounds[3] + 128
    block = width // 16
    high_columns = (3 * width + columns - low_columns) // 2
    return pl.pallas_call(
        functools.partial(
            leave_kernel, qkv_parts.pieces, starts, bounds, spots, low_columns, chunk
        ),
        out_shape=[jax.ShapeDtypeStruct((rows, width), BF16)]
        + [jax.ShapeDtypeStruct((8, block, low_columns), BF16)] * 2
        + [jax.ShapeDtypeStruct((2, 8, block, high_columns), BF16)] * 2,
        in_specs=[pl.BlockSpec(memory_space=pltpu.SMEM)]
        + [whole] * 11
        + [anywhere] * len(parts),
        out_specs=[whole] + [anywhere] * 4,
        scratch_shapes=[
            pltpu.VMEM((rows, width), BF16),
            pltpu.VMEM((width, 3 * width), BF16),
            pltpu.VMEM((width, columns), BF16),
            pltpu.VMEM((width, 3 * width), BF16),
            pltpu.VMEM((16, width), F32),
            pltpu.SemaphoreType.DMA((copies_of(qkv_parts.pieces),)),
            pltpu.SemaphoreType.DMA((96,)),
        ],
        compiler_params=pltpu.CompilerParams(vmem_limit_bytes=44 * 2**20),
        cost_estimate=BRIEF,
    )(
        qkv_parts.where,
        grad_qkv,
        units,
        branch,
        lines,
        given,
        bias,
        inverse,
        maps,
        *patches,
        *parts,
    )


def dot(first, second):
    return jnp.dot(first, second, preferred_element_type=F32)


def inner_t(first, second):
    return lax.dot_general(first, second, (((0,), (0,)), ((), ())), preferred_element_type=F32)


def body(count, pixels, resizes, posmaps, weights, cotangents):
    base_kernel, patch_bias, posemb = weights[:3]
    ln1_gain, ln1_bias, qkv_weight, qv_bias, out_weight, out_bias = weights[3:9]
    ln2_gain, ln2_bias, up_weight, up_bias, down_weight, down_bias = weights[9:]
    channels, base_pixels, share = base_kernel.shape
    width = share * count
    spots = posemb.shape[0]
    where = jnp.stack([lax.axis_index("fsdp"), lax.axis_index("rep")]).astype(jnp.int32)
    tokens = [c.shape[1] for c in cotangents]
    starts = [sum(tokens[:i]) for i in range(4)]
    bits = [2**i for i in range(1, count.bit_length() - 1)]
    inward = [(bit,) for bit in bits]
    outward = inward[::-1]
    turned = inward[:1] + outward[:-1]
    short = inward[:-2] + [(bits[-2], bits[-1], bits[-2] + bits[-1])]

    up_per = up_bias.shape[0] // share
    used = spots + 9 + up_per
    bounds = [0]
    for side in SIDES:
        bounds.append(bounds[-1] + up_to(3 * side * SLOT, 128))
    columns = bounds[3] + 128
    vectors = [
        v.reshape(1, -1)
        for v in (
            patch_bias,
            ln1_gain,
            ln1_bias,
            qv_bias[0],
            qv_bias[1],
            out_bias,
            ln2_gain,
            ln2_bias,
            down_bias,
            up_bias,
        )
    ]
    maps = jnp.concatenate(posmaps)
    maps = jnp.concatenate(
        [maps, jnp.ones((maps.shape[0], 1), F32), jnp.zeros((maps.shape[0], 127 - spots), F32)],
        axis=1,
    )

    base_turned = base_kernel.swapaxes(1, 2)
    down_rows = (down_weight.shape[0], out_weight.shape[0])
    down_block = jnp.concatenate([down_weight, out_weight])
    qkv_shards = Gather(qkv_weight, where, count, outward, split=True).send()
    up_shards = Gather(up_weight, where, count, outward, split=True).send()
    shards = resize_all(resizes, base_turned, posemb.T, vectors, bounds, columns)
    embed_low = Gather(shards[0], where, count, outward).send()
    embed_high = Gather(shards[1], where, count, outward).send()
    held = go_on((pixels, maps, *shards), qkv_shards, embed_low, qkv_shards, embed_high, up_shards)
    pixels, maps, *_ = go_on(held, embed_low, qkv_shards)
    patches = patch_all(pixels)
    patches = finish(patches, embed_high, up_shards)
    embed_high.send()
    patches, down_block = after(patches, down_block)
    down_shards = Gather(down_block, where, count, outward).send()
    patches = go_on(patches, embed_low, qkv_shards, embed_high, down_shards)
    up_shards.send()
    patches, maps = complete((patches, maps), embed_low, qkv_shards, embed_high)
    w_qkv = Parts([qkv_shards], where, count)
    w_embed = Parts([embed_low, embed_high], where, count)
    embedded, units, qkv, lines, inverse, columns_small = enter_all(
        w_embed, w_qkv, patches, maps, starts, bounds, spots
    )
    qkv = together(qkv, up_shards, down_shards)
    mixed, totals = attend_forward(qkv, starts)
    mixed = together(mixed, up_shards, down_shards)
    mixed = complete(mixed, up_shards, down_shards)
    w_up = Parts([up_shards], where, count)
    w_down = Parts([down_shards], where, count, down_rows)
    b_up = columns_small[:, spots + 9 : used].astype(F32)
    b_up = b_up.reshape(count, share, up_per).swapaxes(1, 2).reshape(1, -1)
    (
        *results,
        up_keep,
        up_give,
        down_keep,
        down_give,
        grad_b_up,
        branch,
        grad_mixed,
        sums,
    ) = feed_all(
        w_up.where, mixed, embedded, lines, b_up, w_up.pairs(2), w_down.pairs(1), cotangents, starts
    )
    rows16 = (down_rows[0] * count // 16, down_rows[1] * count // 16)
    down_sums = Scatter(
        *ordered(down_keep, down_give, where, count, rows16), where, count, inward
    ).send()
    up_sums = Scatter(
        *ordered(up_keep, up_give, where, count, split=True), where, count, inward, split=True
    ).send()
    grad_qkv = attend_backward(qkv, mixed, totals, grad_mixed, starts[:3])
    grad_qkv = together(grad_qkv, down_sums, up_sums)
    grad_qkv = attend_backward(qkv, mixed, totals, grad_mixed, starts[2:], (grad_qkv,))
    grad_qkv = together(grad_qkv, down_sums, up_sums)
    half = columns // 2
    low_columns = half + 5 * width // 3
    grad_low, *shares = leave_all(
        w_qkv,
        grad_qkv,
        units,
        branch,
        lines,
        sums,
        grad_b_up.reshape(width, up_per).astype(BF16),
        inverse,
        maps,
        patches,
        starts,
        bounds,
        spots,
        low_columns,
    )
    grad_low, *shares = together((grad_low, *shares), down_sums, up_sums)
    low_sums = Scatter(*ordered(*shares[:2], where, count), where, count, short).send()
    high_sums = Scatter(
        *ordered(*shares[2:], where, count, split=True), where, count, short, split=True
    ).send()
    grad_low = go_on(grad_low, low_sums, high_sums)
    pixel_grads = unpatch_all(grad_low, w_embed, starts, bounds, [p.shape[2] for p in pixels])
    pixel_grads = complete(pixel_grads, low_sums, high_sums, down_sums, up_sums)

    low, high = low_sums.result, high_sums.result
    quarter = half // 2
    embed_sum = jnp.concatenate([low[:, :half]] + [h[:, :quarter] for h in high], axis=1)
    qkv_sum = jnp.concatenate([low[:, half:]] + [h[:, quarter:] for h in high], axis=1).astype(F32)
    down_sum = down_sums.result.astype(F32)
    up_sum = jnp.concatenate(up_sums.result, axis=1).astype(F32)
    base_grad = base_gradient(resizes, embed_sum, base_turned.shape, bounds).swapaxes(1, 2)
    small_sum = embed_sum[:, bounds[3] : bounds[3] + used].astype(F32)
    vectors = small_sum[:, spots : spots + 9].T
    return (
        *results,
        *pixel_grads,
        base_grad,
        vectors[0],
        small_sum[:, :spots].T,
        vectors[1],
        vectors[2],
        qkv_sum,
        vectors[3:5],
        down_sum[down_rows[0] :],
        vectors[5],
        vectors[6],
        vectors[7],
        up_sum,
        small_sum[:, spots + 9 :].reshape(-1),
        down_sum[: down_rows[0]],
        vectors[8],
    )


def solution(mesh):
    count = mesh.shape["fsdp"]

    def run(*args):
        return body(count, args[:3], args[3:6], args[6:9], args[9:24], args[24:])

    images = ("rep", "fsdp")
    weight_specs = (
        P(None, None, "fsdp"),
        P("fsdp"),
        P(None, "fsdp"),
        P("fsdp"),
        P("fsdp"),
        P("fsdp", None),
        P(None, "fsdp"),
        P("fsdp", None),
        P("fsdp"),
        P("fsdp"),
        P("fsdp"),
        P("fsdp", None),
        P("fsdp"),
        P("fsdp", None),
        P("fsdp"),
    )
    return jax.shard_map(
        run,
        mesh=mesh,
        in_specs=(P(images, None, None, None),) * 3
        + (P(),) * 6
        + weight_specs
        + (P(images, None, None),) * 3,
        out_specs=(P(images, None, None),) * 3
        + (P(images, None, None, None),) * 3
        + weight_specs,
        check_vma=False,
    )
```

profile of v0, /device:TPU:0, one launch (start us, length us, event | category | flops | bytes accessed | tf_op | source)
XLA Modules:
  0.0 381.0 jit_solution(14841351193435725331)
XLA Ops:
  1.7 4.1 %collective-permute-start = (bf16[1,48,1152]{2,1,0:T(8,128)(2,1)S(1)}, bf16[1,48,1152]{2,1,0:T(8,128)(2,1)S(1)}, u32[]{:S(2)}, u32[]{:S(2)}) collective-permute-start(bf16[1,48,1152]{2,1,0:T(8,128)(2,1)S(1)} %dynamic-slice_bitcast_fusion.1.refs_0_), channel_id=1, source_target_pairs={{0,8},{1,9},{2,10},{3,11},{4,12},{5,13},{6,14},{7,15},{8,0},{9,1},... | collective-permute-start | bytes 331784 | tf_op jit(solution)/shard_map/ppermute | solution.py:21
  8.5 4.6 %shard_map.418 = (bf16[48,1024]{1,0:T(8,128)(2,1)}, bf16[48,1024]{1,0:T(8,128)(2,1)}) custom-call(f32[100,1024]{1,0:T(8,128)} %refs_0_.4, f32[144,1024]{1,0:T(8,128)} %refs_1_.4, f32[256,1024]{1,0:T(8,128)} %refs_2_.4, bf16[3,48,1024]{2,1,0:T(8,128)(2,1)} %bitcast.59, bf16[48,49]{1,0:T(8,128)(2,1)} %bitcast.61, bf16[1,48]{1,0:T(2,128)(2,1)} %bitcast.62, ...), custom_call_target="tpu_custom_call" | custom-call | flops 1 | bytes 1 | tf_op jit(solution)/shard_map/pallas_call | solution.py:741
  13.2 1.6 collective-permute-start.2
  15.4 7.3 %collective-permute-done.1.refs_1_ = bf16[1,48,1024]{2,1,0:T(8,128)(2,1)S(1)} collective-permute-done((bf16[1,48,1024]{2,1,0:T(8,128)(2,1)}, bf16[1,48,1024]{2,1,0:T(8,128)(2,1)S(1)}, u32[]{:S(2)}, u32[]{:S(2)}) %collective-permute-start.1) | collective-permute-done | bytes 98336 | tf_op jit(solution)/shard_map/ppermute | solution.py:21
  23.6 1.6 collective-permute-start.6
  25.7 1.6 collective-permute-start.4
  28.7 9.6 %collective-permute-done.3.refs_1_ = bf16[1,48,1024]{2,1,0:T(8,128)(2,1)S(1)} collective-permute-done((bf16[1,48,1024]{2,1,0:T(8,128)(2,1)S(1)}, bf16[1,48,1024]{2,1,0:T(8,128)(2,1)S(1)}, u32[]{:S(2)}, u32[]{:S(2)}) %collective-permute-start.3) | collective-permute-done | bytes 98336 | tf_op jit(solution)/shard_map/ppermute | solution.py:21
  38.6 1.6 collective-permute-start.10
  40.7 2.0 collective-permute-start.7
  42.8 6.8 %shard_map.426 = (bf16[256,512]{1,0:T(8,128)(2,1)S(1)}, bf16[400,640]{1,0:T(8,128)(2,1)S(1)}, bf16[576,768]{1,0:T(8,128)(2,1)S(1)}) custom-call(bf16[1,3,160,160]{3,2,1,0:T(8,128)(2,1)S(1)} %copy-done.46, bf16[1,3,240,240]{3,2,1,0:T(8,128)(2,1)S(1)} %copy-done.45, bf16[1,3,384,384]{3,2,1,0:T(8,128)(2,1)S(1)} %copy-done.38), custom_call_target="tpu_custom_call" | custom-call | flops 1 | bytes 1 | tf_op jit(solution)/shard_map/pallas_call | solution.py:462
  52.7 2.3 collective-permute-start.12
  56.5 7.1 %collective-permute-done.11.refs_1_ = bf16[4,48,1024]{2,1,0:T(8,128)(2,1)S(1)} collective-permute-done((bf16[4,48,1024]{2,1,0:T(8,128)(2,1)S(1)}, bf16[4,48,1024]{2,1,0:T(8,128)(2,1)S(1)}, u32[]{:S(2)}, u32[]{:S(2)}) %collective-permute-start.11) | collective-permute-done | bytes 393248 | tf_op jit(solution)/shard_map/ppermute | solution.py:21
  63.7 8.4 %collective-permute-done.12.refs_1_ = bf16[1,240,768]{2,1,0:T(8,128)(2,1)S(1)} collective-permute-done((bf16[1,240,768]{2,1,0:T(8,128)(2,1)S(1)}, bf16[1,240,768]{2,1,0:T(8,128)(2,1)S(1)}, u32[]{:S(2)}, u32[]{:S(2)}) %collective-permute-start.12) | collective-permute-done | bytes 368672 | tf_op jit(solution)/shard_map/ppermute | solution.py:21
  78.8 14.9 %shard_map.432 = (f32[1232,768]{1,0:T(8,128)}, bf16[1232,768]{1,0:T(8,128)(2,1)S(1)}, bf16[1232,2304]{1,0:T(8,128)(2,1)}, f32[16,768]{1,0:T(8,128)S(1)}, f32[123...) custom-call(s32[2]{0:T(128)S(1)} %pad_add_fusion.where_ref, bf16[256,512]{1,0:T(8,128)(2,1)S(1)} %get-tuple-element.518.refs_0_.refs_8_, ...), custom_call_target="tpu_custom_call" | custom-call | flops 1 | bytes 1 | tf_op jit(solution)/shard_map/pallas_call | solution.py:801
  93.8 3.2 shard_map.433.refs_4_
  100.6 2.6 copy-done.2
  103.2 18.2 %shard_map.435 = (bf16[1232,768]{1,0:T(8,128)(2,1)S(1)}, f32[1232,128]{1,0:T(8,128)S(1)}) custom-call(bf16[1232,2304]{1,0:T(8,128)(2,1)S(1)} %copy-done.2, bf16[1232,2304]{1,0:T(8,128)(2,1)S(1)} %copy-done.2, bf16[1232,2304]{1,0:T(8,128)(2,1)S(1)} %copy-done.2), custom_call_target="tpu_custom_call" | custom-call | flops 1 | bytes 1 | tf_op jit(solution)/shard_map/pallas_call | solution.py:597
  121.4 5.6 %collective-permute-done.19.refs_5_ = bf16[8,48,1536]{2,1,0:T(8,128)(2,1)} collective-permute-done((bf16[8,48,1536]{2,1,0:T(8,128)(2,1)}, bf16[8,48,1536]{2,1,0:T(8,128)(2,1)}, u32[]{:S(2)}, u32[]{:S(2)}) %collective-permute-start.19) | collective-permute-done | bytes 1179680 | tf_op jit(solution)/shard_map/ppermute | solution.py:21
  127.0 5.5 %collective-permute-done.20.refs_1_ = bf16[4,240,768]{2,1,0:T(8,128)(2,1)S(1)} collective-permute-done((bf16[4,240,768]{2,1,0:T(8,128)(2,1)S(1)}, bf16[4,240,768]{2,1,0:T(8,128)(2,1)S(1)}, u32[]{:S(2)}, u32[]{:S(2)}) %collective-permute-start.20) | collective-permute-done | bytes 1474592 | tf_op jit(solution)/shard_map/ppermute | solution.py:21
  134.4 5.4 %collective-permute-done.21.refs_6_ = bf16[8,48,1536]{2,1,0:T(8,128)(2,1)} collective-permute-done((bf16[8,48,1536]{2,1,0:T(8,128)(2,1)}, bf16[8,48,1536]{2,1,0:T(8,128)(2,1)}, u32[]{:S(2)}, u32[]{:S(2)}) %collective-permute-start.21) | collective-permute-done | bytes 1179680 | tf_op jit(solution)/shard_map/ppermute | solution.py:21
  139.8 2.0 collective-permute-done.22.refs_7_
  141.9 68.6 %shard_map.437 = (bf16[1,256,768]{2,1,0:T(8,128)(2,1)}, bf16[1,400,768]{2,1,0:T(8,128)(2,1)}, bf16[1,576,768]{2,1,0:T(8,128)(2,1)}, bf16[2,8,48,1536]{3,2,1,0:T(...) custom-call(s32[2]{0:T(128)} %copy-done.52, ...), custom_call_target="tpu_custom_call" | custom-call | flops 1 | bytes 1 | tf_op jit(solution)/shard_map/pallas_call | solution.py:1077
  211.1 1.5 copy-done.9
  212.6 15.7 %shard_map.438.refs_0_ = bf16[3,1232,768]{2,1,0:T(8,128)(2,1)S(1)} custom-call(bf16[1232,2304]{1,0:T(8,128)(2,1)S(1)} %bitcast.42, bf16[1232,2304]{1,0:T(8,128)(2,1)S(1)} %bitcast.42, bf16[1232,2304]{1,0:T(8,128)(2,1)S(1)} %bitcast.42, bf16[1232,768]{1,0:T(8,128)(2,1)S(1)} %copy-done.5, bf16[1232,768]{1,0:T(8,128)(2,1)S(1)} %copy-done.9, ...), custom_call_target="tpu_custom_call" | custom-call | flops 1 | bytes 1 | tf_op jit(solution)/shard_map/pallas_call | solution.py:667
  232.6 18.5 %shard_map.441.refs_0_ = bf16[3,1232,768]{2,1,0:T(8,128)(2,1)S(1)} custom-call(bf16[1232,2304]{1,0:T(8,128)(2,1)S(1)} %bitcast.42, bf16[1232,2304]{1,0:T(8,128)(2,1)S(1)} %bitcast.42, bf16[1232,2304]{1,0:T(8,128)(2,1)S(1)} %bitcast.42, bf16[1232,768]{1,0:T(8,128)(2,1)S(1)} %copy-done.5, bf16[1232,768]{1,0:T(8,128)(2,1)S(1)} %copy-done.10, ...), custom_call_target="tpu_custom_call" | custom-call | flops 1 | bytes 1 | tf_op jit(solution)/shard_map/pallas_call | solution.py:667
  251.1 2.4 copy-done.3
  253.6 5.5 %collective-permute-done.27.refs_1_ = bf16[8,48,1536]{2,1,0:T(8,128)(2,1)S(1)} collective-permute-done((bf16[8,48,1536]{2,1,0:T(8,128)(2,1)S(1)}, bf16[8,48,1536]{2,1,0:T(8,128)(2,1)S(1)}, u32[]{:S(2)}, u32[]{:S(2)}) %collective-permute-start.27) | collective-permute-done | bytes 1179680 | tf_op jit(solution)/shard_map/ppermute | solution.py:21
  259.1 5.9 %collective-permute-done.26.refs_1_ = bf16[4,240,768]{2,1,0:T(8,128)(2,1)S(1)} collective-permute-done((bf16[4,240,768]{2,1,0:T(8,128)(2,1)S(1)}, bf16[4,240,768]{2,1,0:T(8,128)(2,1)S(1)}, u32[]{:S(2)}, u32[]{:S(2)}) %collective-permute-start.26) | collective-permute-done | bytes 1474592 | tf_op jit(solution)/shard_map/ppermute | solution.py:21
  268.0 1.7 collective-permute-start.28
  271.6 23.9 %shard_map.444 = (bf16[1232,768]{1,0:T(8,128)(2,1)}, bf16[8,48,2304]{2,1,0:T(8,128)(2,1)}, bf16[8,48,2304]{2,1,0:T(8,128)(2,1)}, bf16[2,8,48,1024]{3,2,1,0:T(8,128)(2,1)S(1)}, bf16[2,8,48,1024]{3,2,1,0:T(8,128)(2,1)S(1)}) custom-call(s32[2]{0:T(128)S(1)} %copy-done.53, bf16[3,1232,768]{2,1,0:T(8,128)(2,1)} %copy-done.3, bf16[1232,768]{1,0:T(8,128)(2,1)} %copy-done.33, ...), custom_call_target="tpu_custom_call" | custom-call | flops 1 | bytes 1 | tf_op jit(solution)/shard_map/pallas_call | solution.py:1243
  298.8 5.1 %collective-permute-done.30.refs_1_ = bf16[8,48,2304]{2,1,0:T(8,128)(2,1)S(1)} collective-permute-done((bf16[8,48,2304]{2,1,0:T(8,128)(2,1)}, bf16[8,48,2304]{2,1,0:T(8,128)(2,1)S(1)}, u32[]{:S(2)}, u32[]{:S(2)}) %collective-permute-start.30) | collective-permute-done | bytes 1769504 | tf_op jit(solution)/shard_map/ppermute | solution.py:21
  304.4 1.8 collective-permute-start.32
  306.6 1.6 collective-permute-start.33
  308.4 1.8 collective-permute-start.35
  310.2 8.4 %shard_map.449 = (bf16[1,3,160,160]{3,2,1,0:T(8,128)(2,1)}, bf16[1,3,240,240]{3,2,1,0:T(8,128)(2,1)}, bf16[1,3,384,384]{3,2,1,0:T(8,128)(2,1)}) custom-call(s32[2]{0:T(128)S(1)} %copy-done.53, bf16[1232,768]{1,0:T(8,128)(2,1)S(1)} %copy-done.32, bf16[8,48,1024]{2,1,0:T(8,128)(2,1)S(1)} %copy-done.12, bf16[8,48,1024]{2,1,0:T(8,128)(2,1)S(1)} %copy-done.23, ...), custom_call_target="tpu_custom_call" | custom-call | flops 1 | bytes 1 | tf_op jit(solution)/shard_map/pallas_call | solution.py:513
  318.5 7.6 %collective-permute-done.32.refs_1_ = bf16[4,48,2304]{2,1,0:T(8,128)(2,1)S(1)} collective-permute-done((bf16[4,48,2304]{2,1,0:T(8,128)(2,1)S(1)}, bf16[4,48,2304]{2,1,0:T(8,128)(2,1)S(1)}, u32[]{:S(2)}, u32[]{:S(2)}) %collective-permute-start.32) | collective-permute-done | bytes 884768 | tf_op jit(solution)/shard_map/ppermute | solution.py:21
  327.2 1.8 collective-permute-start.39
  329.1 1.6 collective-permute-start.40
  331.0 1.7 collective-permute-start.37
  332.7 2.4 collective-permute-start.38
  335.1 5.5 %collective-permute-done.36.refs_1_ = bf16[1,48,2304]{2,1,0:T(8,128)(2,1)S(1)} collective-permute-done((bf16[1,48,2304]{2,1,0:T(8,128)(2,1)S(1)}, bf16[1,48,2304]{2,1,0:T(8,128)(2,1)S(1)}, u32[]{:S(2)}, u32[]{:S(2)}) %collective-permute-start.36) | collective-permute-done | bytes 221216 | tf_op jit(solution)/shard_map/ppermute | solution.py:21
  340.6 11.8 %collective-permute-done.37.refs_2_ = bf16[1,48,2304]{2,1,0:T(8,128)(2,1)S(1)} collective-permute-done((bf16[1,48,2304]{2,1,0:T(8,128)(2,1)}, bf16[1,48,2304]{2,1,0:T(8,128)(2,1)S(1)}, u32[]{:S(2)}, u32[]{:S(2)}) %collective-permute-start.37) | collective-permute-done | bytes 221216 | tf_op jit(solution)/shard_map/ppermute | solution.py:21
  353.6 4.8 %collective-permute-done.41.refs_1_ = bf16[1,48,1536]{2,1,0:T(8,128)(2,1)S(1)} collective-permute-done((bf16[1,48,1536]{2,1,0:T(8,128)(2,1)S(1)}, bf16[1,48,1536]{2,1,0:T(8,128)(2,1)S(1)}, u32[]{:S(2)}, u32[]{:S(2)}) %collective-permute-start.41) | collective-permute-done | bytes 147488 | tf_op jit(solution)/shard_map/ppermute | solution.py:21
  361.1 2.0 collective-permute-start.44
  363.1 2.4 collective-permute-start.45
  367.1 2.9 collective-permute-done.44.refs_2_
  372.6 2.2 collective-permute-done.47
  377.8 2.1 shard_map.458
  (252 shorter events, 51.8 us)
Async XLA Ops:
  1.7 11.5 %collective-permute-start = (bf16[1,48,1152]{2,1,0:T(8,128)(2,1)S(1)}, bf16[1,48,1152]{2,1,0:T(8,128)(2,1)S(1)}, u32[]{:S(2)}, u32[]{:S(2)}) collective-permute-start(bf16[1,48,1152]{2,1,0:T(8,128)(2,1)S(1)} %dynamic-slice_bitcast_fusion.1.refs_0_), channel_id=1, source_target_pairs={{0,8},{1,9},{2,10},{3,11},{4,12},{5,13},{6,14},{7,15},{8,0},{9,1},... | collective-permute-start | bytes 331784 | tf_op jit(solution)/shard_map/ppermute | solution.py:21
  13.2 10.4 %collective-permute-start.2 = (bf16[2,48,1152]{2,1,0:T(8,128)(2,1)S(1)}, bf16[2,48,1152]{2,1,0:T(8,128)(2,1)S(1)}, u32[]{:S(2)}, u32[]{:S(2)}) collective-permute-start(bf16[2,48,1152]{2,1,0:T(8,128)(2,1)S(1)} %shard_map.419.refs_0_), channel_id=1, source_target_pairs={{0,4},{1,5},{2,6},{3,7},{4,0},{5,1},{6,2},{7,3},{8,12},{9,13},{10,... | collective-permute-start | bytes 663560 | tf_op jit(solution)/shard_map/ppermute | solution.py:21
  14.8 7.8 %collective-permute-start.1 = (bf16[1,48,1024]{2,1,0:T(8,128)(2,1)}, bf16[1,48,1024]{2,1,0:T(8,128)(2,1)S(1)}, u32[]{:S(2)}, u32[]{:S(2)}) collective-permute-start(bf16[1,48,1024]{2,1,0:T(8,128)(2,1)} %bitcast.55), channel_id=1, source_target_pairs={{0,8},{1,9},{2,10},{3,11},{4,12},{5,13},{6,14},{7,15},{8,0},{9,1},... | collective-permute-start | bytes 294920 | tf_op jit(solution)/shard_map/ppermute | solution.py:21
  23.6 14.9 %collective-permute-start.6 = (bf16[4,48,1152]{2,1,0:T(8,128)(2,1)S(1)}, bf16[4,48,1152]{2,1,0:T(8,128)(2,1)S(1)}, u32[]{:S(2)}, u32[]{:S(2)}) collective-permute-start(bf16[4,48,1152]{2,1,0:T(8,128)(2,1)S(1)} %shard_map.421.refs_0_), channel_id=1, source_target_pairs={{0,2},{1,3},{2,0},{3,1},{4,6},{5,7},{6,4},{7,5},{8,10},{9,11},{10,... | collective-permute-start | bytes 1327112 | tf_op jit(solution)/shard_map/ppermute | solution.py:21
  25.2 13.3 %collective-permute-start.5 = (bf16[2,48,1024]{2,1,0:T(8,128)(2,1)S(1)}, bf16[2,48,1024]{2,1,0:T(8,128)(2,1)S(1)}, u32[]{:S(2)}, u32[]{:S(2)}) collective-permute-start(bf16[2,48,1024]{2,1,0:T(8,128)(2,1)S(1)} %shard_map.420.refs_0_), channel_id=1, source_target_pairs={{0,4},{1,5},{2,6},{3,7},{4,0},{5,1},{6,2},{7,3},{8,12},{9,13},{10,... | collective-permute-start | bytes 589832 | tf_op jit(solution)/shard_map/ppermute | solution.py:21
  25.7 12.7 %collective-permute-start.4 = (bf16[1,48,1536]{2,1,0:T(8,128)(2,1)S(1)}, bf16[1,48,1536]{2,1,0:T(8,128)(2,1)S(1)}, u32[]{:S(2)}, u32[]{:S(2)}) collective-permute-start(bf16[1,48,1536]{2,1,0:T(8,128)(2,1)S(1)} %dynamic-slice_bitcast_fusion.refs_0_), channel_id=1, source_target_pairs={{0,8},{1,9},{2,10},{3,11},{4,12},{5,13},{6,14},{7,15},{8,0},{9,1},... | collective-permute-start | bytes 442376 | tf_op jit(solution)/shard_map/ppermute | solution.py:21
  27.3 11.0 %collective-permute-start.3 = (bf16[1,48,1024]{2,1,0:T(8,128)(2,1)S(1)}, bf16[1,48,1024]{2,1,0:T(8,128)(2,1)S(1)}, u32[]{:S(2)}, u32[]{:S(2)}) collective-permute-start(bf16[1,48,1024]{2,1,0:T(8,128)(2,1)S(1)} %bitcast.53), channel_id=1, source_target_pairs={{0,8},{1,9},{2,10},{3,11},{4,12},{5,13},{6,14},{7,15},{8,0},{9,1},... | collective-permute-start | bytes 294920 | tf_op jit(solution)/shard_map/ppermute | solution.py:21
  38.6 17.4 %collective-permute-start.10 = (bf16[8,48,1152]{2,1,0:T(8,128)(2,1)S(1)}, bf16[8,48,1152]{2,1,0:T(8,128)(2,1)}, u32[]{:S(2)}, u32[]{:S(2)}) collective-permute-start(bf16[8,48,1152]{2,1,0:T(8,128)(2,1)S(1)} %shard_map.425.refs_8_.refs_11_), channel_id=1, source_target_pairs={{0,16},{16,0},{1,17},{17,1},{2,18},{18,2},{3,19},{19,3},{4,20},{20... | collective-permute-start | bytes 2654216 | tf_op jit(solution)/shard_map/ppermute | solution.py:21
  40.2 11.7 %collective-permute-start.9 = (bf16[4,48,1024]{2,1,0:T(8,128)(2,1)S(1)}, bf16[4,48,1024]{2,1,0:T(8,128)(2,1)S(1)}, u32[]{:S(2)}, u32[]{:S(2)}) collective-permute-start(bf16[4,48,1024]{2,1,0:T(8,128)(2,1)S(1)} %shard_map.424.refs_0_), channel_id=1, source_target_pairs={{0,2},{1,3},{2,0},{3,1},{4,6},{5,7},{6,4},{7,5},{8,10},{9,11},{10,... | collective-permute-start | bytes 1179656 | tf_op jit(solution)/shard_map/ppermute | solution.py:21
  40.7 10.3 %collective-permute-start.8 = (bf16[2,48,1536]{2,1,0:T(8,128)(2,1)S(1)}, bf16[2,48,1536]{2,1,0:T(8,128)(2,1)S(1)}, u32[]{:S(2)}, u32[]{:S(2)}) collective-permute-start(bf16[2,48,1536]{2,1,0:T(8,128)(2,1)S(1)} %shard_map.423.refs_0_), channel_id=1, source_target_pairs={{0,4},{1,5},{2,6},{3,7},{4,0},{5,1},{6,2},{7,3},{8,12},{9,13},{10,... | collective-permute-start | bytes 884744 | tf_op jit(solution)/shard_map/ppermute | solution.py:21
  40.7 10.3 %collective-permute-start.7 = (bf16[2,48,1024]{2,1,0:T(8,128)(2,1)S(1)}, bf16[2,48,1024]{2,1,0:T(8,128)(2,1)S(1)}, u32[]{:S(2)}, u32[]{:S(2)}) collective-permute-start(bf16[2,48,1024]{2,1,0:T(8,128)(2,1)S(1)} %shard_map.422.refs_0_), channel_id=1, source_target_pairs={{0,4},{1,5},{2,6},{3,7},{4,0},{5,1},{6,2},{7,3},{8,12},{9,13},{10,... | collective-permute-start | bytes 589832 | tf_op jit(solution)/shard_map/ppermute | solution.py:21
  52.0 21.4 %collective-permute-start.13 = (bf16[8,48,1024]{2,1,0:T(8,128)(2,1)S(1)}, bf16[8,48,1024]{2,1,0:T(8,128)(2,1)S(1)}, u32[]{:S(2)}, u32[]{:S(2)}) collective-permute-start(bf16[8,48,1024]{2,1,0:T(8,128)(2,1)S(1)} %shard_map.429.refs_4_.refs_0_), channel_id=1, source_target_pairs={{0,1},{1,0},{2,3},{3,2},{4,5},{5,4},{6,7},{7,6},{8,9},{9,8},{10,11... | collective-permute-start | bytes 2359304 | tf_op jit(solution)/shard_map/ppermute | solution.py:21
  52.1 11.5 %collective-permute-start.11 = (bf16[4,48,1024]{2,1,0:T(8,128)(2,1)S(1)}, bf16[4,48,1024]{2,1,0:T(8,128)(2,1)S(1)}, u32[]{:S(2)}, u32[]{:S(2)}) collective-permute-start(bf16[4,48,1024]{2,1,0:T(8,128)(2,1)S(1)} %shard_map.427.refs_0_), channel_id=1, source_target_pairs={{0,2},{1,3},{2,0},{3,1},{4,6},{5,7},{6,4},{7,5},{8,10},{9,11},{10,... | collective-permute-start | bytes 1179656 | tf_op jit(solution)/shard_map/ppermute | solution.py:21
  52.7 19.5 %collective-permute-start.12 = (bf16[1,240,768]{2,1,0:T(8,128)(2,1)S(1)}, bf16[1,240,768]{2,1,0:T(8,128)(2,1)S(1)}, u32[]{:S(2)}, u32[]{:S(2)}) collective-permute-start(bf16[1,240,768]{2,1,0:T(8,128)(2,1)S(1)} %bitcast.48), channel_id=1, source_target_pairs={{0,8},{1,9},{2,10},{3,11},{4,12},{5,13},{6,14},{7,15},{8,0},{9,1},... | collective-permute-start | bytes 1105928 | tf_op jit(solution)/shard_map/ppermute | solution.py:21
  56.0 19.4 %collective-permute-start.14 = (bf16[8,48,1152]{2,1,0:T(8,128)(2,1)S(1)}, bf16[8,48,1152]{2,1,0:T(8,128)(2,1)}, u32[]{:S(2)}, u32[]{:S(2)}) collective-permute-start(bf16[8,48,1152]{2,1,0:T(8,128)(2,1)S(1)} %shard_map.425.refs_8_.refs_11_), channel_id=1, source_target_pairs={{0,1},{1,0},{2,3},{3,2},{4,5},{5,4},{6,7},{7,6},{8,9},{9,8},{10,11... | collective-permute-start | bytes 2654216 | tf_op jit(solution)/shard_map/ppermute | solution.py:21
  56.0 19.4 %collective-permute-start.15 = (bf16[8,48,1152]{2,1,0:T(8,128)(2,1)}, bf16[8,48,1152]{2,1,0:T(8,128)(2,1)}, u32[]{:S(2)}, u32[]{:S(2)}) collective-permute-start(bf16[8,48,1152]{2,1,0:T(8,128)(2,1)} %collective-permute-done.10.refs_9_.refs_12_), channel_id=1, source_target_pairs={{0,1},{1,0},{2,3},{3,2},{4,5},{5,4},{6,7},{7,6},{8,9},{9,8},{10,11... | collective-permute-start | bytes 2654216 | tf_op jit(solution)/shard_map/ppermute | solution.py:21
  63.7 11.8 %collective-permute-start.16 = (bf16[8,48,1024]{2,1,0:T(8,128)(2,1)S(1)}, bf16[8,48,1024]{2,1,0:T(8,128)(2,1)}, u32[]{:S(2)}, u32[]{:S(2)}) collective-permute-start(bf16[8,48,1024]{2,1,0:T(8,128)(2,1)S(1)} %shard_map.430.refs_6_.refs_2_), channel_id=1, source_target_pairs={{0,1},{1,0},{2,3},{3,2},{4,5},{5,4},{6,7},{7,6},{8,9},{9,8},{10,11... | collective-permute-start | bytes 2359304 | tf_op jit(solution)/shard_map/ppermute | solution.py:21
  73.1 20.7 %collective-permute-start.18 = (bf16[2,240,768]{2,1,0:T(8,128)(2,1)}, bf16[2,240,768]{2,1,0:T(8,128)(2,1)}, u32[]{:S(2)}, u32[]{:S(2)}) collective-permute-start(bf16[2,240,768]{2,1,0:T(8,128)(2,1)} %shard_map.431.refs_0_), channel_id=1, source_target_pairs={{0,4},{1,5},{2,6},{3,7},{4,0},{5,1},{6,2},{7,3},{8,12},{9,13},{10,... | collective-permute-start | bytes 2211848 | tf_op jit(solution)/shard_map/ppermute | solution.py:21
  74.3 19.5 %collective-permute-start.17 = (bf16[4,48,1536]{2,1,0:T(8,128)(2,1)}, bf16[4,48,1536]{2,1,0:T(8,128)(2,1)}, u32[]{:S(2)}, u32[]{:S(2)}) collective-permute-start(bf16[4,48,1536]{2,1,0:T(8,128)(2,1)} %shard_map.428.refs_0_), channel_id=1, source_target_pairs={{0,2},{1,3},{2,0},{3,1},{4,6},{5,7},{6,4},{7,5},{8,10},{9,11},{10,... | collective-permute-start | bytes 1769480 | tf_op jit(solution)/shard_map/ppermute | solution.py:21
  98.5 34.0 %collective-permute-start.20 = (bf16[4,240,768]{2,1,0:T(8,128)(2,1)S(1)}, bf16[4,240,768]{2,1,0:T(8,128)(2,1)S(1)}, u32[]{:S(2)}, u32[]{:S(2)}) collective-permute-start(bf16[4,240,768]{2,1,0:T(8,128)(2,1)S(1)} %shard_map.434.refs_0_), channel_id=1, source_target_pairs={{0,2},{1,3},{2,0},{3,1},{4,6},{5,7},{6,4},{7,5},{8,10},{9,11},{10,... | collective-permute-start | bytes 4423688 | tf_op jit(solution)/shard_map/ppermute | solution.py:21
  99.6 27.4 %collective-permute-start.19 = (bf16[8,48,1536]{2,1,0:T(8,128)(2,1)}, bf16[8,48,1536]{2,1,0:T(8,128)(2,1)}, u32[]{:S(2)}, u32[]{:S(2)}) collective-permute-start(bf16[8,48,1536]{2,1,0:T(8,128)(2,1)} %shard_map.433.refs_4_), channel_id=1, source_target_pairs={{0,16},{16,0},{1,17},{17,1},{2,18},{18,2},{3,19},{19,3},{4,20},{20... | collective-permute-start | bytes 3538952 | tf_op jit(solution)/shard_map/ppermute | solution.py:21
  132.7 9.1 %collective-permute-start.23 = (bf16[8,240,768]{2,1,0:T(8,128)(2,1)S(1)}, bf16[8,240,768]{2,1,0:T(8,128)(2,1)}, u32[]{:S(2)}, u32[]{:S(2)}) collective-permute-start(bf16[8,240,768]{2,1,0:T(8,128)(2,1)S(1)} %shard_map.436.refs_8_), channel_id=1, source_target_pairs={{0,1},{1,0},{2,3},{3,2},{4,5},{5,4},{6,7},{7,6},{8,9},{9,8},{10,11... | collective-permute-start | bytes 8847368 | tf_op jit(solution)/shard_map/ppermute | solution.py:21
  132.8 7.0 %collective-permute-start.21 = (bf16[8,48,1536]{2,1,0:T(8,128)(2,1)}, bf16[8,48,1536]{2,1,0:T(8,128)(2,1)}, u32[]{:S(2)}, u32[]{:S(2)}) collective-permute-start(bf16[8,48,1536]{2,1,0:T(8,128)(2,1)} %shard_map.433.refs_4_), channel_id=1, source_target_pairs={{0,1},{1,0},{2,3},{3,2},{4,5},{5,4},{6,7},{7,6},{8,9},{9,8},{10,11... | collective-permute-start | bytes 3538952 | tf_op jit(solution)/shard_map/ppermute | solution.py:21
  133.3 8.5 %collective-permute-start.22 = (bf16[8,48,1536]{2,1,0:T(8,128)(2,1)}, bf16[8,48,1536]{2,1,0:T(8,128)(2,1)}, u32[]{:S(2)}, u32[]{:S(2)}) collective-permute-start(bf16[8,48,1536]{2,1,0:T(8,128)(2,1)} %collective-permute-done.19.refs_5_), channel_id=1, source_target_pairs={{0,1},{1,0},{2,3},{3,2},{4,5},{5,4},{6,7},{7,6},{8,9},{9,8},{10,11... | collective-permute-start | bytes 3538952 | tf_op jit(solution)/shard_map/ppermute | solution.py:21
  210.5 17.9 %collective-permute-start.24 = (bf16[8,240,768]{2,1,0:T(8,128)(2,1)}, bf16[8,240,768]{2,1,0:T(8,128)(2,1)S(1)}, u32[]{:S(2)}, u32[]{:S(2)}) collective-permute-start(bf16[8,240,768]{2,1,0:T(8,128)(2,1)} %get-tuple-element.556), channel_id=1, source_target_pairs={{0,1},{1,0},{2,3},{3,2},{4,5},{5,4},{6,7},{7,6},{8,9},{9,8},{10,11... | collective-permute-start | bytes 8847368 | tf_op jit(solution)/shard_map/ppermute | solution.py:21
  210.7 17.7 %collective-permute-start.25 = (bf16[2,8,48,1536]{3,2,1,0:T(8,128)(2,1)}, bf16[2,8,48,1536]{3,2,1,0:T(8,128)(2,1)S(1)}, u32[]{:S(2)}, u32[]{:S(2)}) collective-permute-start(bf16[2,8,48,1536]{3,2,1,0:T(8,128)(2,1)} %get-tuple-element.557), channel_id=1, source_target_pairs={{0,1},{1,0},{2,3},{3,2},{4,5},{5,4},{6,7},{7,6},{8,9},{9,8},{10,11... | collective-permute-start | bytes 7077896 | tf_op jit(solution)/shard_map/ppermute | solution.py:21
  230.6 34.4 %collective-permute-start.26 = (bf16[4,240,768]{2,1,0:T(8,128)(2,1)S(1)}, bf16[4,240,768]{2,1,0:T(8,128)(2,1)S(1)}, u32[]{:S(2)}, u32[]{:S(2)}) collective-permute-start(bf16[4,240,768]{2,1,0:T(8,128)(2,1)S(1)} %get-tuple-element.566), channel_id=1, source_target_pairs={{0,2},{1,3},{2,0},{3,1},{4,6},{5,7},{6,4},{7,5},{8,10},{9,11},{10,... | collective-permute-start | bytes 4423688 | tf_op jit(solution)/shard_map/ppermute | solution.py:21
  231.4 27.7 %collective-permute-start.27 = (bf16[8,48,1536]{2,1,0:T(8,128)(2,1)S(1)}, bf16[8,48,1536]{2,1,0:T(8,128)(2,1)S(1)}, u32[]{:S(2)}, u32[]{:S(2)}) collective-permute-start(bf16[8,48,1536]{2,1,0:T(8,128)(2,1)S(1)} %get-tuple-element.567), channel_id=1, source_target_pairs={{0,16},{16,0},{1,17},{17,1},{2,18},{18,2},{3,19},{19,3},{4,20},{20... | collective-permute-start | bytes 3538952 | tf_op jit(solution)/shard_map/ppermute | solution.py:21
  268.0 27.6 %collective-permute-start.28 = (bf16[2,240,768]{2,1,0:T(8,128)(2,1)}, bf16[2,240,768]{2,1,0:T(8,128)(2,1)}, u32[]{:S(2)}, u32[]{:S(2)}) collective-permute-start(bf16[2,240,768]{2,1,0:T(8,128)(2,1)} %get-tuple-element.586), channel_id=1, source_target_pairs={{0,4},{1,5},{2,6},{3,7},{4,0},{5,1},{6,2},{7,3},{8,12},{9,13},{10,... | collective-permute-start | bytes 2211848 | tf_op jit(solution)/shard_map/ppermute | solution.py:21
  269.7 25.9 %collective-permute-start.29 = (bf16[4,48,1536]{2,1,0:T(8,128)(2,1)}, bf16[4,48,1536]{2,1,0:T(8,128)(2,1)}, u32[]{:S(2)}, u32[]{:S(2)}) collective-permute-start(bf16[4,48,1536]{2,1,0:T(8,128)(2,1)} %get-tuple-element.587), channel_id=1, source_target_pairs={{0,2},{1,3},{2,0},{3,1},{4,6},{5,7},{6,4},{7,5},{8,10},{9,11},{10,... | collective-permute-start | bytes 1769480 | tf_op jit(solution)/shard_map/ppermute | solution.py:21
  298.2 5.7 %collective-permute-start.30 = (bf16[8,48,2304]{2,1,0:T(8,128)(2,1)}, bf16[8,48,2304]{2,1,0:T(8,128)(2,1)S(1)}, u32[]{:S(2)}, u32[]{:S(2)}) collective-permute-start(bf16[8,48,2304]{2,1,0:T(8,128)(2,1)} %get-tuple-element.600), channel_id=1, source_target_pairs={{0,1},{1,0},{2,3},{3,2},{4,5},{5,4},{6,7},{7,6},{8,9},{9,8},{10,11... | collective-permute-start | bytes 5308424 | tf_op jit(solution)/shard_map/ppermute | solution.py:21
  298.3 7.9 %collective-permute-start.31 = (bf16[2,8,48,1024]{3,2,1,0:T(8,128)(2,1)S(1)}, bf16[2,8,48,1024]{3,2,1,0:T(8,128)(2,1)S(1)}, u32[]{:S(2)}, u32[]{:S(2)}) collective-permute-start(bf16[2,8,48,1024]{3,2,1,0:T(8,128)(2,1)S(1)} %get-tuple-element.606), channel_id=1, source_target_pairs={{0,1},{1,0},{2,3},{3,2},{4,5},{5,4},{6,7},{7,6},{8,9},{9,8},{10,11... | collective-permute-start | bytes 4718600 | tf_op jit(solution)/shard_map/ppermute | solution.py:21
  304.4 21.8 %collective-permute-start.32 = (bf16[4,48,2304]{2,1,0:T(8,128)(2,1)S(1)}, bf16[4,48,2304]{2,1,0:T(8,128)(2,1)S(1)}, u32[]{:S(2)}, u32[]{:S(2)}) collective-permute-start(bf16[4,48,2304]{2,1,0:T(8,128)(2,1)S(1)} %get-tuple-element.615), channel_id=1, source_target_pairs={{0,2},{1,3},{2,0},{3,1},{4,6},{5,7},{6,4},{7,5},{8,10},{9,11},{10,... | collective-permute-start | bytes 2654216 | tf_op jit(solution)/shard_map/ppermute | solution.py:21
  306.6 20.5 %collective-permute-start.33 = (bf16[8,48,1024]{2,1,0:T(8,128)(2,1)S(1)}, bf16[8,48,1024]{2,1,0:T(8,128)(2,1)S(1)}, u32[]{:S(2)}, u32[]{:S(2)}) collective-permute-start(bf16[8,48,1024]{2,1,0:T(8,128)(2,1)S(1)} %get-tuple-element.627), channel_id=1, source_target_pairs={{0,16},{16,0},{1,17},{17,1},{2,18},{18,2},{3,19},{19,3},{4,20},{20... | collective-permute-start | bytes 2359304 | tf_op jit(solution)/shard_map/ppermute | solution.py:21
  308.1 20.9 %collective-permute-start.34 = (bf16[1,240,768]{2,1,0:T(8,128)(2,1)S(1)}, bf16[1,240,768]{2,1,0:T(8,128)(2,1)S(1)}, u32[]{:S(2)}, u32[]{:S(2)}) collective-permute-start(bf16[1,240,768]{2,1,0:T(8,128)(2,1)S(1)} %get-tuple-element.637), channel_id=1, source_target_pairs={{0,8},{1,9},{2,10},{3,11},{4,12},{5,13},{6,14},{7,15},{8,0},{9,1},... | collective-permute-start | bytes 1105928 | tf_op jit(solution)/shard_map/ppermute | solution.py:21
  308.4 24.3 %collective-permute-start.35 = (bf16[2,48,1536]{2,1,0:T(8,128)(2,1)S(1)}, bf16[2,48,1536]{2,1,0:T(8,128)(2,1)S(1)}, u32[]{:S(2)}, u32[]{:S(2)}) collective-permute-start(bf16[2,48,1536]{2,1,0:T(8,128)(2,1)S(1)} %get-tuple-element.646), channel_id=1, source_target_pairs={{0,4},{1,5},{2,6},{3,7},{4,0},{5,1},{6,2},{7,3},{8,12},{9,13},{10,... | collective-permute-start | bytes 884744 | tf_op jit(solution)/shard_map/ppermute | solution.py:21
  327.2 26.3 %collective-permute-start.39 = (bf16[4,48,1024]{2,1,0:T(8,128)(2,1)S(1)}, bf16[4,48,1024]{2,1,0:T(8,128)(2,1)S(1)}, u32[]{:S(2)}, u32[]{:S(2)}) collective-permute-start(bf16[4,48,1024]{2,1,0:T(8,128)(2,1)S(1)} %get-tuple-element.669), channel_id=1, source_target_pairs={{0,2},{1,3},{2,0},{3,1},{4,6},{5,7},{6,4},{7,5},{8,10},{9,11},{10,... | collective-permute-start | bytes 1179656 | tf_op jit(solution)/shard_map/ppermute | solution.py:21
  329.1 24.5 %collective-permute-start.40 = (bf16[240,768]{1,0:T(8,128)(2,1)S(1)}, bf16[240,768]{1,0:T(8,128)(2,1)}, u32[]{:S(2)}, u32[]{:S(2)}) collective-permute-start(bf16[240,768]{1,0:T(8,128)(2,1)S(1)} %bitcast.47), channel_id=1, source_target_pairs={{0,16},{16,0},{1,17},{17,1},{2,18},{18,2},{3,19},{19,3},{4,20},{20... | collective-permute-start | bytes 1105928 | tf_op jit(solution)/shard_map/ppermute | solution.py:21
  330.7 9.9 %collective-permute-start.36 = (bf16[1,48,2304]{2,1,0:T(8,128)(2,1)S(1)}, bf16[1,48,2304]{2,1,0:T(8,128)(2,1)S(1)}, u32[]{:S(2)}, u32[]{:S(2)}) collective-permute-start(bf16[1,48,2304]{2,1,0:T(8,128)(2,1)S(1)} %get-tuple-element.656), channel_id=1, source_target_pairs={{0,4},{1,5},{2,6},{3,7},{4,0},{5,1},{6,2},{7,3},{8,12},{9,13},{10,... | collective-permute-start | bytes 663560 | tf_op jit(solution)/shard_map/ppermute | solution.py:21
  331.0 21.4 %collective-permute-start.37 = (bf16[1,48,2304]{2,1,0:T(8,128)(2,1)}, bf16[1,48,2304]{2,1,0:T(8,128)(2,1)S(1)}, u32[]{:S(2)}, u32[]{:S(2)}) collective-permute-start(bf16[1,48,2304]{2,1,0:T(8,128)(2,1)} %get-tuple-element.657), channel_id=1, source_target_pairs={{0,8},{1,9},{2,10},{3,11},{4,12},{5,13},{6,14},{7,15},{8,0},{9,1},... | collective-permute-start | bytes 663560 | tf_op jit(solution)/shard_map/ppermute | solution.py:21
  332.7 19.7 %collective-permute-start.38 = (bf16[1,48,2304]{2,1,0:T(8,128)(2,1)}, bf16[1,48,2304]{2,1,0:T(8,128)(2,1)S(1)}, u32[]{:S(2)}, u32[]{:S(2)}) collective-permute-start(bf16[1,48,2304]{2,1,0:T(8,128)(2,1)} %get-tuple-element.658), channel_id=1, source_target_pairs={{0,12},{1,13},{2,14},{3,15},{4,8},{5,9},{6,10},{7,11},{8,4},{9,5},... | collective-permute-start | bytes 663560 | tf_op jit(solution)/shard_map/ppermute | solution.py:21
  340.6 17.9 %collective-permute-start.41 = (bf16[1,48,1536]{2,1,0:T(8,128)(2,1)S(1)}, bf16[1,48,1536]{2,1,0:T(8,128)(2,1)S(1)}, u32[]{:S(2)}, u32[]{:S(2)}) collective-permute-start(bf16[1,48,1536]{2,1,0:T(8,128)(2,1)S(1)} %get-tuple-element.688), channel_id=1, source_target_pairs={{0,8},{1,9},{2,10},{3,11},{4,12},{5,13},{6,14},{7,15},{8,0},{9,1},... | collective-permute-start | bytes 442376 | tf_op jit(solution)/shard_map/ppermute | solution.py:21
  352.5 13.5 %collective-permute-start.42 = (bf16[48,2304]{1,0:T(8,128)(2,1)S(1)}, bf16[48,2304]{1,0:T(8,128)(2,1)S(1)}, u32[]{:S(2)}, u32[]{:S(2)}) collective-permute-start(bf16[48,2304]{1,0:T(8,128)(2,1)S(1)} %bitcast.50), channel_id=1, source_target_pairs={{0,16},{16,0},{1,17},{17,1},{2,18},{18,2},{3,19},{19,3},{4,20},{20... | collective-permute-start | bytes 663560 | tf_op jit(solution)/shard_map/ppermute | solution.py:21
  361.1 6.0 %collective-permute-start.43 = (bf16[1,48,1024]{2,1,0:T(8,128)(2,1)S(1)}, bf16[1,48,1024]{2,1,0:T(8,128)(2,1)S(1)}, u32[]{:S(2)}, u32[]{:S(2)}) collective-permute-start(bf16[1,48,1024]{2,1,0:T(8,128)(2,1)S(1)} %get-tuple-element.704), channel_id=1, source_target_pairs={{0,4},{1,5},{2,6},{3,7},{4,0},{5,1},{6,2},{7,3},{8,12},{9,13},{10,... | collective-permute-start | bytes 294920 | tf_op jit(solution)/shard_map/ppermute | solution.py:21
  361.1 8.9 %collective-permute-start.44 = (bf16[1,48,1024]{2,1,0:T(8,128)(2,1)S(1)}, bf16[1,48,1024]{2,1,0:T(8,128)(2,1)S(1)}, u32[]{:S(2)}, u32[]{:S(2)}) collective-permute-start(bf16[1,48,1024]{2,1,0:T(8,128)(2,1)S(1)} %get-tuple-element.705), channel_id=1, source_target_pairs={{0,8},{1,9},{2,10},{3,11},{4,12},{5,13},{6,14},{7,15},{8,0},{9,1},... | collective-permute-start | bytes 294920 | tf_op jit(solution)/shard_map/ppermute | solution.py:21
  363.1 6.9 %collective-permute-start.45 = (bf16[1,48,1024]{2,1,0:T(8,128)(2,1)S(1)}, bf16[1,48,1024]{2,1,0:T(8,128)(2,1)S(1)}, u32[]{:S(2)}, u32[]{:S(2)}) collective-permute-start(bf16[1,48,1024]{2,1,0:T(8,128)(2,1)S(1)} %get-tuple-element.706), channel_id=1, source_target_pairs={{0,12},{1,13},{2,14},{3,15},{4,8},{5,9},{6,10},{7,11},{8,4},{9,5},... | collective-permute-start | bytes 294920 | tf_op jit(solution)/shard_map/ppermute | solution.py:21
  365.5 6.2 %collective-permute-start.46 = (bf16[48,1536]{1,0:T(8,128)(2,1)S(1)}, bf16[48,1536]{1,0:T(8,128)(2,1)S(1)}, u32[]{:S(2)}, u32[]{:S(2)}) collective-permute-start(bf16[48,1536]{1,0:T(8,128)(2,1)S(1)} %bitcast.51), channel_id=1, source_target_pairs={{0,16},{16,0},{1,17},{17,1},{2,18},{18,2},{3,19},{19,3},{4,20},{20... | collective-permute-start | bytes 442376 | tf_op jit(solution)/shard_map/ppermute | solution.py:21
  370.1 4.7 %collective-permute-start.47 = (bf16[48,1024]{1,0:T(8,128)(2,1)S(1)}, bf16[48,1024]{1,0:T(8,128)(2,1)S(1)}, u32[]{:S(2)}, u32[]{:S(2)}) collective-permute-start(bf16[48,1024]{1,0:T(8,128)(2,1)S(1)} %bitcast.52), channel_id=1, source_target_pairs={{0,16},{16,0},{1,17},{17,1},{2,18},{18,2},{3,19},{19,3},{4,20},{20... | collective-permute-start | bytes 294920 | tf_op jit(solution)/shard_map/ppermute | solution.py:21
  (63 other events, 847.2 us)
where the time goes:
time: 382 us; the launch traced here: 381 us
  Pallas kernels  197 us (52%)
  waiting for transfers between devices  106 us (28%)
  starting transfers between devices  48.5 us (13%)
  local copies, waits for them, and re-layouts  24.3 us (6%)
    ppermute x48, waiting for transfers between devices, swap(): return lax.ppermute(value, axis, [(i, i ^ bit) for i in range(size)])  106 us
    pallas_call x1, Pallas kernels, feed_all(): pl.pallas_call(functools.partial(feed_kernel, starts, chunk), grid_spec=p...  68.6 us
    ppermute x48, starting transfers between devices, swap(): return lax.ppermute(value, axis, [(i, i ^ bit) for i in range(size)])  48.5 us
    pallas_call x2, Pallas kernels, attend_backward(): pl.pallas_call(functools.partial(attend_back_kernel, starts, chunk), grid...  34.2 us
    pallas_call x1, Pallas kernels, leave_all(): pl.pallas_call(functools.partial(leave_kernel, qkv_parts.pieces, starts,...  23.9 us
    pallas_call x1, Pallas kernels, attend_forward(): pl.pallas_call(functools.partial(attend_kernel, starts, chunk), grid=(pai...  18.2 us
    unnamed x125, local copies, waits for them, and re-layouts  15.4 us
    pallas_call x1, Pallas kernels, enter_all(): pl.pallas_call(functools.partial(enter_kernel, embed_parts.pieces, qkv_pa...  14.9 us
  transfers between devices with their start and end apart: 48, of which 21 were waited for; matrix products, arithmetic and copies ran while one was open for 2% of the time, Pallas kernels for 30%

commit v1 on v0

--- a/solution.py
+++ b/solution.py
@@ -26,8 +26,8 @@
 
 
 class Gather:
-    def __init__(self, shard, where, count, steps, split=False):
-        self.count, self.split, self.columns = count, split, shard.shape[1]
+    def __init__(self, shard, where, count, steps, split=False, joined=True):
+        self.count, self.split, self.columns, self.joined = count, split, shard.shape[1], joined
         if split:
             width = shard.shape[1] // 2
             shard = lax.dynamic_slice_in_dim(shard, where[1] * width, width, 1)
@@ -41,7 +41,8 @@
         if not self.steps:
             self.ready = []
             return
-        if len(self.held) > 1 and len(self.held[0]) == 2:
+        last = self.steps[0] in ("rep", "core")
+        if len(self.held) > 1 and len(self.held[0]) == 2 and (self.joined or not last):
             offsets = [o for _, offsets in self.held for o in offsets]
             self.held = [(join([blocks for blocks, _ in self.held]), offsets)]
         self.ready = [blocks for blocks, *_ in self.held]
@@ -85,6 +86,7 @@
         chain.take(flat[:size])
         chain.prepare()
         flat = flat[size:]
+        chain.sent = []
     sizes = [len(chain.ready) for chain in chains]
     anchor, *flat = after(anchor, *[part for chain in chains for part in chain.ready])
     for chain, size in zip(chains, sizes):
@@ -108,6 +110,7 @@
 
 
 def complete(anchor, *chains):
+    chains = [chain for chain in chains if chain.sent]
     while chains:
         left = [chain for chain in chains if chain.steps]
         anchor = go_on(anchor, *chains)
@@ -205,16 +208,17 @@
             self.pieces = [(tuple(range(16)), None, 0, self.columns)]
             self.where = jnp.zeros_like(where)
 
-    def pairs(self, halves):
+    def quarters(self, halves):
         if len(self.parts) > 1:
-            near = len(self.parts) // 2
-            assert near == halves and all(piece[0] == ORDER for piece in self.pieces[:near])
+            assert len(self.parts) == 4 * halves
+            assert self.pieces[0][0] + self.pieces[1][0] == ORDER
             return self.parts
         size = self.columns // halves
         return [
-            jnp.stack([self.parts[0][o + core, :, h * size : (h + 1) * size] for o in ORDER])
+            jnp.stack([self.parts[0][o + core, :, h * size : (h + 1) * size] for o in quarter])
             for core in range(2)
             for h in range(halves)
+            for quarter in (ORDER[:4], ORDER[4:])
         ]
 
 
@@ -514,7 +518,7 @@
         functools.partial(unpatch_kernel, embed_parts.pieces, starts, bounds),
         out_shape=[jax.ShapeDtypeStruct((1, 3, s, s), BF16) for s in sides],
         in_specs=[pl.BlockSpec(memory_space=pltpu.SMEM), whole]
-        + [pl.BlockSpec(memory_space=pl.ANY)] * len(parts),
+        + [pl.BlockSpec(memory_space=pltpu.HBM)] * len(parts),
         out_specs=[whole] * 3,
         scratch_shapes=[
             pltpu.VMEM(
@@ -615,7 +619,7 @@
     pair = pl.program_id(0)
     *done, out_ref, left, right, acc = refs
     if done:
-        out_ref[:, : starts[0], :] = done[0][:, : starts[0], :]
+        out_ref[:, : starts[0], :] = done[0][...]
     scale = HEAD ** -0.5
     zero = jnp.zeros((), BF16)
     for begin, end in zip(starts, starts[1:]):
@@ -660,7 +664,7 @@
         out_ref[0, begin:end, :] = (jnp.where(lane < HEAD, acc[0, :size, :], acc[1, :size, :]) * scale).astype(BF16)
 
 def attend_backward(qkv, mixed, totals, grad_mixed, starts, done=(), chunk=400):
-    rows, width = mixed.shape
+    rows, width = starts[-1], mixed.shape[1]
     pairs = width // 128
     longest = max(e - s for s, e in zip(starts, starts[1:]))
     block = lambda first: pl.BlockSpec((rows, 128), lambda j: (0, first * pairs + j))
@@ -668,10 +672,15 @@
         functools.partial(attend_back_kernel, starts, chunk),
         grid=(pairs,),
         out_shape=jax.ShapeDtypeStruct((3, rows, width), BF16),
-        in_specs=[block(0), block(1), block(2), block(0), block(0), pl.BlockSpec((rows, 128), lambda j: (0, 0))]
-        + [pl.BlockSpec((3, rows, 128), lambda j: (0, 0, j))][: len(done)],
+        in_specs=[block(0), block(1), block(2), block(0), block(0)]
+        + [pl.BlockSpec((rows, 128), lambda j: (0, 0))]
+        + [pl.BlockSpec((3, starts[0], 128), lambda j: (0, 0, j))][: len(done)],
         out_specs=pl.BlockSpec((3, rows, 128), lambda j: (0, 0, j)),
-        scratch_shapes=[pltpu.VMEM((2, longest, 128), BF16), pltpu.VMEM((2, longest, 128), BF16), pltpu.VMEM((2, longest, 128), F32)],
+        scratch_shapes=[
+            pltpu.VMEM((2, longest, 128), BF16),
+            pltpu.VMEM((2, longest, 128), BF16),
+            pltpu.VMEM((2, longest, 128), F32),
+        ],
         compiler_params=pltpu.CompilerParams(vmem_limit_bytes=24 * 2**20),
         cost_estimate=BRIEF,
     )(qkv, qkv, qkv, mixed, grad_mixed, totals, *done)
@@ -812,7 +821,7 @@
         ),
         in_specs=[pl.BlockSpec(memory_space=pltpu.SMEM)]
         + [whole] * 4
-        + [anywhere] * len(parts),
+        + [pl.BlockSpec(memory_space=pltpu.HBM)] * len(parts),
         out_specs=[whole] * 6,
         scratch_shapes=[
             pltpu.VMEM((rows, width), BF16),
@@ -872,13 +881,13 @@
 
 def feed_kernel(starts, chunk, where_ref, *refs):
     mixed_ref, embedded_ref, lines_ref, b_up_ref = refs[:4]
-    up_parts, down_parts, cotangents = refs[4:8], refs[8:10], refs[10:13]
-    finals = refs[13:16]
-    up_keep, up_give, down_keep, down_give, g_bias_ref = refs[16:21]
-    branch_ref, g_mixed_ref, sums_ref = refs[21:24]
-    middle, normed, grads, act, grad_up, total, back = refs[24:31]
-    w_up, w_down, w_out, g_up, g_down, g_out = refs[31:37]
-    up_in, down_in, out_in, up_out, down_out, out_out, one, ends = refs[37:]
+    up_parts, down_parts, cotangents, refs = refs[4:12], refs[12:16], refs[16:19], refs[19:]
+    finals = refs[:3]
+    up_keep, up_give, down_keep, down_give, g_bias_ref = refs[3:8]
+    branch_ref, g_mixed_ref, sums_ref = refs[8:11]
+    middle, normed, grads, act, grad_up, total, back = refs[11:18]
+    w_up, w_down, w_out, g_up, g_down, g_out = refs[18:24]
+    up_in, down_in, out_in, up_out, down_out, out_out, one, ends = refs[24:]
     step, steps = pl.program_id(0), pl.num_programs(0)
     rows = middle.shape[0]
     me, other = where_ref[0], where_ref[1]
@@ -894,7 +903,9 @@
         t = lax.bitwise_xor(s, me // 4)
         return [
             pltpu.make_async_copy(
-                up_parts[2 * (d % 2) + half].at[ORDER.index(d - d % 2), :, at(lax.rem(t, 2), tile)],
+                up_parts[4 * (d % 2) + 2 * half + ORDER.index(d - d % 2) // 4].at[
+                    ORDER.index(d - d % 2) % 4, :, at(lax.rem(t, 2), tile)
+                ],
                 w_up.at[lax.rem(s, 2), at(lax.bitwise_xor(me, d), up_rows), :],
                 up_in.at[lax.rem(s, 2), d],
             )
@@ -904,10 +915,10 @@
     def load_down(s):
         copies = []
         for j in range(4):
-            place_ = s // 2 + 2 * lax.rem(s, 2) + 4 * (j // 2)
+            place_ = s // 2 + 2 * lax.rem(s, 2)
             copies.append(
                 pltpu.make_async_copy(
-                    down_parts[j % 2].at[place_, pl.ds(0, down_rows), :],
+                    down_parts[2 * (j % 2) + j // 2].at[place_, pl.ds(0, down_rows), :],
                     w_down.at[lax.rem(s, 2), at(lax.bitwise_xor(lax.rem(me, 4), j), down_rows), :],
                     down_in.at[lax.rem(s, 2), j],
                 )
@@ -930,7 +941,9 @@
     def load_out():
         return [
             pltpu.make_async_copy(
-                down_parts[d % 2].at[ORDER.index(d - d % 2), pl.ds(down_rows, up_rows), :],
+                down_parts[2 * (d % 2) + ORDER.index(d - d % 2) // 4].at[
+                    ORDER.index(d - d % 2) % 4, pl.ds(down_rows, up_rows), :
+                ],
                 w_out.at[at(lax.bitwise_xor(me, d), up_rows), :],
                 out_in.at[d],
             )
@@ -1080,7 +1093,7 @@
             num_scalar_prefetch=1,
             grid=(4,),
             in_specs=[fixed(rows, width), anywhere, fixed(16, width), mine]
-            + [anywhere] * 6
+            + [pl.BlockSpec(memory_space=pltpu.HBM)] * 12
             + [fixed(*c.shape) for c in cotangents],
             out_specs=[anywhere] * 7 + [mine, anywhere, anywhere, whole(8, width)],
             scratch_shapes=[
@@ -1249,7 +1262,7 @@
         + [jax.ShapeDtypeStruct((2, 8, block, high_columns), BF16)] * 2,
         in_specs=[pl.BlockSpec(memory_space=pltpu.SMEM)]
         + [whole] * 11
-        + [anywhere] * len(parts),
+        + [pl.BlockSpec(memory_space=pltpu.HBM)] * len(parts),
         out_specs=[whole] + [anywhere] * 4,
         scratch_shapes=[
             pltpu.VMEM((rows, width), BF16),
@@ -1299,7 +1312,6 @@
     inward = [(bit,) for bit in bits]
     outward = inward[::-1]
     turned = inward[:1] + outward[:-1]
-    short = inward[:-2] + [(bits[-2], bits[-1], bits[-2] + bits[-1])]
 
     up_per = up_bias.shape[0] // share
     used = spots + 9 + up_per
@@ -1332,20 +1344,21 @@
     down_rows = (down_weight.shape[0], out_weight.shape[0])
     down_block = jnp.concatenate([down_weight, out_weight])
     qkv_shards = Gather(qkv_weight, where, count, outward, split=True).send()
-    up_shards = Gather(up_weight, where, count, outward, split=True).send()
+    up_shards = Gather(up_weight, where, count, outward, split=True, joined=False).send()
     shards = resize_all(resizes, base_turned, posemb.T, vectors, bounds, columns)
     embed_low = Gather(shards[0], where, count, outward).send()
     embed_high = Gather(shards[1], where, count, outward).send()
     held = go_on((pixels, maps, *shards), qkv_shards, embed_low, qkv_shards, embed_high, up_shards)
-    pixels, maps, *_ = go_on(held, embed_low, qkv_shards)
+    held = go_on(held, embed_low, qkv_shards)
+    held, down_block = after(held, down_block)
+    down_shards = Gather(down_block, where, count, outward, joined=False).send()
+    held = finish(held, embed_high, up_shards)
+    embed_high.send()
+    pixels, maps, *_ = held
     patches = patch_all(pixels)
-    patches = finish(patches, embed_high, up_shards)
-    embed_high.send()
-    patches, down_block = after(patches, down_block)
-    down_shards = Gather(down_block, where, count, outward).send()
-    patches = go_on(patches, embed_low, qkv_shards, embed_high, down_shards)
+    patches, maps = together((patches, maps), embed_low, embed_high, qkv_shards, down_shards)
+    patches, maps = complete((patches, maps), embed_low, qkv_shards, embed_high)
     up_shards.send()
-    patches, maps = complete((patches, maps), embed_low, qkv_shards, embed_high)
     w_qkv = Parts([qkv_shards], where, count)
     w_embed = Parts([embed_low, embed_high], where, count)
     embedded, units, qkv, lines, inverse, columns_small = enter_all(
@@ -1370,7 +1383,7 @@
         grad_mixed,
         sums,
     ) = feed_all(
-        w_up.where, mixed, embedded, lines, b_up, w_up.pairs(2), w_down.pairs(1), cotangents, starts
+        w_up.where, mixed, embedded, lines, b_up, w_up.quarters(2), w_down.quarters(1), cotangents, starts
     )
     rows16 = (down_rows[0] * count // 16, down_rows[1] * count // 16)
     down_sums = Scatter(
@@ -1379,9 +1392,9 @@
     up_sums = Scatter(
         *ordered(up_keep, up_give, where, count, split=True), where, count, inward, split=True
     ).send()
-    grad_qkv = attend_backward(qkv, mixed, totals, grad_mixed, starts[:3])
+    grad_qkv = attend_backward(qkv, mixed, totals, grad_mixed, starts[:2])
     grad_qkv = together(grad_qkv, down_sums, up_sums)
-    grad_qkv = attend_backward(qkv, mixed, totals, grad_mixed, starts[2:], (grad_qkv,))
+    grad_qkv = attend_backward(qkv, mixed, totals, grad_mixed, starts[1:], (grad_qkv,))
     grad_qkv = together(grad_qkv, down_sums, up_sums)
     half = columns // 2
     low_columns = half + 5 * width // 3
@@ -1401,14 +1414,22 @@
         spots,
         low_columns,
     )
-    grad_low, *shares = together((grad_low, *shares), down_sums, up_sums)
-    low_sums = Scatter(*ordered(*shares[:2], where, count), where, count, short).send()
+    grad_low, *arrived = after((grad_low, *shares), *down_sums.sent, *up_sums.sent)
+    grad_low, *shares = grad_low
+    low_sums = Scatter(*ordered(*shares[:2], where, count), where, count, inward).send()
     high_sums = Scatter(
-        *ordered(*shares[2:], where, count, split=True), where, count, short, split=True
+        *ordered(*shares[2:], where, count, split=True), where, count, inward, split=True
     ).send()
-    grad_low = go_on(grad_low, low_sums, high_sums)
+    for chain in (down_sums, up_sums):
+        chain.sent, arrived = arrived[: len(chain.sent)], arrived[len(chain.sent) :]
+    grad_low = together(grad_low, down_sums, up_sums)
+    grad_low = together(grad_low, low_sums)
+    grad_low = together(grad_low, high_sums)
     pixel_grads = unpatch_all(grad_low, w_embed, starts, bounds, [p.shape[2] for p in pixels])
-    pixel_grads = complete(pixel_grads, low_sums, high_sums, down_sums, up_sums)
+    pixel_grads = together(pixel_grads, down_sums, up_sums)
+    pixel_grads = go_on(pixel_grads, high_sums, low_sums, high_sums, low_sums, high_sums)
+    pixel_grads = go_on(pixel_grads, up_sums, low_sums)
+    pixel_grads = complete(pixel_grads, down_sums, high_sums, up_sums, low_sums)
 
     low, high = low_sums.result, high_sums.result
     quarter = half // 2

time: 382 us -> 364 us (0.953)
  waiting for transfers between devices: 106 us -> 96.5 us
  Pallas kernels: 197 us -> 190 us
  local copies, waits for them, and re-layouts: 24.3 us -> 29.2 us
  starting transfers between devices: 48.5 us -> 43.8 us
    ppermute x48 -> x50, waiting for transfers between devices: 106 us -> 96.5 us  [swap(): return lax.ppermute(value, axis, [(i, i ^ bit) for i in range(size)])]
    unnamed x125, local copies, waits for them, and re-layouts: 15.4 us -> 20.4 us
    ppermute x48 -> x50, starting transfers between devices: 48.5 us -> 43.8 us  [swap(): return lax.ppermute(value, axis, [(i, i ^ bit) for i in range(size)])]
    pallas_call x2, Pallas kernels: 34.2 us -> 30.4 us  [attend_backward(): pl.pallas_call(functools.partial(attend_back_kernel, starts, chunk), grid...]
    pallas_call x16 -> x18, Pallas kernels: 8.22 us -> 7.54 us  [merge(): pl.pallas_call(functools.partial(merge_kernel, groups, len(parts)), out_s...]
  transfers between devices with their start and end apart: 48 -> 50, of which waited for: 21 -> 23; matrix products, arithmetic and copies ran while one was open for 2% -> 2% of each run, Pallas kernels for 30% -> 31%
where the time goes in v1:
time: 364 us; the launch traced here: 363 us
  Pallas kernels  190 us (52%)
  waiting for transfers between devices  96.5 us (27%)
  starting transfers between devices  43.8 us (12%)
  local copies, waits for them, and re-layouts  29.2 us (8%)
    ppermute x50, waiting for transfers between devices, swap(): return lax.ppermute(value, axis, [(i, i ^ bit) for i in range(size)])  96.5 us
    pallas_call x1, Pallas kernels, feed_all(): pl.pallas_call(functools.partial(feed_kernel, starts, chunk), grid_spec=p...  68.6 us
    ppermute x50, starting transfers between devices, swap(): return lax.ppermute(value, axis, [(i, i ^ bit) for i in range(size)])  43.8 us
    pallas_call x2, Pallas kernels, attend_backward(): pl.pallas_call(functools.partial(attend_back_kernel, starts, chunk), grid...  30.4 us
    pallas_call x1, Pallas kernels, leave_all(): pl.pallas_call(functools.partial(leave_kernel, qkv_parts.pieces, starts,...  23.9 us
    unnamed x125, local copies, waits for them, and re-layouts  20.4 us
    pallas_call x1, Pallas kernels, attend_forward(): pl.pallas_call(functools.partial(attend_kernel, starts, chunk), grid=(pai...  18.2 us
    pallas_call x1, Pallas kernels, enter_all(): pl.pallas_call(functools.partial(enter_kernel, embed_parts.pieces, qkv_pa...  14.9 us
  transfers between devices with their start and end apart: 50, of which 23 were waited for; matrix products, arithmetic and copies ran while one was open for 2% of the time, Pallas kernels for 31%

profile of v1, /device:TPU:0, one launch (start us, length us, event | category | flops | bytes accessed | tf_op | source)
XLA Modules:
  0.0 363.2 jit_solution(10484329030449869572)
XLA Ops:
  1.7 4.1 %collective-permute-start = (bf16[1,48,1152]{2,1,0:T(8,128)(2,1)S(1)}, bf16[1,48,1152]{2,1,0:T(8,128)(2,1)S(1)}, u32[]{:S(2)}, u32[]{:S(2)}) collective-permute-start(bf16[1,48,1152]{2,1,0:T(8,128)(2,1)S(1)} %dynamic-slice_bitcast_fusion.1.refs_0_), channel_id=1, source_target_pairs={{0,8},{1,9},{2,10},{3,11},{4,12},{5,13},{6,14},{7,15},{8,0},{9,1},... | collective-permute-start | bytes 331784 | tf_op jit(solution)/shard_map/ppermute | solution.py:21
  8.5 4.6 %shard_map.418 = (bf16[48,1024]{1,0:T(8,128)(2,1)}, bf16[48,1024]{1,0:T(8,128)(2,1)}) custom-call(f32[100,1024]{1,0:T(8,128)} %refs_0_.4, f32[144,1024]{1,0:T(8,128)} %refs_1_.4, f32[256,1024]{1,0:T(8,128)} %refs_2_.4, bf16[3,48,1024]{2,1,0:T(8,128)(2,1)} %bitcast.59, bf16[48,49]{1,0:T(8,128)(2,1)} %bitcast.61, bf16[1,48]{1,0:T(2,128)(2,1)} %bitcast.62, ...), custom_call_target="tpu_custom_call" | custom-call | flops 1 | bytes 1 | tf_op jit(solution)/shard_map/pallas_call | solution.py:750
  13.1 1.6 collective-permute-start.2
  15.4 6.0 %collective-permute-done.1.refs_1_ = bf16[1,48,1024]{2,1,0:T(8,128)(2,1)S(1)} collective-permute-done((bf16[1,48,1024]{2,1,0:T(8,128)(2,1)}, bf16[1,48,1024]{2,1,0:T(8,128)(2,1)S(1)}, u32[]{:S(2)}, u32[]{:S(2)}) %collective-permute-start.1) | collective-permute-done | bytes 98336 | tf_op jit(solution)/shard_map/ppermute | solution.py:21
  22.4 1.6 collective-permute-start.6
  23.9 1.8 collective-permute-start.5
  25.7 1.6 collective-permute-start.4
  27.3 1.4 collective-permute-start.3
  28.7 9.8 %collective-permute-done.3.refs_1_ = bf16[1,48,1024]{2,1,0:T(8,128)(2,1)S(1)} collective-permute-done((bf16[1,48,1024]{2,1,0:T(8,128)(2,1)S(1)}, bf16[1,48,1024]{2,1,0:T(8,128)(2,1)S(1)}, u32[]{:S(2)}, u32[]{:S(2)}) %collective-permute-start.3) | collective-permute-done | bytes 98336 | tf_op jit(solution)/shard_map/ppermute | solution.py:21
  38.7 1.6 collective-permute-start.11
  40.3 2.0 collective-permute-start.7
  43.0 8.7 %collective-permute-done.7.refs_1_ = bf16[2,48,1024]{2,1,0:T(8,128)(2,1)S(1)} collective-permute-done((bf16[2,48,1024]{2,1,0:T(8,128)(2,1)S(1)}, bf16[2,48,1024]{2,1,0:T(8,128)(2,1)S(1)}, u32[]{:S(2)}, u32[]{:S(2)}) %collective-permute-start.7) | collective-permute-done | bytes 196640 | tf_op jit(solution)/shard_map/ppermute | solution.py:21
  53.1 6.8 %shard_map.428 = (bf16[256,512]{1,0:T(8,128)(2,1)S(1)}, bf16[400,640]{1,0:T(8,128)(2,1)S(1)}, bf16[576,768]{1,0:T(8,128)(2,1)S(1)}) custom-call(bf16[1,3,160,160]{3,2,1,0:T(8,128)(2,1)S(1)} %copy-done.46, bf16[1,3,240,240]{3,2,1,0:T(8,128)(2,1)S(1)} %copy-done.45, bf16[1,3,384,384]{3,2,1,0:T(8,128)(2,1)S(1)} %copy-done.38), custom_call_target="tpu_custom_call" | custom-call | flops 1 | bytes 1 | tf_op jit(solution)/shard_map/pallas_call | solution.py:466
  60.8 8.7 %collective-permute-done.12.refs_1_ = bf16[1,240,768]{2,1,0:T(8,128)(2,1)S(1)} collective-permute-done((bf16[1,240,768]{2,1,0:T(8,128)(2,1)S(1)}, bf16[1,240,768]{2,1,0:T(8,128)(2,1)S(1)}, u32[]{:S(2)}, u32[]{:S(2)}) %collective-permute-start.12) | collective-permute-done | bytes 368672 | tf_op jit(solution)/shard_map/ppermute | solution.py:21
  71.6 1.6 collective-permute-done.13.refs_5_.refs_1_
  74.2 1.5 collective-permute-start.17
  81.0 14.9 %shard_map.432 = (f32[1232,768]{1,0:T(8,128)}, bf16[1232,768]{1,0:T(8,128)(2,1)S(1)}, bf16[1232,2304]{1,0:T(8,128)(2,1)}, f32[16,768]{1,0:T(8,128)S(1)}, f32[123...) custom-call(s32[2]{0:T(128)S(1)} %pad_add_fusion.where_ref, bf16[256,512]{1,0:T(8,128)(2,1)S(1)} %copy-done.36, ...), custom_call_target="tpu_custom_call" | custom-call | flops 1 | bytes 1 | tf_op jit(solution)/shard_map/pallas_call | solution.py:810
  96.0 2.3 shard_map.433.refs_12_
  98.3 1.6 collective-permute-start.21
  100.4 1.5 collective-permute-start.20
  102.0 2.6 copy-done.2
  104.6 18.2 %shard_map.434 = (bf16[1232,768]{1,0:T(8,128)(2,1)S(1)}, f32[1232,128]{1,0:T(8,128)S(1)}) custom-call(bf16[1232,2304]{1,0:T(8,128)(2,1)S(1)} %copy-done.2, bf16[1232,2304]{1,0:T(8,128)(2,1)S(1)} %copy-done.2, bf16[1232,2304]{1,0:T(8,128)(2,1)S(1)} %copy-done.2), custom_call_target="tpu_custom_call" | custom-call | flops 1 | bytes 1 | tf_op jit(solution)/shard_map/pallas_call | solution.py:601
  124.1 3.9 %collective-permute-done.20.refs_7_ = bf16[4,48,1536]{2,1,0:T(8,128)(2,1)} collective-permute-done((bf16[4,48,1536]{2,1,0:T(8,128)(2,1)}, bf16[4,48,1536]{2,1,0:T(8,128)(2,1)}, u32[]{:S(2)}, u32[]{:S(2)}) %collective-permute-start.20) | collective-permute-done | bytes 589856 | tf_op jit(solution)/shard_map/ppermute | solution.py:21
  128.0 4.9 %collective-permute-done.21.refs_13_ = bf16[4,240,768]{2,1,0:T(8,128)(2,1)} collective-permute-done((bf16[4,240,768]{2,1,0:T(8,128)(2,1)S(1)}, bf16[4,240,768]{2,1,0:T(8,128)(2,1)}, u32[]{:S(2)}, u32[]{:S(2)}) %collective-permute-start.21) | collective-permute-done | bytes 1474592 | tf_op jit(solution)/shard_map/ppermute | solution.py:21
  133.9 6.2 %collective-permute-done.22.refs_8_ = bf16[4,48,1536]{2,1,0:T(8,128)(2,1)S(1)} collective-permute-done((bf16[4,48,1536]{2,1,0:T(8,128)(2,1)}, bf16[4,48,1536]{2,1,0:T(8,128)(2,1)S(1)}, u32[]{:S(2)}, u32[]{:S(2)}) %collective-permute-start.22) | collective-permute-done | bytes 589856 | tf_op jit(solution)/shard_map/ppermute | solution.py:21
  142.5 68.6 %shard_map.435 = (bf16[1,256,768]{2,1,0:T(8,128)(2,1)}, bf16[1,400,768]{2,1,0:T(8,128)(2,1)}, bf16[1,576,768]{2,1,0:T(8,128)(2,1)}, bf16[2,8,48,1536]{3,2,1,0:T(...) custom-call(s32[2]{0:T(128)} %copy-done.52, ...), custom_call_target="tpu_custom_call" | custom-call | flops 1 | bytes 1 | tf_op jit(solution)/shard_map/pallas_call | solution.py:1090
  211.6 1.5 copy-done.8
  214.2 6.4 %shard_map.436.refs_0_ = bf16[3,256,768]{2,1,0:T(8,128)(2,1)S(1)} custom-call(bf16[1232,2304]{1,0:T(8,128)(2,1)S(1)} %bitcast.42, bf16[1232,2304]{1,0:T(8,128)(2,1)S(1)} %bitcast.42, bf16[1232,2304]{1,0:T(8,128)(2,1)S(1)} %bitcast.42, bf16[1232,768]{1,0:T(8,128)(2,1)S(1)} %copy-done.5, bf16[1232,768]{1,0:T(8,128)(2,1)S(1)} %copy-done.8, ...), custom_call_target="tpu_custom_call" | custom-call | flops 1 | bytes 1 | tf_op jit(solution)/shard_map/pallas_call | solution.py:671
  222.9 1.6 collective-permute-start.30
  225.0 24.0 %shard_map.439.refs_0_ = bf16[3,1232,768]{2,1,0:T(8,128)(2,1)S(1)} custom-call(bf16[1232,2304]{1,0:T(8,128)(2,1)S(1)} %bitcast.42, bf16[1232,2304]{1,0:T(8,128)(2,1)S(1)} %bitcast.42, bf16[1232,2304]{1,0:T(8,128)(2,1)S(1)} %bitcast.42, bf16[1232,768]{1,0:T(8,128)(2,1)S(1)} %copy-done.5, bf16[1232,768]{1,0:T(8,128)(2,1)S(1)} %copy-done.9, ...), custom_call_target="tpu_custom_call" | custom-call | flops 1 | bytes 1 | tf_op jit(solution)/shard_map/pallas_call | solution.py:671
  249.0 2.4 copy-done.3
  252.2 5.1 %collective-permute-done.30.refs_1_ = bf16[4,240,768]{2,1,0:T(8,128)(2,1)S(1)} collective-permute-done((bf16[4,240,768]{2,1,0:T(8,128)(2,1)S(1)}, bf16[4,240,768]{2,1,0:T(8,128)(2,1)S(1)}, u32[]{:S(2)}, u32[]{:S(2)}) %collective-permute-start.30) | collective-permute-done | bytes 1474592 | tf_op jit(solution)/shard_map/ppermute | solution.py:21
  260.3 1.5 collective-permute-start.33
  263.5 23.9 %shard_map.442 = (bf16[1232,768]{1,0:T(8,128)(2,1)}, bf16[8,48,2304]{2,1,0:T(8,128)(2,1)}, bf16[8,48,2304]{2,1,0:T(8,128)(2,1)}, bf16[2,8,48,1024]{3,2,1,0:T(8,128)(2,1)S(1)}, bf16[2,8,48,1024]{3,2,1,0:T(8,128)(2,1)S(1)}) custom-call(s32[2]{0:T(128)S(1)} %copy-done.53, bf16[3,1232,768]{2,1,0:T(8,128)(2,1)} %copy-done.3, bf16[1232,768]{1,0:T(8,128)(2,1)} %copy-done.32, ...), custom_call_target="tpu_custom_call" | custom-call | flops 1 | bytes 1 | tf_op jit(solution)/shard_map/pallas_call | solution.py:1256
  290.5 2.6 collective-permute-done.34.refs_1_
  297.8 8.4 %shard_map.447 = (bf16[1,3,160,160]{3,2,1,0:T(8,128)(2,1)}, bf16[1,3,240,240]{3,2,1,0:T(8,128)(2,1)}, bf16[1,3,384,384]{3,2,1,0:T(8,128)(2,1)}) custom-call(s32[2]{0:T(128)S(1)} %copy-done.53, bf16[1232,768]{1,0:T(8,128)(2,1)S(1)} %copy-done.31, bf16[8,48,1024]{2,1,0:T(8,128)(2,1)S(1)} %copy-done.11, bf16[8,48,1024]{2,1,0:T(8,128)(2,1)S(1)} %copy-done.21, ...), custom_call_target="tpu_custom_call" | custom-call | flops 1 | bytes 1 | tf_op jit(solution)/shard_map/pallas_call | solution.py:517
  306.2 4.3 %collective-permute-done.37.refs_1_ = bf16[2,48,1536]{2,1,0:T(8,128)(2,1)S(1)} collective-permute-done((bf16[2,48,1536]{2,1,0:T(8,128)(2,1)S(1)}, bf16[2,48,1536]{2,1,0:T(8,128)(2,1)S(1)}, u32[]{:S(2)}, u32[]{:S(2)}) %collective-permute-start.37) | collective-permute-done | bytes 294944 | tf_op jit(solution)/shard_map/ppermute | solution.py:21
  310.5 4.1 %collective-permute-done.36.refs_1_ = bf16[1,240,768]{2,1,0:T(8,128)(2,1)S(1)} collective-permute-done((bf16[1,240,768]{2,1,0:T(8,128)(2,1)S(1)}, bf16[1,240,768]{2,1,0:T(8,128)(2,1)S(1)}, u32[]{:S(2)}, u32[]{:S(2)}) %collective-permute-start.36) | collective-permute-done | bytes 368672 | tf_op jit(solution)/shard_map/ppermute | solution.py:21
  316.2 1.8 collective-permute-start.41
  318.5 6.4 %collective-permute-done.40.refs_1_ = bf16[4,48,1024]{2,1,0:T(8,128)(2,1)S(1)} collective-permute-done((bf16[4,48,1024]{2,1,0:T(8,128)(2,1)S(1)}, bf16[4,48,1024]{2,1,0:T(8,128)(2,1)S(1)}, u32[]{:S(2)}, u32[]{:S(2)}) %collective-permute-start.40) | collective-permute-done | bytes 393248 | tf_op jit(solution)/shard_map/ppermute | solution.py:21
  326.3 2.2 collective-permute-start.43
  328.6 2.2 collective-permute-done.41.refs_1_
  330.9 3.8 %collective-permute-done.42.refs_1_ = bf16[2,48,1024]{2,1,0:T(8,128)(2,1)S(1)} collective-permute-done((bf16[2,48,1024]{2,1,0:T(8,128)(2,1)S(1)}, bf16[2,48,1024]{2,1,0:T(8,128)(2,1)S(1)}, u32[]{:S(2)}, u32[]{:S(2)}) %collective-permute-start.42) | collective-permute-done | bytes 196640 | tf_op jit(solution)/shard_map/ppermute | solution.py:21
  334.7 8.1 %collective-permute-done.43.refs_1_ = bf16[1,48,1536]{2,1,0:T(8,128)(2,1)S(1)} collective-permute-done((bf16[1,48,1536]{2,1,0:T(8,128)(2,1)S(1)}, bf16[1,48,1536]{2,1,0:T(8,128)(2,1)S(1)}, u32[]{:S(2)}, u32[]{:S(2)}) %collective-permute-start.43) | collective-permute-done | bytes 147488 | tf_op jit(solution)/shard_map/ppermute | solution.py:21
  344.2 3.9 %collective-permute-done.44.refs_1_ = bf16[1,48,2304]{2,1,0:T(8,128)(2,1)S(1)} collective-permute-done((bf16[1,48,2304]{2,1,0:T(8,128)(2,1)S(1)}, bf16[1,48,2304]{2,1,0:T(8,128)(2,1)S(1)}, u32[]{:S(2)}, u32[]{:S(2)}) %collective-permute-start.44) | collective-permute-done | bytes 221216 | tf_op jit(solution)/shard_map/ppermute | solution.py:21
  348.2 1.6 collective-permute-done.46.refs_1_
  354.4 2.5 collective-permute-done.48
  360.0 2.1 shard_map.458
  (255 shorter events, 53.0 us)
Async XLA Ops:
  1.7 11.5 %collective-permute-start = (bf16[1,48,1152]{2,1,0:T(8,128)(2,1)S(1)}, bf16[1,48,1152]{2,1,0:T(8,128)(2,1)S(1)}, u32[]{:S(2)}, u32[]{:S(2)}) collective-permute-start(bf16[1,48,1152]{2,1,0:T(8,128)(2,1)S(1)} %dynamic-slice_bitcast_fusion.1.refs_0_), channel_id=1, source_target_pairs={{0,8},{1,9},{2,10},{3,11},{4,12},{5,13},{6,14},{7,15},{8,0},{9,1},... | collective-permute-start | bytes 331784 | tf_op jit(solution)/shard_map/ppermute | solution.py:21
  13.1 9.2 %collective-permute-start.2 = (bf16[2,48,1152]{2,1,0:T(8,128)(2,1)S(1)}, bf16[2,48,1152]{2,1,0:T(8,128)(2,1)S(1)}, u32[]{:S(2)}, u32[]{:S(2)}) collective-permute-start(bf16[2,48,1152]{2,1,0:T(8,128)(2,1)S(1)} %shard_map.419.refs_0_), channel_id=1, source_target_pairs={{0,4},{1,5},{2,6},{3,7},{4,0},{5,1},{6,2},{7,3},{8,12},{9,13},{10,... | collective-permute-start | bytes 663560 | tf_op jit(solution)/shard_map/ppermute | solution.py:21
  14.8 6.6 %collective-permute-start.1 = (bf16[1,48,1024]{2,1,0:T(8,128)(2,1)}, bf16[1,48,1024]{2,1,0:T(8,128)(2,1)S(1)}, u32[]{:S(2)}, u32[]{:S(2)}) collective-permute-start(bf16[1,48,1024]{2,1,0:T(8,128)(2,1)} %bitcast.55), channel_id=1, source_target_pairs={{0,8},{1,9},{2,10},{3,11},{4,12},{5,13},{6,14},{7,15},{8,0},{9,1},... | collective-permute-start | bytes 294920 | tf_op jit(solution)/shard_map/ppermute | solution.py:21
  22.4 16.2 %collective-permute-start.6 = (bf16[4,48,1152]{2,1,0:T(8,128)(2,1)S(1)}, bf16[4,48,1152]{2,1,0:T(8,128)(2,1)S(1)}, u32[]{:S(2)}, u32[]{:S(2)}) collective-permute-start(bf16[4,48,1152]{2,1,0:T(8,128)(2,1)S(1)} %shard_map.421.refs_0_), channel_id=1, source_target_pairs={{0,2},{1,3},{2,0},{3,1},{4,6},{5,7},{6,4},{7,5},{8,10},{9,11},{10,... | collective-permute-start | bytes 1327112 | tf_op jit(solution)/shard_map/ppermute | solution.py:21
  23.9 14.6 %collective-permute-start.5 = (bf16[2,48,1024]{2,1,0:T(8,128)(2,1)S(1)}, bf16[2,48,1024]{2,1,0:T(8,128)(2,1)S(1)}, u32[]{:S(2)}, u32[]{:S(2)}) collective-permute-start(bf16[2,48,1024]{2,1,0:T(8,128)(2,1)S(1)} %shard_map.420.refs_0_), channel_id=1, source_target_pairs={{0,4},{1,5},{2,6},{3,7},{4,0},{5,1},{6,2},{7,3},{8,12},{9,13},{10,... | collective-permute-start | bytes 589832 | tf_op jit(solution)/shard_map/ppermute | solution.py:21
  25.7 12.8 %collective-permute-start.4 = (bf16[1,48,1536]{2,1,0:T(8,128)(2,1)S(1)}, bf16[1,48,1536]{2,1,0:T(8,128)(2,1)S(1)}, u32[]{:S(2)}, u32[]{:S(2)}) collective-permute-start(bf16[1,48,1536]{2,1,0:T(8,128)(2,1)S(1)} %dynamic-slice_bitcast_fusion.refs_0_), channel_id=1, source_target_pairs={{0,8},{1,9},{2,10},{3,11},{4,12},{5,13},{6,14},{7,15},{8,0},{9,1},... | collective-permute-start | bytes 442376 | tf_op jit(solution)/shard_map/ppermute | solution.py:21
  27.3 11.2 %collective-permute-start.3 = (bf16[1,48,1024]{2,1,0:T(8,128)(2,1)S(1)}, bf16[1,48,1024]{2,1,0:T(8,128)(2,1)S(1)}, u32[]{:S(2)}, u32[]{:S(2)}) collective-permute-start(bf16[1,48,1024]{2,1,0:T(8,128)(2,1)S(1)} %bitcast.53), channel_id=1, source_target_pairs={{0,8},{1,9},{2,10},{3,11},{4,12},{5,13},{6,14},{7,15},{8,0},{9,1},... | collective-permute-start | bytes 294920 | tf_op jit(solution)/shard_map/ppermute | solution.py:21
  38.7 30.8 %collective-permute-start.11 = (bf16[8,48,1152]{2,1,0:T(8,128)(2,1)S(1)}, bf16[8,48,1152]{2,1,0:T(8,128)(2,1)}, u32[]{:S(2)}, u32[]{:S(2)}) collective-permute-start(bf16[8,48,1152]{2,1,0:T(8,128)(2,1)S(1)} %shard_map.425.refs_8_.refs_11_), channel_id=1, source_target_pairs={{0,16},{16,0},{1,17},{17,1},{2,18},{18,2},{3,19},{19,3},{4,20},{20... | collective-permute-start | bytes 2654216 | tf_op jit(solution)/shard_map/ppermute | solution.py:21
  40.3 11.4 %collective-permute-start.8 = (bf16[2,48,1536]{2,1,0:T(8,128)(2,1)S(1)}, bf16[2,48,1536]{2,1,0:T(8,128)(2,1)S(1)}, u32[]{:S(2)}, u32[]{:S(2)}) collective-permute-start(bf16[2,48,1536]{2,1,0:T(8,128)(2,1)S(1)} %shard_map.423.refs_0_), channel_id=1, source_target_pairs={{0,4},{1,5},{2,6},{3,7},{4,0},{5,1},{6,2},{7,3},{8,12},{9,13},{10,... | collective-permute-start | bytes 884744 | tf_op jit(solution)/shard_map/ppermute | solution.py:21
  40.3 11.4 %collective-permute-start.7 = (bf16[2,48,1024]{2,1,0:T(8,128)(2,1)S(1)}, bf16[2,48,1024]{2,1,0:T(8,128)(2,1)S(1)}, u32[]{:S(2)}, u32[]{:S(2)}) collective-permute-start(bf16[2,48,1024]{2,1,0:T(8,128)(2,1)S(1)} %shard_map.422.refs_0_), channel_id=1, source_target_pairs={{0,4},{1,5},{2,6},{3,7},{4,0},{5,1},{6,2},{7,3},{8,12},{9,13},{10,... | collective-permute-start | bytes 589832 | tf_op jit(solution)/shard_map/ppermute | solution.py:21
  42.4 18.4 %collective-permute-start.9 = (bf16[4,48,1024]{2,1,0:T(8,128)(2,1)S(1)}, bf16[4,48,1024]{2,1,0:T(8,128)(2,1)S(1)}, u32[]{:S(2)}, u32[]{:S(2)}) collective-permute-start(bf16[4,48,1024]{2,1,0:T(8,128)(2,1)S(1)} %shard_map.424.refs_0_), channel_id=1, source_target_pairs={{0,2},{1,3},{2,0},{3,1},{4,6},{5,7},{6,4},{7,5},{8,10},{9,11},{10,... | collective-permute-start | bytes 1179656 | tf_op jit(solution)/shard_map/ppermute | solution.py:21
  52.5 16.9 %collective-permute-start.10 = (bf16[4,48,1024]{2,1,0:T(8,128)(2,1)S(1)}, bf16[4,48,1024]{2,1,0:T(8,128)(2,1)S(1)}, u32[]{:S(2)}, u32[]{:S(2)}) collective-permute-start(bf16[4,48,1024]{2,1,0:T(8,128)(2,1)S(1)} %shard_map.426.refs_0_), channel_id=1, source_target_pairs={{0,2},{1,3},{2,0},{3,1},{4,6},{5,7},{6,4},{7,5},{8,10},{9,11},{10,... | collective-permute-start | bytes 1179656 | tf_op jit(solution)/shard_map/ppermute | solution.py:21
  53.1 16.4 %collective-permute-start.12 = (bf16[1,240,768]{2,1,0:T(8,128)(2,1)S(1)}, bf16[1,240,768]{2,1,0:T(8,128)(2,1)S(1)}, u32[]{:S(2)}, u32[]{:S(2)}) collective-permute-start(bf16[1,240,768]{2,1,0:T(8,128)(2,1)S(1)} %bitcast.48), channel_id=1, source_target_pairs={{0,8},{1,9},{2,10},{3,11},{4,12},{5,13},{6,14},{7,15},{8,0},{9,1},... | collective-permute-start | bytes 1105928 | tf_op jit(solution)/shard_map/ppermute | solution.py:21
  70.6 5.1 %collective-permute-start.14 = (bf16[8,48,1152]{2,1,0:T(8,128)(2,1)S(1)}, bf16[8,48,1152]{2,1,0:T(8,128)(2,1)}, u32[]{:S(2)}, u32[]{:S(2)}) collective-permute-start(bf16[8,48,1152]{2,1,0:T(8,128)(2,1)S(1)} %shard_map.425.refs_8_.refs_11_), channel_id=1, source_target_pairs={{0,1},{1,0},{2,3},{3,2},{4,5},{5,4},{6,7},{7,6},{8,9},{9,8},{10,11... | collective-permute-start | bytes 2654216 | tf_op jit(solution)/shard_map/ppermute | solution.py:21
  71.1 5.0 %collective-permute-start.15 = (bf16[8,48,1152]{2,1,0:T(8,128)(2,1)}, bf16[8,48,1152]{2,1,0:T(8,128)(2,1)}, u32[]{:S(2)}, u32[]{:S(2)}) collective-permute-start(bf16[8,48,1152]{2,1,0:T(8,128)(2,1)} %collective-permute-done.11.refs_9_.refs_12_), channel_id=1, source_target_pairs={{0,1},{1,0},{2,3},{3,2},{4,5},{5,4},{6,7},{7,6},{8,9},{9,8},{10,11... | collective-permute-start | bytes 2654216 | tf_op jit(solution)/shard_map/ppermute | solution.py:21
  71.2 5.5 %collective-permute-start.16 = (bf16[8,48,1024]{2,1,0:T(8,128)(2,1)S(1)}, bf16[8,48,1024]{2,1,0:T(8,128)(2,1)}, u32[]{:S(2)}, u32[]{:S(2)}) collective-permute-start(bf16[8,48,1024]{2,1,0:T(8,128)(2,1)S(1)} %shard_map.430.refs_6_.refs_2_), channel_id=1, source_target_pairs={{0,1},{1,0},{2,3},{3,2},{4,5},{5,4},{6,7},{7,6},{8,9},{9,8},{10,11... | collective-permute-start | bytes 2359304 | tf_op jit(solution)/shard_map/ppermute | solution.py:21
  71.6 24.4 %collective-permute-start.18 = (bf16[2,240,768]{2,1,0:T(8,128)(2,1)}, bf16[2,240,768]{2,1,0:T(8,128)(2,1)}, u32[]{:S(2)}, u32[]{:S(2)}) collective-permute-start(bf16[2,240,768]{2,1,0:T(8,128)(2,1)} %shard_map.431.refs_0_), channel_id=1, source_target_pairs={{0,4},{1,5},{2,6},{3,7},{4,0},{5,1},{6,2},{7,3},{8,12},{9,13},{10,... | collective-permute-start | bytes 2211848 | tf_op jit(solution)/shard_map/ppermute | solution.py:21
  74.2 21.8 %collective-permute-start.17 = (bf16[4,48,1536]{2,1,0:T(8,128)(2,1)}, bf16[4,48,1536]{2,1,0:T(8,128)(2,1)}, u32[]{:S(2)}, u32[]{:S(2)}) collective-permute-start(bf16[4,48,1536]{2,1,0:T(8,128)(2,1)} %shard_map.427.refs_4_), channel_id=1, source_target_pairs={{0,2},{1,3},{2,0},{3,1},{4,6},{5,7},{6,4},{7,5},{8,10},{9,11},{10,... | collective-permute-start | bytes 1769480 | tf_op jit(solution)/shard_map/ppermute | solution.py:21
  98.3 34.5 %collective-permute-start.21 = (bf16[4,240,768]{2,1,0:T(8,128)(2,1)S(1)}, bf16[4,240,768]{2,1,0:T(8,128)(2,1)}, u32[]{:S(2)}, u32[]{:S(2)}) collective-permute-start(bf16[4,240,768]{2,1,0:T(8,128)(2,1)S(1)} %shard_map.433.refs_12_), channel_id=1, source_target_pairs={{0,2},{1,3},{2,0},{3,1},{4,6},{5,7},{6,4},{7,5},{8,10},{9,11},{10,... | collective-permute-start | bytes 4423688 | tf_op jit(solution)/shard_map/ppermute | solution.py:21
  99.9 24.2 %collective-permute-start.19 = (bf16[4,48,1536]{2,1,0:T(8,128)(2,1)}, bf16[4,48,1536]{2,1,0:T(8,128)(2,1)}, u32[]{:S(2)}, u32[]{:S(2)}) collective-permute-start(bf16[4,48,1536]{2,1,0:T(8,128)(2,1)} %shard_map.427.refs_4_), channel_id=1, source_target_pairs={{0,16},{16,0},{1,17},{17,1},{2,18},{18,2},{3,19},{19,3},{4,20},{20... | collective-permute-start | bytes 1769480 | tf_op jit(solution)/shard_map/ppermute | solution.py:21
  100.4 27.5 %collective-permute-start.20 = (bf16[4,48,1536]{2,1,0:T(8,128)(2,1)}, bf16[4,48,1536]{2,1,0:T(8,128)(2,1)}, u32[]{:S(2)}, u32[]{:S(2)}) collective-permute-start(bf16[4,48,1536]{2,1,0:T(8,128)(2,1)} %collective-permute-done.17.refs_5_), channel_id=1, source_target_pairs={{0,16},{16,0},{1,17},{17,1},{2,18},{18,2},{3,19},{19,3},{4,20},{20... | collective-permute-start | bytes 1769480 | tf_op jit(solution)/shard_map/ppermute | solution.py:21
  132.8 9.6 %collective-permute-start.26 = (bf16[4,240,768]{2,1,0:T(8,128)(2,1)S(1)}, bf16[4,240,768]{2,1,0:T(8,128)(2,1)}, u32[]{:S(2)}, u32[]{:S(2)}) collective-permute-start(bf16[4,240,768]{2,1,0:T(8,128)(2,1)S(1)} %shard_map.433.refs_12_), channel_id=1, source_target_pairs={{0,1},{1,0},{2,3},{3,2},{4,5},{5,4},{6,7},{7,6},{8,9},{9,8},{10,11... | collective-permute-start | bytes 4423688 | tf_op jit(solution)/shard_map/ppermute | solution.py:21
  132.8 9.6 %collective-permute-start.27 = (bf16[4,240,768]{2,1,0:T(8,128)(2,1)}, bf16[4,240,768]{2,1,0:T(8,128)(2,1)}, u32[]{:S(2)}, u32[]{:S(2)}) collective-permute-start(bf16[4,240,768]{2,1,0:T(8,128)(2,1)} %collective-permute-done.21.refs_13_), channel_id=1, source_target_pairs={{0,1},{1,0},{2,3},{3,2},{4,5},{5,4},{6,7},{7,6},{8,9},{9,8},{10,11... | collective-permute-start | bytes 4423688 | tf_op jit(solution)/shard_map/ppermute | solution.py:21
  133.4 6.7 %collective-permute-start.22 = (bf16[4,48,1536]{2,1,0:T(8,128)(2,1)}, bf16[4,48,1536]{2,1,0:T(8,128)(2,1)S(1)}, u32[]{:S(2)}, u32[]{:S(2)}) collective-permute-start(bf16[4,48,1536]{2,1,0:T(8,128)(2,1)} %shard_map.427.refs_4_), channel_id=1, source_target_pairs={{0,1},{1,0},{2,3},{3,2},{4,5},{5,4},{6,7},{7,6},{8,9},{9,8},{10,11... | collective-permute-start | bytes 1769480 | tf_op jit(solution)/shard_map/ppermute | solution.py:21
  133.4 8.6 %collective-permute-start.23 = (bf16[4,48,1536]{2,1,0:T(8,128)(2,1)}, bf16[4,48,1536]{2,1,0:T(8,128)(2,1)}, u32[]{:S(2)}, u32[]{:S(2)}) collective-permute-start(bf16[4,48,1536]{2,1,0:T(8,128)(2,1)} %collective-permute-done.17.refs_5_), channel_id=1, source_target_pairs={{0,1},{1,0},{2,3},{3,2},{4,5},{5,4},{6,7},{7,6},{8,9},{9,8},{10,11... | collective-permute-start | bytes 1769480 | tf_op jit(solution)/shard_map/ppermute | solution.py:21
  133.9 8.1 %collective-permute-start.24 = (bf16[4,48,1536]{2,1,0:T(8,128)(2,1)}, bf16[4,48,1536]{2,1,0:T(8,128)(2,1)}, u32[]{:S(2)}, u32[]{:S(2)}) collective-permute-start(bf16[4,48,1536]{2,1,0:T(8,128)(2,1)} %collective-permute-done.19.refs_6_), channel_id=1, source_target_pairs={{0,1},{1,0},{2,3},{3,2},{4,5},{5,4},{6,7},{7,6},{8,9},{9,8},{10,11... | collective-permute-start | bytes 1769480 | tf_op jit(solution)/shard_map/ppermute | solution.py:21
  211.0 9.6 %collective-permute-start.28 = (bf16[8,240,768]{2,1,0:T(8,128)(2,1)}, bf16[8,240,768]{2,1,0:T(8,128)(2,1)S(1)}, u32[]{:S(2)}, u32[]{:S(2)}) collective-permute-start(bf16[8,240,768]{2,1,0:T(8,128)(2,1)} %get-tuple-element.555), channel_id=1, source_target_pairs={{0,1},{1,0},{2,3},{3,2},{4,5},{5,4},{6,7},{7,6},{8,9},{9,8},{10,11... | collective-permute-start | bytes 8847368 | tf_op jit(solution)/shard_map/ppermute | solution.py:21
  211.2 9.4 %collective-permute-start.29 = (bf16[2,8,48,1536]{3,2,1,0:T(8,128)(2,1)}, bf16[2,8,48,1536]{3,2,1,0:T(8,128)(2,1)S(1)}, u32[]{:S(2)}, u32[]{:S(2)}) collective-permute-start(bf16[2,8,48,1536]{3,2,1,0:T(8,128)(2,1)} %get-tuple-element.556), channel_id=1, source_target_pairs={{0,1},{1,0},{2,3},{3,2},{4,5},{5,4},{6,7},{7,6},{8,9},{9,8},{10,11... | collective-permute-start | bytes 7077896 | tf_op jit(solution)/shard_map/ppermute | solution.py:21
  222.9 34.4 %collective-permute-start.30 = (bf16[4,240,768]{2,1,0:T(8,128)(2,1)S(1)}, bf16[4,240,768]{2,1,0:T(8,128)(2,1)S(1)}, u32[]{:S(2)}, u32[]{:S(2)}) collective-permute-start(bf16[4,240,768]{2,1,0:T(8,128)(2,1)S(1)} %get-tuple-element.565), channel_id=1, source_target_pairs={{0,2},{1,3},{2,0},{3,1},{4,6},{5,7},{6,4},{7,5},{8,10},{9,11},{10,... | collective-permute-start | bytes 4423688 | tf_op jit(solution)/shard_map/ppermute | solution.py:21
  224.5 27.7 %collective-permute-start.31 = (bf16[8,48,1536]{2,1,0:T(8,128)(2,1)S(1)}, bf16[8,48,1536]{2,1,0:T(8,128)(2,1)S(1)}, u32[]{:S(2)}, u32[]{:S(2)}) collective-permute-start(bf16[8,48,1536]{2,1,0:T(8,128)(2,1)S(1)} %get-tuple-element.566), channel_id=1, source_target_pairs={{0,16},{16,0},{1,17},{17,1},{2,18},{18,2},{3,19},{19,3},{4,20},{20... | collective-permute-start | bytes 3538952 | tf_op jit(solution)/shard_map/ppermute | solution.py:21
  260.3 27.1 %collective-permute-start.32 = (bf16[2,240,768]{2,1,0:T(8,128)(2,1)}, bf16[2,240,768]{2,1,0:T(8,128)(2,1)}, u32[]{:S(2)}, u32[]{:S(2)}) collective-permute-start(bf16[2,240,768]{2,1,0:T(8,128)(2,1)} %get-tuple-element.585), channel_id=1, source_target_pairs={{0,4},{1,5},{2,6},{3,7},{4,0},{5,1},{6,2},{7,3},{8,12},{9,13},{10,... | collective-permute-start | bytes 2211848 | tf_op jit(solution)/shard_map/ppermute | solution.py:21
  260.3 27.1 %collective-permute-start.33 = (bf16[4,48,1536]{2,1,0:T(8,128)(2,1)}, bf16[4,48,1536]{2,1,0:T(8,128)(2,1)}, u32[]{:S(2)}, u32[]{:S(2)}) collective-permute-start(bf16[4,48,1536]{2,1,0:T(8,128)(2,1)} %get-tuple-element.586), channel_id=1, source_target_pairs={{0,2},{1,3},{2,0},{3,1},{4,6},{5,7},{6,4},{7,5},{8,10},{9,11},{10,... | collective-permute-start | bytes 1769480 | tf_op jit(solution)/shard_map/ppermute | solution.py:21
  287.4 5.7 %collective-permute-start.34 = (bf16[8,48,2304]{2,1,0:T(8,128)(2,1)}, bf16[8,48,2304]{2,1,0:T(8,128)(2,1)S(1)}, u32[]{:S(2)}, u32[]{:S(2)}) collective-permute-start(bf16[8,48,2304]{2,1,0:T(8,128)(2,1)} %get-tuple-element.598), channel_id=1, source_target_pairs={{0,1},{1,0},{2,3},{3,2},{4,5},{5,4},{6,7},{7,6},{8,9},{9,8},{10,11... | collective-permute-start | bytes 5308424 | tf_op jit(solution)/shard_map/ppermute | solution.py:21
  287.5 6.6 %collective-permute-start.35 = (bf16[2,8,48,1024]{3,2,1,0:T(8,128)(2,1)S(1)}, bf16[2,8,48,1024]{3,2,1,0:T(8,128)(2,1)S(1)}, u32[]{:S(2)}, u32[]{:S(2)}) collective-permute-start(bf16[2,8,48,1024]{3,2,1,0:T(8,128)(2,1)S(1)} %get-tuple-element.604), channel_id=1, source_target_pairs={{0,1},{1,0},{2,3},{3,2},{4,5},{5,4},{6,7},{7,6},{8,9},{9,8},{10,11... | collective-permute-start | bytes 4718600 | tf_op jit(solution)/shard_map/ppermute | solution.py:21
  293.6 22.4 %collective-permute-start.39 = (bf16[4,48,2304]{2,1,0:T(8,128)(2,1)S(1)}, bf16[4,48,2304]{2,1,0:T(8,128)(2,1)S(1)}, u32[]{:S(2)}, u32[]{:S(2)}) collective-permute-start(bf16[4,48,2304]{2,1,0:T(8,128)(2,1)S(1)} %get-tuple-element.636), channel_id=1, source_target_pairs={{0,2},{1,3},{2,0},{3,1},{4,6},{5,7},{6,4},{7,5},{8,10},{9,11},{10,... | collective-permute-start | bytes 2654216 | tf_op jit(solution)/shard_map/ppermute | solution.py:21
  294.5 20.3 %collective-permute-start.38 = (bf16[8,48,1024]{2,1,0:T(8,128)(2,1)S(1)}, bf16[8,48,1024]{2,1,0:T(8,128)(2,1)S(1)}, u32[]{:S(2)}, u32[]{:S(2)}) collective-permute-start(bf16[8,48,1024]{2,1,0:T(8,128)(2,1)S(1)} %get-tuple-element.626), channel_id=1, source_target_pairs={{0,16},{16,0},{1,17},{17,1},{2,18},{18,2},{3,19},{19,3},{4,20},{20... | collective-permute-start | bytes 2359304 | tf_op jit(solution)/shard_map/ppermute | solution.py:21
  295.8 18.9 %collective-permute-start.36 = (bf16[1,240,768]{2,1,0:T(8,128)(2,1)S(1)}, bf16[1,240,768]{2,1,0:T(8,128)(2,1)S(1)}, u32[]{:S(2)}, u32[]{:S(2)}) collective-permute-start(bf16[1,240,768]{2,1,0:T(8,128)(2,1)S(1)} %get-tuple-element.613), channel_id=1, source_target_pairs={{0,8},{1,9},{2,10},{3,11},{4,12},{5,13},{6,14},{7,15},{8,0},{9,1},... | collective-permute-start | bytes 1105928 | tf_op jit(solution)/shard_map/ppermute | solution.py:21
  296.6 14.0 %collective-permute-start.37 = (bf16[2,48,1536]{2,1,0:T(8,128)(2,1)S(1)}, bf16[2,48,1536]{2,1,0:T(8,128)(2,1)S(1)}, u32[]{:S(2)}, u32[]{:S(2)}) collective-permute-start(bf16[2,48,1536]{2,1,0:T(8,128)(2,1)S(1)} %get-tuple-element.614), channel_id=1, source_target_pairs={{0,4},{1,5},{2,6},{3,7},{4,0},{5,1},{6,2},{7,3},{8,12},{9,13},{10,... | collective-permute-start | bytes 884744 | tf_op jit(solution)/shard_map/ppermute | solution.py:21
  315.0 9.8 %collective-permute-start.40 = (bf16[4,48,1024]{2,1,0:T(8,128)(2,1)S(1)}, bf16[4,48,1024]{2,1,0:T(8,128)(2,1)S(1)}, u32[]{:S(2)}, u32[]{:S(2)}) collective-permute-start(bf16[4,48,1024]{2,1,0:T(8,128)(2,1)S(1)} %get-tuple-element.646), channel_id=1, source_target_pairs={{0,2},{1,3},{2,0},{3,1},{4,6},{5,7},{6,4},{7,5},{8,10},{9,11},{10,... | collective-permute-start | bytes 1179656 | tf_op jit(solution)/shard_map/ppermute | solution.py:21
  316.2 14.5 %collective-permute-start.41 = (bf16[2,48,2304]{2,1,0:T(8,128)(2,1)S(1)}, bf16[2,48,2304]{2,1,0:T(8,128)(2,1)S(1)}, u32[]{:S(2)}, u32[]{:S(2)}) collective-permute-start(bf16[2,48,2304]{2,1,0:T(8,128)(2,1)S(1)} %get-tuple-element.656), channel_id=1, source_target_pairs={{0,4},{1,5},{2,6},{3,7},{4,0},{5,1},{6,2},{7,3},{8,12},{9,13},{10,... | collective-permute-start | bytes 1327112 | tf_op jit(solution)/shard_map/ppermute | solution.py:21
  318.0 30.2 %collective-permute-start.45 = (bf16[240,768]{1,0:T(8,128)(2,1)S(1)}, bf16[240,768]{1,0:T(8,128)(2,1)S(1)}, u32[]{:S(2)}, u32[]{:S(2)}) collective-permute-start(bf16[240,768]{1,0:T(8,128)(2,1)S(1)} %bitcast.47), channel_id=1, source_target_pairs={{0,16},{16,0},{1,17},{17,1},{2,18},{18,2},{3,19},{19,3},{4,20},{20... | collective-permute-start | bytes 1105928 | tf_op jit(solution)/shard_map/ppermute | solution.py:21
  324.9 9.8 %collective-permute-start.42 = (bf16[2,48,1024]{2,1,0:T(8,128)(2,1)S(1)}, bf16[2,48,1024]{2,1,0:T(8,128)(2,1)S(1)}, u32[]{:S(2)}, u32[]{:S(2)}) collective-permute-start(bf16[2,48,1024]{2,1,0:T(8,128)(2,1)S(1)} %get-tuple-element.666), channel_id=1, source_target_pairs={{0,4},{1,5},{2,6},{3,7},{4,0},{5,1},{6,2},{7,3},{8,12},{9,13},{10,... | collective-permute-start | bytes 589832 | tf_op jit(solution)/shard_map/ppermute | solution.py:21
  326.3 16.5 %collective-permute-start.43 = (bf16[1,48,1536]{2,1,0:T(8,128)(2,1)S(1)}, bf16[1,48,1536]{2,1,0:T(8,128)(2,1)S(1)}, u32[]{:S(2)}, u32[]{:S(2)}) collective-permute-start(bf16[1,48,1536]{2,1,0:T(8,128)(2,1)S(1)} %get-tuple-element.676), channel_id=1, source_target_pairs={{0,8},{1,9},{2,10},{3,11},{4,12},{5,13},{6,14},{7,15},{8,0},{9,1},... | collective-permute-start | bytes 442376 | tf_op jit(solution)/shard_map/ppermute | solution.py:21
  330.8 17.3 %collective-permute-start.44 = (bf16[1,48,2304]{2,1,0:T(8,128)(2,1)S(1)}, bf16[1,48,2304]{2,1,0:T(8,128)(2,1)S(1)}, u32[]{:S(2)}, u32[]{:S(2)}) collective-permute-start(bf16[1,48,2304]{2,1,0:T(8,128)(2,1)S(1)} %get-tuple-element.685), channel_id=1, source_target_pairs={{0,8},{1,9},{2,10},{3,11},{4,12},{5,13},{6,14},{7,15},{8,0},{9,1},... | collective-permute-start | bytes 663560 | tf_op jit(solution)/shard_map/ppermute | solution.py:21
  342.9 6.9 %collective-permute-start.47 = (bf16[48,1536]{1,0:T(8,128)(2,1)S(1)}, bf16[48,1536]{1,0:T(8,128)(2,1)S(1)}, u32[]{:S(2)}, u32[]{:S(2)}) collective-permute-start(bf16[48,1536]{1,0:T(8,128)(2,1)S(1)} %bitcast.51), channel_id=1, source_target_pairs={{0,16},{16,0},{1,17},{17,1},{2,18},{18,2},{3,19},{19,3},{4,20},{20... | collective-permute-start | bytes 442376 | tf_op jit(solution)/shard_map/ppermute | solution.py:21
  344.2 5.5 %collective-permute-start.46 = (bf16[1,48,1024]{2,1,0:T(8,128)(2,1)S(1)}, bf16[1,48,1024]{2,1,0:T(8,128)(2,1)S(1)}, u32[]{:S(2)}, u32[]{:S(2)}) collective-permute-start(bf16[1,48,1024]{2,1,0:T(8,128)(2,1)S(1)} %get-tuple-element.701), channel_id=1, source_target_pairs={{0,8},{1,9},{2,10},{3,11},{4,12},{5,13},{6,14},{7,15},{8,0},{9,1},... | collective-permute-start | bytes 294920 | tf_op jit(solution)/shard_map/ppermute | solution.py:21
  349.8 7.1 %collective-permute-start.49 = (bf16[48,1024]{1,0:T(8,128)(2,1)S(1)}, bf16[48,1024]{1,0:T(8,128)(2,1)S(1)}, u32[]{:S(2)}, u32[]{:S(2)}) collective-permute-start(bf16[48,1024]{1,0:T(8,128)(2,1)S(1)} %bitcast.52), channel_id=1, source_target_pairs={{0,16},{16,0},{1,17},{17,1},{2,18},{18,2},{3,19},{19,3},{4,20},{20... | collective-permute-start | bytes 294920 | tf_op jit(solution)/shard_map/ppermute | solution.py:21
  350.6 6.3 %collective-permute-start.48 = (bf16[48,2304]{1,0:T(8,128)(2,1)S(1)}, bf16[48,2304]{1,0:T(8,128)(2,1)S(1)}, u32[]{:S(2)}, u32[]{:S(2)}) collective-permute-start(bf16[48,2304]{1,0:T(8,128)(2,1)S(1)} %bitcast.50), channel_id=1, source_target_pairs={{0,16},{16,0},{1,17},{17,1},{2,18},{18,2},{3,19},{19,3},{4,20},{20... | collective-permute-start | bytes 663560 | tf_op jit(solution)/shard_map/ppermute | solution.py:21
  (64 other events, 765.7 us)

commit v2 on v1

--- a/solution.py
+++ b/solution.py
@@ -41,14 +41,26 @@
         if not self.steps:
             self.ready = []
             return
-        last = self.steps[0] in ("rep", "core")
-        if len(self.held) > 1 and len(self.held[0]) == 2 and (self.joined or not last):
-            offsets = [o for _, offsets in self.held for o in offsets]
-            self.held = [(join([blocks for blocks, _ in self.held]), offsets)]
+        if self.steps[0] == "core":
+            if self.joined:
+                size = len(self.held) // (2 if self.split else 1)
+                self.held = [
+                    self.join(self.held[i : i + size]) for i in range(0, len(self.held), size)
+                ]
+        elif self.steps[0] != "rep" and len(self.held) > 1:
+            self.held = [self.join(self.held)]
         self.ready = [blocks for blocks, *_ in self.held]
+        if self.steps[0] == "rep":
+            self.ready = self.ready[1:2]
+
+    def join(self, held):
+        offsets = [o for h in held for o in h[1]]
+        return (join([h[0] for h in held]) if len(held) > 1 else held[0][0], offsets, *held[0][2:])
 
     def renew(self, ready):
-        if ready:
+        if self.steps and self.steps[0] == "rep":
+            self.held = [self.held[0], (ready[0], *self.held[1][1:]), *self.held[2:]]
+        elif ready:
             self.held = [(blocks, *h[1:]) for blocks, h in zip(ready, self.held)]
         self.ready = ready
 
@@ -59,12 +71,18 @@
             self.sent = [swap(blocks, axis, size, 1) for blocks in self.ready]
         else:
             self.sent = [swap(self.ready[0], "fsdp", self.count, offset) for offset in self.step]
+            if self.steps[0] == "rep":
+                self.sent.append(swap(self.ready[0], "rep", 2, 1))
         return self
 
     def take(self, arrived):
         if self.step == "rep":
-            self.held = [(*h, 0) for h in self.held] + [
-                (blocks, h[1], 1) for blocks, h in zip(arrived, self.held)
+            own, given, early = self.held
+            self.held = [
+                (*own, 0),
+                (*given, 0),
+                (early[0], own[1], 1),
+                (arrived[0], given[1], 1),
             ]
         elif self.step == "core":
             held = [h if len(h) == 3 else (*h, None) for h in self.held]
@@ -77,6 +95,8 @@
                 (blocks, [o ^ offset for o in offsets])
                 for blocks, offset in zip(arrived, self.step)
             ]
+            if self.steps[0] == "rep":
+                self.held.append((arrived[-1], offsets))
 
 
 def finish(anchor, *chains):
@@ -605,7 +625,7 @@
         in_specs=[block(0), block(1), block(2)]
         + [block(0), pl.BlockSpec((rows, 128), lambda j: (0, 0))][: len(done)],
         out_specs=[pl.BlockSpec((rows, 128), lambda j: (0, j)), pl.BlockSpec((rows, 128), lambda j: (0, 0))],
-        compiler_params=pltpu.CompilerParams(vmem_limit_bytes=24 * 2**20),
+        compiler_params=pltpu.CompilerParams(vmem_limit_bytes=60 * 2**20),
         cost_estimate=BRIEF,
     )(qkv, qkv, qkv, *done)
 
@@ -830,7 +850,7 @@
             pltpu.SemaphoreType.DMA((copies_of(embed_parts.pieces),)),
             pltpu.SemaphoreType.DMA((copies_of(qkv_parts.pieces),)),
         ],
-        compiler_params=pltpu.CompilerParams(vmem_limit_bytes=40 * 2**20),
+        compiler_params=pltpu.CompilerParams(vmem_limit_bytes=58 * 2**20),
         cost_estimate=BRIEF,
     )(embed_parts.where, *patches, maps, *parts)
 
@@ -894,6 +914,7 @@
     slot = lax.rem(step, 2)
     tile = w_up.shape[2]
     up_rows, down_rows = up_keep.shape[2], w_down.shape[1] // 4
+    out_columns = up_parts[0].shape[2] - 2 * tile
     count = 16
 
     def at(index, size):
@@ -918,7 +939,7 @@
             place_ = s // 2 + 2 * lax.rem(s, 2)
             copies.append(
                 pltpu.make_async_copy(
-                    down_parts[2 * (j % 2) + j // 2].at[place_, pl.ds(0, down_rows), :],
+                    down_parts[2 * (j % 2) + j // 2].at[place_],
                     w_down.at[lax.rem(s, 2), at(lax.bitwise_xor(lax.rem(me, 4), j), down_rows), :],
                     down_in.at[lax.rem(s, 2), j],
                 )
@@ -941,12 +962,15 @@
     def load_out():
         return [
             pltpu.make_async_copy(
-                down_parts[2 * (d % 2) + ORDER.index(d - d % 2) // 4].at[
-                    ORDER.index(d - d % 2) % 4, pl.ds(down_rows, up_rows), :
+                up_parts[4 * (d % 2) + 2 * half + ORDER.index(d - d % 2) // 4].at[
+                    ORDER.index(d - d % 2) % 4, :, pl.ds(2 * tile, out_columns)
                 ],
-                w_out.at[at(lax.bitwise_xor(me, d), up_rows), :],
-                out_in.at[d],
+                w_out.at[
+                    at(lax.bitwise_xor(me, d), up_rows), at(lax.bitwise_xor(other, half), out_columns)
+                ],
+                out_in.at[half, d],
             )
+            for half in range(2)
             for d in range(count)
         ]
 
@@ -1076,7 +1100,7 @@
 
 def feed_all(where, mixed, embedded, lines, b_up, up_parts, down_parts, cotangents, starts, chunk=624):
     rows, width = mixed.shape
-    tile = up_parts[0].shape[2] // 2
+    tile = (up_parts[0].shape[2] - width // 2) // 2
     hidden = 4 * tile
     up_rows = up_parts[0].shape[1]
     down_rows = down_parts[0].shape[1]
@@ -1112,7 +1136,7 @@
                 pltpu.VMEM((width, width), BF16),
                 pltpu.SemaphoreType.DMA((2, 16)),
                 pltpu.SemaphoreType.DMA((2, 4)),
-                pltpu.SemaphoreType.DMA((16,)),
+                pltpu.SemaphoreType.DMA((2, 16)),
                 pltpu.SemaphoreType.DMA((2, 16)),
                 pltpu.SemaphoreType.DMA((2, 4)),
                 pltpu.SemaphoreType.DMA((16,)),
@@ -1122,7 +1146,7 @@
         ),
         out_shape=[like(c.shape, BF16) for c in cotangents]
         + [like((2, 8, up_rows, hidden // 2), BF16)] * 2
-        + [like((8, down_rows, width), BF16)] * 2
+        + [like((8, down_rows + up_rows, width), BF16)] * 2
         + [
             like((1, hidden), F32),
             like((rows, width), BF16),
@@ -1342,22 +1366,36 @@
 
     base_turned = base_kernel.swapaxes(1, 2)
     down_rows = (down_weight.shape[0], out_weight.shape[0])
-    down_block = jnp.concatenate([down_weight, out_weight])
+    up_half, out_half = up_weight.shape[1] // 2, width // 2
+    up_block = jnp.concatenate(
+        [
+            up_weight[:, :up_half],
+            out_weight[:, :out_half],
+            up_weight[:, up_half:],
+            out_weight[:, out_half:],
+        ],
+        axis=1,
+    )
     qkv_shards = Gather(qkv_weight, where, count, outward, split=True).send()
-    up_shards = Gather(up_weight, where, count, outward, split=True, joined=False).send()
+    up_shards = Gather(up_block, where, count, outward, split=True, joined=False).send()
     shards = resize_all(resizes, base_turned, posemb.T, vectors, bounds, columns)
     embed_low = Gather(shards[0], where, count, outward).send()
     embed_high = Gather(shards[1], where, count, outward).send()
-    held = go_on((pixels, maps, *shards), qkv_shards, embed_low, qkv_shards, embed_high, up_shards)
-    held = go_on(held, embed_low, qkv_shards)
-    held, down_block = after(held, down_block)
-    down_shards = Gather(down_block, where, count, outward, joined=False).send()
-    held = finish(held, embed_high, up_shards)
-    embed_high.send()
+    held = go_on((pixels, maps, *shards), qkv_shards)
+    held = together(held, embed_low, embed_high)
+    held = go_on(held, qkv_shards)
+    held = together(held, embed_low, embed_high)
+    held, down_weight = after(held, down_weight)
+    down_shards = Gather(down_weight, where, count, outward, joined=False).send()
+    held = together(held, qkv_shards, up_shards)
     pixels, maps, *_ = held
     patches = patch_all(pixels)
-    patches, maps = together((patches, maps), embed_low, embed_high, qkv_shards, down_shards)
-    patches, maps = complete((patches, maps), embed_low, qkv_shards, embed_high)
+    patches, maps = finish(
+        (patches, maps), embed_low, embed_high, qkv_shards, down_shards, up_shards
+    )
+    for chain in (embed_low, embed_high, qkv_shards, down_shards):
+        chain.send()
+    patches, maps = complete((patches, maps), embed_low, embed_high, qkv_shards)
     up_shards.send()
     w_qkv = Parts([qkv_shards], where, count)
     w_embed = Parts([embed_low, embed_high], where, count)
@@ -1369,7 +1407,7 @@
     mixed = together(mixed, up_shards, down_shards)
     mixed = complete(mixed, up_shards, down_shards)
     w_up = Parts([up_shards], where, count)
-    w_down = Parts([down_shards], where, count, down_rows)
+    w_down = Parts([down_shards], where, count)
     b_up = columns_small[:, spots + 9 : used].astype(F32)
     b_up = b_up.reshape(count, share, up_per).swapaxes(1, 2).reshape(1, -1)
     (

time: 364 us -> 357 us (0.981)
  waiting for transfers between devices: 96.5 us -> 80.1 us
  starting transfers between devices: 43.8 us -> 48.1 us
    ppermute x50 -> x51, waiting for transfers between devices: 96.5 us -> 80.1 us  [swap(): return lax.ppermute(value, axis, [(i, i ^ bit) for i in range(size)])]
    unnamed x125 -> x127, local copies, waits for them, and re-layouts: 20.4 us -> 14.8 us
    ppermute x50 -> x51, starting transfers between devices: 43.8 us -> 48.1 us  [swap(): return lax.ppermute(value, axis, [(i, i ^ bit) for i in range(size)])]
  transfers between devices with their start and end apart: 50 -> 51, of which waited for: 23 -> 24; matrix products, arithmetic and copies ran while one was open for 2% -> 4% of each run, Pallas kernels for 31% -> 32%
where the time goes in v2:
time: 357 us; the launch traced here: 353 us
  Pallas kernels  191 us (54%)
  waiting for transfers between devices  80.1 us (22%)
  starting transfers between devices  48.1 us (13%)
  local copies, waits for them, and re-layouts  27.5 us (8%)
  other arithmetic  4.2 us (1%)
    ppermute x51, waiting for transfers between devices, swap(): return lax.ppermute(value, axis, [(i, i ^ bit) for i in range(size)])  80.1 us
    pallas_call x1, Pallas kernels, feed_all(): pl.pallas_call(functools.partial(feed_kernel, starts, chunk), grid_spec=p...  68.9 us
    ppermute x51, starting transfers between devices, swap(): return lax.ppermute(value, axis, [(i, i ^ bit) for i in range(size)])  48.1 us
    pallas_call x2, Pallas kernels, attend_backward(): pl.pallas_call(functools.partial(attend_back_kernel, starts, chunk), grid...  30.4 us
    pallas_call x1, Pallas kernels, leave_all(): pl.pallas_call(functools.partial(leave_kernel, qkv_parts.pieces, starts,...  24.1 us
    pallas_call x1, Pallas kernels, attend_forward(): pl.pallas_call(functools.partial(attend_kernel, starts, chunk), grid=(pai...  19.1 us
    pallas_call x1, Pallas kernels, enter_all(): pl.pallas_call(functools.partial(enter_kernel, embed_parts.pieces, qkv_pa...  17.1 us
    unnamed x127, local copies, waits for them, and re-layouts  14.8 us
  transfers between devices with their start and end apart: 51, of which 24 were waited for; matrix products, arithmetic and copies ran while one was open for 4% of the time, Pallas kernels for 32%

profile of v2, /device:TPU:0, one launch (start us, length us, event | category | flops | bytes accessed | tf_op | source)
XLA Modules:
  0.0 353.1 jit_solution(16109792668422585793)
XLA Ops:
  1.6 4.1 %collective-permute-start = (bf16[1,48,1152]{2,1,0:T(8,128)(2,1)S(1)}, bf16[1,48,1152]{2,1,0:T(8,128)(2,1)S(1)}, u32[]{:S(2)}, u32[]{:S(2)}) collective-permute-start(bf16[1,48,1152]{2,1,0:T(8,128)(2,1)S(1)} %dynamic-slice_bitcast_fusion.refs_0_), channel_id=1, source_target_pairs={{0,8},{1,9},{2,10},{3,11},{4,12},{5,13},{6,14},{7,15},{8,0},{9,1},... | collective-permute-start | bytes 331784 | tf_op jit(solution)/shard_map/ppermute | solution.py:21
  8.2 4.6 %shard_map.418 = (bf16[48,1024]{1,0:T(8,128)(2,1)}, bf16[48,1024]{1,0:T(8,128)(2,1)}) custom-call(f32[100,1024]{1,0:T(8,128)} %refs_0_.4, f32[144,1024]{1,0:T(8,128)} %refs_1_.4, f32[256,1024]{1,0:T(8,128)} %refs_2_.4, bf16[3,48,1024]{2,1,0:T(8,128)(2,1)} %bitcast.59, bf16[48,49]{1,0:T(8,128)(2,1)} %bitcast.61, bf16[1,48]{1,0:T(2,128)(2,1)} %bitcast.62, ...), custom_call_target="tpu_custom_call" | custom-call | flops 1 | bytes 1 | tf_op jit(solution)/shard_map/pallas_call | solution.py:770
  12.9 2.9 collective-permute-start.1
  17.3 1.6 collective-permute-start.3
  19.0 4.6 %collective-permute-done.2.refs_1_ = bf16[1,48,1024]{2,1,0:T(8,128)(2,1)S(1)} collective-permute-done((bf16[1,48,1024]{2,1,0:T(8,128)(2,1)}, bf16[1,48,1024]{2,1,0:T(8,128)(2,1)S(1)}, u32[]{:S(2)}, u32[]{:S(2)}) %collective-permute-start.2) | collective-permute-done | bytes 98336 | tf_op jit(solution)/shard_map/ppermute | solution.py:21
  24.8 2.1 collective-permute-done.3.refs_1_
  26.9 1.6 collective-permute-start.7
  28.5 1.5 collective-permute-start.6
  30.0 2.0 collective-permute-start.5
  33.1 7.7 %collective-permute-done.4.refs_1_ = bf16[2,48,1024]{2,1,0:T(8,128)(2,1)S(1)} collective-permute-done((bf16[2,48,1024]{2,1,0:T(8,128)(2,1)S(1)}, bf16[2,48,1024]{2,1,0:T(8,128)(2,1)S(1)}, u32[]{:S(2)}, u32[]{:S(2)}) %collective-permute-start.4) | collective-permute-done | bytes 196640 | tf_op jit(solution)/shard_map/ppermute | solution.py:21
  40.8 2.1 collective-permute-done.5.refs_1_
  44.2 1.5 collective-permute-start.10
  46.7 1.9 collective-permute-start.12
  48.7 6.8 %shard_map.426 = (bf16[256,512]{1,0:T(8,128)(2,1)S(1)}, bf16[400,640]{1,0:T(8,128)(2,1)S(1)}, bf16[576,768]{1,0:T(8,128)(2,1)S(1)}) custom-call(bf16[1,3,160,160]{3,2,1,0:T(8,128)(2,1)S(1)} %copy-done.46, bf16[1,3,240,240]{3,2,1,0:T(8,128)(2,1)S(1)} %copy-done.43, bf16[1,3,384,384]{3,2,1,0:T(8,128)(2,1)S(1)} %copy-done.34), custom_call_target="tpu_custom_call" | custom-call | flops 1 | bytes 1 | tf_op jit(solution)/shard_map/pallas_call | solution.py:486
  55.5 1.8 collective-permute-done.12.refs_1_
  57.4 2.2 collective-permute-done.10.refs_1_
  63.6 1.5 collective-permute-start.19
  68.0 1.4 collective-permute-start.20
  70.0 17.1 %shard_map.433 = (f32[1232,768]{1,0:T(8,128)}, bf16[1232,768]{1,0:T(8,128)(2,1)}, bf16[1232,2304]{1,0:T(8,128)(2,1)}, f32[16,768]{1,0:T(8,128)}, f32[1232,1]{1,0:T(8,128)}, /*index=5*/bf16[768,128]{1,0:T(8,128)(2,1)}) custom-call(s32[2]{0:T(128)} %pad_add_fusion.where_ref, bf16[256,512]{1,0:T(8,128)(2,1)} %copy-done.32, bf16[400,640]{1,0:T(8,128)(2,1)} %copy-done.27, ...), custom_call_target="tpu_custom_call" | custom-call | flops 1 | bytes 1 | tf_op jit(solution)/shard_map/pallas_call | solution.py:830
  90.5 19.1 %shard_map.435 = (bf16[1232,768]{1,0:T(8,128)(2,1)}, f32[1232,128]{1,0:T(8,128)}) custom-call(bf16[1232,2304]{1,0:T(8,128)(2,1)} %get-tuple-element.468.q_ref.k_ref.v_ref, bf16[1232,2304]{1,0:T(8,128)(2,1)} %get-tuple-element.468.q_ref.k_ref.v_ref, bf16[1232,2304]{1,0:T(8,128)(2,1)} %get-tuple-element.468.q_ref.k_ref.v_ref), custom_call_target="tpu_custom_call" | custom-call | flops 1 | bytes 1 | tf_op jit(solution)/shard_map/pallas_call | solution.py:621
  109.6 6.5 %collective-permute-done.22.refs_13_ = bf16[4,192,768]{2,1,0:T(8,128)(2,1)S(1)} collective-permute-done((bf16[4,192,768]{2,1,0:T(8,128)(2,1)S(1)}, bf16[4,192,768]{2,1,0:T(8,128)(2,1)S(1)}, u32[]{:S(2)}, u32[]{:S(2)}) %collective-permute-start.22) | collective-permute-done | bytes 1179680 | tf_op jit(solution)/shard_map/ppermute | solution.py:21
  117.2 1.8 collective-permute-done.23.refs_8_
  120.0 1.7 copy.59
  121.7 1.5 reshape.109.refs_3_
  126.3 68.9 %shard_map.436 = (bf16[1,256,768]{2,1,0:T(8,128)(2,1)}, bf16[1,400,768]{2,1,0:T(8,128)(2,1)}, bf16[1,576,768]{2,1,0:T(8,128)(2,1)}, bf16[2,8,48,1536]{3,2,1,0:T(...) custom-call(s32[2]{0:T(128)} %pad_add_fusion.where_ref, ...), custom_call_target="tpu_custom_call" | custom-call | flops 1 | bytes 1 | tf_op jit(solution)/shard_map/pallas_call | solution.py:1114
  195.8 1.5 copy-done.8
  197.3 6.4 %shard_map.437.refs_0_ = bf16[3,256,768]{2,1,0:T(8,128)(2,1)S(1)} custom-call(bf16[1232,2304]{1,0:T(8,128)(2,1)S(1)} %bitcast.42, bf16[1232,2304]{1,0:T(8,128)(2,1)S(1)} %bitcast.42, bf16[1232,2304]{1,0:T(8,128)(2,1)S(1)} %bitcast.42, bf16[1232,768]{1,0:T(8,128)(2,1)S(1)} %copy-done.3, bf16[1232,768]{1,0:T(8,128)(2,1)S(1)} %copy-done.8, ...), custom_call_target="tpu_custom_call" | custom-call | flops 1 | bytes 1 | tf_op jit(solution)/shard_map/pallas_call | solution.py:691
  208.5 24.0 %shard_map.440.refs_0_ = bf16[3,1232,768]{2,1,0:T(8,128)(2,1)S(1)} custom-call(bf16[1232,2304]{1,0:T(8,128)(2,1)S(1)} %bitcast.42, bf16[1232,2304]{1,0:T(8,128)(2,1)S(1)} %bitcast.42, bf16[1232,2304]{1,0:T(8,128)(2,1)S(1)} %bitcast.42, bf16[1232,768]{1,0:T(8,128)(2,1)S(1)} %copy-done.3, bf16[1232,768]{1,0:T(8,128)(2,1)S(1)} %copy-done.9, ...), custom_call_target="tpu_custom_call" | custom-call | flops 1 | bytes 1 | tf_op jit(solution)/shard_map/pallas_call | solution.py:691
  232.5 2.4 copy-done.2
  235.2 5.6 %collective-permute-done.31.refs_1_ = bf16[4,240,768]{2,1,0:T(8,128)(2,1)S(1)} collective-permute-done((bf16[4,240,768]{2,1,0:T(8,128)(2,1)S(1)}, bf16[4,240,768]{2,1,0:T(8,128)(2,1)S(1)}, u32[]{:S(2)}, u32[]{:S(2)}) %collective-permute-start.31) | collective-permute-done | bytes 1474592 | tf_op jit(solution)/shard_map/ppermute | solution.py:21
  246.1 1.8 convert_element_type.37.refs_5_
  252.5 24.1 %shard_map.443 = (bf16[1232,768]{1,0:T(8,128)(2,1)}, bf16[8,48,2304]{2,1,0:T(8,128)(2,1)}, bf16[8,48,2304]{2,1,0:T(8,128)(2,1)}, bf16[2,8,48,1024]{3,2,1,0:T(8,128)(2,1)S(1)}, bf16[2,8,48,1024]{3,2,1,0:T(8,128)(2,1)S(1)}) custom-call(s32[2]{0:T(128)S(1)} %copy-done.51, bf16[3,1232,768]{2,1,0:T(8,128)(2,1)} %copy-done.2, ...), custom_call_target="tpu_custom_call" | custom-call | flops 1 | bytes 1 | tf_op jit(solution)/shard_map/pallas_call | solution.py:1280
  279.7 2.6 collective-permute-done.35.refs_1_
  284.2 1.5 collective-permute-start.39
  285.8 1.4 collective-permute-start.37
  287.1 1.6 collective-permute-start.38
  288.8 7.4 %shard_map.448 = (bf16[1,3,160,160]{3,2,1,0:T(8,128)(2,1)}, bf16[1,3,240,240]{3,2,1,0:T(8,128)(2,1)}, bf16[1,3,384,384]{3,2,1,0:T(8,128)(2,1)}) custom-call(s32[2]{0:T(128)S(1)} %copy-done.51, bf16[1232,768]{1,0:T(8,128)(2,1)S(1)} %copy-done.29, bf16[8,48,1024]{2,1,0:T(8,128)(2,1)S(1)} %copy-done.11, bf16[8,48,1024]{2,1,0:T(8,128)(2,1)S(1)} %copy-done.20, ...), custom_call_target="tpu_custom_call" | custom-call | flops 1 | bytes 1 | tf_op jit(solution)/shard_map/pallas_call | solution.py:537
  296.2 4.8 %collective-permute-done.38.refs_1_ = bf16[2,48,1536]{2,1,0:T(8,128)(2,1)S(1)} collective-permute-done((bf16[2,48,1536]{2,1,0:T(8,128)(2,1)S(1)}, bf16[2,48,1536]{2,1,0:T(8,128)(2,1)S(1)}, u32[]{:S(2)}, u32[]{:S(2)}) %collective-permute-start.38) | collective-permute-done | bytes 294944 | tf_op jit(solution)/shard_map/ppermute | solution.py:21
  301.1 3.6 %collective-permute-done.37.refs_1_ = bf16[1,240,768]{2,1,0:T(8,128)(2,1)S(1)} collective-permute-done((bf16[1,240,768]{2,1,0:T(8,128)(2,1)S(1)}, bf16[1,240,768]{2,1,0:T(8,128)(2,1)S(1)}, u32[]{:S(2)}, u32[]{:S(2)}) %collective-permute-start.37) | collective-permute-done | bytes 368672 | tf_op jit(solution)/shard_map/ppermute | solution.py:21
  307.6 7.6 %collective-permute-done.41.refs_1_ = bf16[4,48,1024]{2,1,0:T(8,128)(2,1)S(1)} collective-permute-done((bf16[4,48,1024]{2,1,0:T(8,128)(2,1)S(1)}, bf16[4,48,1024]{2,1,0:T(8,128)(2,1)S(1)}, u32[]{:S(2)}, u32[]{:S(2)}) %collective-permute-start.41) | collective-permute-done | bytes 393248 | tf_op jit(solution)/shard_map/ppermute | solution.py:21
  315.7 3.4 collective-permute-start.44
  319.3 5.5 %collective-permute-done.43.refs_1_ = bf16[2,48,1024]{2,1,0:T(8,128)(2,1)S(1)} collective-permute-done((bf16[2,48,1024]{2,1,0:T(8,128)(2,1)S(1)}, bf16[2,48,1024]{2,1,0:T(8,128)(2,1)S(1)}, u32[]{:S(2)}, u32[]{:S(2)}) %collective-permute-start.43) | collective-permute-done | bytes 196640 | tf_op jit(solution)/shard_map/ppermute | solution.py:21
  324.9 7.3 %collective-permute-done.44.refs_1_ = bf16[1,48,1536]{2,1,0:T(8,128)(2,1)S(1)} collective-permute-done((bf16[1,48,1536]{2,1,0:T(8,128)(2,1)S(1)}, bf16[1,48,1536]{2,1,0:T(8,128)(2,1)S(1)}, u32[]{:S(2)}, u32[]{:S(2)}) %collective-permute-start.44) | collective-permute-done | bytes 147488 | tf_op jit(solution)/shard_map/ppermute | solution.py:21
  333.2 3.7 %collective-permute-done.45.refs_1_ = bf16[1,48,2304]{2,1,0:T(8,128)(2,1)S(1)} collective-permute-done((bf16[1,48,2304]{2,1,0:T(8,128)(2,1)S(1)}, bf16[1,48,2304]{2,1,0:T(8,128)(2,1)S(1)}, u32[]{:S(2)}, u32[]{:S(2)}) %collective-permute-start.45) | collective-permute-done | bytes 221216 | tf_op jit(solution)/shard_map/ppermute | solution.py:21
  336.9 2.2 collective-permute-done.47.refs_1_
  339.2 1.6 collective-permute-start.50
  343.8 3.0 collective-permute-done.49
  349.9 2.1 shard_map.459
  (261 shorter events, 57.4 us)
Async XLA Ops:
  1.6 15.7 %collective-permute-start = (bf16[1,48,1152]{2,1,0:T(8,128)(2,1)S(1)}, bf16[1,48,1152]{2,1,0:T(8,128)(2,1)S(1)}, u32[]{:S(2)}, u32[]{:S(2)}) collective-permute-start(bf16[1,48,1152]{2,1,0:T(8,128)(2,1)S(1)} %dynamic-slice_bitcast_fusion.refs_0_), channel_id=1, source_target_pairs={{0,8},{1,9},{2,10},{3,11},{4,12},{5,13},{6,14},{7,15},{8,0},{9,1},... | collective-permute-start | bytes 331784 | tf_op jit(solution)/shard_map/ppermute | solution.py:21
  12.8 10.8 %collective-permute-start.2 = (bf16[1,48,1024]{2,1,0:T(8,128)(2,1)}, bf16[1,48,1024]{2,1,0:T(8,128)(2,1)S(1)}, u32[]{:S(2)}, u32[]{:S(2)}) collective-permute-start(bf16[1,48,1024]{2,1,0:T(8,128)(2,1)} %bitcast.53), channel_id=1, source_target_pairs={{0,8},{1,9},{2,10},{3,11},{4,12},{5,13},{6,14},{7,15},{8,0},{9,1},... | collective-permute-start | bytes 294920 | tf_op jit(solution)/shard_map/ppermute | solution.py:21
  12.9 11.8 %collective-permute-start.1 = (bf16[1,48,1024]{2,1,0:T(8,128)(2,1)}, bf16[1,48,1024]{2,1,0:T(8,128)(2,1)S(1)}, u32[]{:S(2)}, u32[]{:S(2)}) collective-permute-start(bf16[1,48,1024]{2,1,0:T(8,128)(2,1)} %bitcast.55), channel_id=1, source_target_pairs={{0,8},{1,9},{2,10},{3,11},{4,12},{5,13},{6,14},{7,15},{8,0},{9,1},... | collective-permute-start | bytes 294920 | tf_op jit(solution)/shard_map/ppermute | solution.py:21
  17.3 9.5 %collective-permute-start.3 = (bf16[2,48,1152]{2,1,0:T(8,128)(2,1)S(1)}, bf16[2,48,1152]{2,1,0:T(8,128)(2,1)S(1)}, u32[]{:S(2)}, u32[]{:S(2)}) collective-permute-start(bf16[2,48,1152]{2,1,0:T(8,128)(2,1)S(1)} %shard_map.419.refs_0_), channel_id=1, source_target_pairs={{0,4},{1,5},{2,6},{3,7},{4,0},{5,1},{6,2},{7,3},{8,12},{9,13},{10,... | collective-permute-start | bytes 663560 | tf_op jit(solution)/shard_map/ppermute | solution.py:21
  26.9 16.2 %collective-permute-start.7 = (bf16[4,48,1152]{2,1,0:T(8,128)(2,1)S(1)}, bf16[4,48,1152]{2,1,0:T(8,128)(2,1)S(1)}, u32[]{:S(2)}, u32[]{:S(2)}) collective-permute-start(bf16[4,48,1152]{2,1,0:T(8,128)(2,1)S(1)} %shard_map.422.refs_0_), channel_id=1, source_target_pairs={{0,16},{16,0},{1,17},{17,1},{2,18},{18,2},{3,19},{19,3},{4,20},{20... | collective-permute-start | bytes 1327112 | tf_op jit(solution)/shard_map/ppermute | solution.py:21
  28.5 14.6 %collective-permute-start.6 = (bf16[4,48,1152]{2,1,0:T(8,128)(2,1)S(1)}, bf16[4,48,1152]{2,1,0:T(8,128)(2,1)S(1)}, u32[]{:S(2)}, u32[]{:S(2)}) collective-permute-start(bf16[4,48,1152]{2,1,0:T(8,128)(2,1)S(1)} %shard_map.422.refs_0_), channel_id=1, source_target_pairs={{0,2},{1,3},{2,0},{3,1},{4,6},{5,7},{6,4},{7,5},{8,10},{9,11},{10,... | collective-permute-start | bytes 1327112 | tf_op jit(solution)/shard_map/ppermute | solution.py:21
  30.0 10.9 %collective-permute-start.4 = (bf16[2,48,1024]{2,1,0:T(8,128)(2,1)S(1)}, bf16[2,48,1024]{2,1,0:T(8,128)(2,1)S(1)}, u32[]{:S(2)}, u32[]{:S(2)}) collective-permute-start(bf16[2,48,1024]{2,1,0:T(8,128)(2,1)S(1)} %shard_map.420.refs_0_), channel_id=1, source_target_pairs={{0,4},{1,5},{2,6},{3,7},{4,0},{5,1},{6,2},{7,3},{8,12},{9,13},{10,... | collective-permute-start | bytes 589832 | tf_op jit(solution)/shard_map/ppermute | solution.py:21
  30.0 12.9 %collective-permute-start.5 = (bf16[2,48,1024]{2,1,0:T(8,128)(2,1)S(1)}, bf16[2,48,1024]{2,1,0:T(8,128)(2,1)S(1)}, u32[]{:S(2)}, u32[]{:S(2)}) collective-permute-start(bf16[2,48,1024]{2,1,0:T(8,128)(2,1)S(1)} %shard_map.421.refs_0_), channel_id=1, source_target_pairs={{0,4},{1,5},{2,6},{3,7},{4,0},{5,1},{6,2},{7,3},{8,12},{9,13},{10,... | collective-permute-start | bytes 589832 | tf_op jit(solution)/shard_map/ppermute | solution.py:21
  32.3 10.8 %collective-permute-start.8 = (bf16[1,48,1920]{2,1,0:T(8,128)(2,1)S(1)}, bf16[1,48,1920]{2,1,0:T(8,128)(2,1)S(1)}, u32[]{:S(2)}, u32[]{:S(2)}) collective-permute-start(bf16[1,48,1920]{2,1,0:T(8,128)(2,1)S(1)} %fusion.4.refs_0_), channel_id=1, source_target_pairs={{0,8},{1,9},{2,10},{3,11},{4,12},{5,13},{6,14},{7,15},{8,0},{9,1},... | collective-permute-start | bytes 552968 | tf_op jit(solution)/shard_map/ppermute | solution.py:21
  43.1 16.5 %collective-permute-start.11 = (bf16[4,48,1152]{2,1,0:T(8,128)(2,1)S(1)}, bf16[4,48,1152]{2,1,0:T(8,128)(2,1)S(1)}, u32[]{:S(2)}, u32[]{:S(2)}) collective-permute-start(bf16[4,48,1152]{2,1,0:T(8,128)(2,1)S(1)} %collective-permute-done.6.refs_1_), channel_id=1, source_target_pairs={{0,16},{16,0},{1,17},{17,1},{2,18},{18,2},{3,19},{19,3},{4,20},{20... | collective-permute-start | bytes 1327112 | tf_op jit(solution)/shard_map/ppermute | solution.py:21
  43.7 13.7 %collective-permute-start.9 = (bf16[4,48,1024]{2,1,0:T(8,128)(2,1)S(1)}, bf16[4,48,1024]{2,1,0:T(8,128)(2,1)S(1)}, u32[]{:S(2)}, u32[]{:S(2)}) collective-permute-start(bf16[4,48,1024]{2,1,0:T(8,128)(2,1)S(1)} %shard_map.423.refs_0_), channel_id=1, source_target_pairs={{0,2},{1,3},{2,0},{3,1},{4,6},{5,7},{6,4},{7,5},{8,10},{9,11},{10,... | collective-permute-start | bytes 1179656 | tf_op jit(solution)/shard_map/ppermute | solution.py:21
  44.2 15.3 %collective-permute-start.10 = (bf16[4,48,1024]{2,1,0:T(8,128)(2,1)S(1)}, bf16[4,48,1024]{2,1,0:T(8,128)(2,1)S(1)}, u32[]{:S(2)}, u32[]{:S(2)}) collective-permute-start(bf16[4,48,1024]{2,1,0:T(8,128)(2,1)S(1)} %shard_map.424.refs_0_), channel_id=1, source_target_pairs={{0,2},{1,3},{2,0},{3,1},{4,6},{5,7},{6,4},{7,5},{8,10},{9,11},{10,... | collective-permute-start | bytes 1179656 | tf_op jit(solution)/shard_map/ppermute | solution.py:21
  45.7 13.9 %collective-permute-start.13 = (bf16[2,48,1920]{2,1,0:T(8,128)(2,1)S(1)}, bf16[2,48,1920]{2,1,0:T(8,128)(2,1)S(1)}, u32[]{:S(2)}, u32[]{:S(2)}) collective-permute-start(bf16[2,48,1920]{2,1,0:T(8,128)(2,1)S(1)} %shard_map.425.refs_0_), channel_id=1, source_target_pairs={{0,4},{1,5},{2,6},{3,7},{4,0},{5,1},{6,2},{7,3},{8,12},{9,13},{10,... | collective-permute-start | bytes 1105928 | tf_op jit(solution)/shard_map/ppermute | solution.py:21
  46.7 10.7 %collective-permute-start.12 = (bf16[1,192,768]{2,1,0:T(8,128)(2,1)S(1)}, bf16[1,192,768]{2,1,0:T(8,128)(2,1)S(1)}, u32[]{:S(2)}, u32[]{:S(2)}) collective-permute-start(bf16[1,192,768]{2,1,0:T(8,128)(2,1)S(1)} %bitcast.51), channel_id=1, source_target_pairs={{0,8},{1,9},{2,10},{3,11},{4,12},{5,13},{6,14},{7,15},{8,0},{9,1},... | collective-permute-start | bytes 884744 | tf_op jit(solution)/shard_map/ppermute | solution.py:21
  63.1 6.9 %collective-permute-start.16 = (bf16[8,48,1152]{2,1,0:T(8,128)(2,1)S(1)}, bf16[8,48,1152]{2,1,0:T(8,128)(2,1)}, u32[]{:S(2)}, u32[]{:S(2)}) collective-permute-start(bf16[8,48,1152]{2,1,0:T(8,128)(2,1)S(1)} %shard_map.429.refs_8_.refs_11_), channel_id=1, source_target_pairs={{0,1},{1,0},{2,3},{3,2},{4,5},{5,4},{6,7},{7,6},{8,9},{9,8},{10,11... | collective-permute-start | bytes 2654216 | tf_op jit(solution)/shard_map/ppermute | solution.py:21
  63.1 6.8 %collective-permute-start.17 = (bf16[8,48,1152]{2,1,0:T(8,128)(2,1)S(1)}, bf16[8,48,1152]{2,1,0:T(8,128)(2,1)}, u32[]{:S(2)}, u32[]{:S(2)}) collective-permute-start(bf16[8,48,1152]{2,1,0:T(8,128)(2,1)S(1)} %shard_map.430.refs_9_.refs_12_), channel_id=1, source_target_pairs={{0,1},{1,0},{2,3},{3,2},{4,5},{5,4},{6,7},{7,6},{8,9},{9,8},{10,11... | collective-permute-start | bytes 2654216 | tf_op jit(solution)/shard_map/ppermute | solution.py:21
  63.6 23.6 %collective-permute-start.19 = (bf16[4,48,1920]{2,1,0:T(8,128)(2,1)}, bf16[4,48,1920]{2,1,0:T(8,128)(2,1)}, u32[]{:S(2)}, u32[]{:S(2)}) collective-permute-start(bf16[4,48,1920]{2,1,0:T(8,128)(2,1)} %shard_map.432.refs_4_), channel_id=1, source_target_pairs={{0,16},{16,0},{1,17},{17,1},{2,18},{18,2},{3,19},{19,3},{4,20},{20... | collective-permute-start | bytes 2211848 | tf_op jit(solution)/shard_map/ppermute | solution.py:21
  65.1 22.1 %collective-permute-start.18 = (bf16[4,48,1920]{2,1,0:T(8,128)(2,1)}, bf16[4,48,1920]{2,1,0:T(8,128)(2,1)}, u32[]{:S(2)}, u32[]{:S(2)}) collective-permute-start(bf16[4,48,1920]{2,1,0:T(8,128)(2,1)} %shard_map.432.refs_4_), channel_id=1, source_target_pairs={{0,2},{1,3},{2,0},{3,1},{4,6},{5,7},{6,4},{7,5},{8,10},{9,11},{10,... | collective-permute-start | bytes 2211848 | tf_op jit(solution)/shard_map/ppermute | solution.py:21
  68.0 19.2 %collective-permute-start.20 = (bf16[2,192,768]{2,1,0:T(8,128)(2,1)}, bf16[2,192,768]{2,1,0:T(8,128)(2,1)S(1)}, u32[]{:S(2)}, u32[]{:S(2)}) collective-permute-start(bf16[2,192,768]{2,1,0:T(8,128)(2,1)} %shard_map.431.refs_0_), channel_id=1, source_target_pairs={{0,4},{1,5},{2,6},{3,7},{4,0},{5,1},{6,2},{7,3},{8,12},{9,13},{10,... | collective-permute-start | bytes 1769480 | tf_op jit(solution)/shard_map/ppermute | solution.py:21
  88.4 27.8 %collective-permute-start.22 = (bf16[4,192,768]{2,1,0:T(8,128)(2,1)S(1)}, bf16[4,192,768]{2,1,0:T(8,128)(2,1)S(1)}, u32[]{:S(2)}, u32[]{:S(2)}) collective-permute-start(bf16[4,192,768]{2,1,0:T(8,128)(2,1)S(1)} %shard_map.434.refs_12_), channel_id=1, source_target_pairs={{0,2},{1,3},{2,0},{3,1},{4,6},{5,7},{6,4},{7,5},{8,10},{9,11},{10,... | collective-permute-start | bytes 3538952 | tf_op jit(solution)/shard_map/ppermute | solution.py:21
  89.4 20.2 %collective-permute-start.21 = (bf16[4,48,1920]{2,1,0:T(8,128)(2,1)}, bf16[4,48,1920]{2,1,0:T(8,128)(2,1)}, u32[]{:S(2)}, u32[]{:S(2)}) collective-permute-start(bf16[4,48,1920]{2,1,0:T(8,128)(2,1)} %collective-permute-done.18.refs_5_), channel_id=1, source_target_pairs={{0,16},{16,0},{1,17},{17,1},{2,18},{18,2},{3,19},{19,3},{4,20},{20... | collective-permute-start | bytes 2211848 | tf_op jit(solution)/shard_map/ppermute | solution.py:21
  116.2 9.1 %collective-permute-start.27 = (bf16[4,192,768]{2,1,0:T(8,128)(2,1)S(1)}, bf16[4,192,768]{2,1,0:T(8,128)(2,1)S(1)}, u32[]{:S(2)}, u32[]{:S(2)}) collective-permute-start(bf16[4,192,768]{2,1,0:T(8,128)(2,1)S(1)} %shard_map.434.refs_12_), channel_id=1, source_target_pairs={{0,1},{1,0},{2,3},{3,2},{4,5},{5,4},{6,7},{7,6},{8,9},{9,8},{10,11... | collective-permute-start | bytes 3538952 | tf_op jit(solution)/shard_map/ppermute | solution.py:21
  116.7 8.6 %collective-permute-start.28 = (bf16[4,192,768]{2,1,0:T(8,128)(2,1)S(1)}, bf16[4,192,768]{2,1,0:T(8,128)(2,1)}, u32[]{:S(2)}, u32[]{:S(2)}) collective-permute-start(bf16[4,192,768]{2,1,0:T(8,128)(2,1)S(1)} %collective-permute-done.22.refs_13_), channel_id=1, source_target_pairs={{0,1},{1,0},{2,3},{3,2},{4,5},{5,4},{6,7},{7,6},{8,9},{9,8},{10,11... | collective-permute-start | bytes 3538952 | tf_op jit(solution)/shard_map/ppermute | solution.py:21
  116.7 6.4 %collective-permute-start.24 = (bf16[4,48,1920]{2,1,0:T(8,128)(2,1)}, bf16[4,48,1920]{2,1,0:T(8,128)(2,1)}, u32[]{:S(2)}, u32[]{:S(2)}) collective-permute-start(bf16[4,48,1920]{2,1,0:T(8,128)(2,1)} %collective-permute-done.18.refs_5_), channel_id=1, source_target_pairs={{0,1},{1,0},{2,3},{3,2},{4,5},{5,4},{6,7},{7,6},{8,9},{9,8},{10,11... | collective-permute-start | bytes 2211848 | tf_op jit(solution)/shard_map/ppermute | solution.py:21
  117.2 7.0 %collective-permute-start.25 = (bf16[4,48,1920]{2,1,0:T(8,128)(2,1)}, bf16[4,48,1920]{2,1,0:T(8,128)(2,1)}, u32[]{:S(2)}, u32[]{:S(2)}) collective-permute-start(bf16[4,48,1920]{2,1,0:T(8,128)(2,1)} %collective-permute-done.19.refs_6_), channel_id=1, source_target_pairs={{0,1},{1,0},{2,3},{3,2},{4,5},{5,4},{6,7},{7,6},{8,9},{9,8},{10,11... | collective-permute-start | bytes 2211848 | tf_op jit(solution)/shard_map/ppermute | solution.py:21
  119.0 6.2 %collective-permute-start.26 = (bf16[4,48,1920]{2,1,0:T(8,128)(2,1)}, bf16[4,48,1920]{2,1,0:T(8,128)(2,1)}, u32[]{:S(2)}, u32[]{:S(2)}) collective-permute-start(bf16[4,48,1920]{2,1,0:T(8,128)(2,1)} %collective-permute-done.21.refs_7_), channel_id=1, source_target_pairs={{0,1},{1,0},{2,3},{3,2},{4,5},{5,4},{6,7},{7,6},{8,9},{9,8},{10,11... | collective-permute-start | bytes 2211848 | tf_op jit(solution)/shard_map/ppermute | solution.py:21
  195.2 9.0 %collective-permute-start.29 = (bf16[8,240,768]{2,1,0:T(8,128)(2,1)}, bf16[8,240,768]{2,1,0:T(8,128)(2,1)S(1)}, u32[]{:S(2)}, u32[]{:S(2)}) collective-permute-start(bf16[8,240,768]{2,1,0:T(8,128)(2,1)} %get-tuple-element.499), channel_id=1, source_target_pairs={{0,1},{1,0},{2,3},{3,2},{4,5},{5,4},{6,7},{7,6},{8,9},{9,8},{10,11... | collective-permute-start | bytes 8847368 | tf_op jit(solution)/shard_map/ppermute | solution.py:21
  195.4 8.8 %collective-permute-start.30 = (bf16[2,8,48,1536]{3,2,1,0:T(8,128)(2,1)}, bf16[2,8,48,1536]{3,2,1,0:T(8,128)(2,1)S(1)}, u32[]{:S(2)}, u32[]{:S(2)}) collective-permute-start(bf16[2,8,48,1536]{3,2,1,0:T(8,128)(2,1)} %get-tuple-element.500), channel_id=1, source_target_pairs={{0,1},{1,0},{2,3},{3,2},{4,5},{5,4},{6,7},{7,6},{8,9},{9,8},{10,11... | collective-permute-start | bytes 7077896 | tf_op jit(solution)/shard_map/ppermute | solution.py:21
  206.4 34.4 %collective-permute-start.31 = (bf16[4,240,768]{2,1,0:T(8,128)(2,1)S(1)}, bf16[4,240,768]{2,1,0:T(8,128)(2,1)S(1)}, u32[]{:S(2)}, u32[]{:S(2)}) collective-permute-start(bf16[4,240,768]{2,1,0:T(8,128)(2,1)S(1)} %get-tuple-element.509), channel_id=1, source_target_pairs={{0,2},{1,3},{2,0},{3,1},{4,6},{5,7},{6,4},{7,5},{8,10},{9,11},{10,... | collective-permute-start | bytes 4423688 | tf_op jit(solution)/shard_map/ppermute | solution.py:21
  207.5 27.7 %collective-permute-start.32 = (bf16[8,48,1536]{2,1,0:T(8,128)(2,1)S(1)}, bf16[8,48,1536]{2,1,0:T(8,128)(2,1)S(1)}, u32[]{:S(2)}, u32[]{:S(2)}) collective-permute-start(bf16[8,48,1536]{2,1,0:T(8,128)(2,1)S(1)} %get-tuple-element.510), channel_id=1, source_target_pairs={{0,16},{16,0},{1,17},{17,1},{2,18},{18,2},{3,19},{19,3},{4,20},{20... | collective-permute-start | bytes 3538952 | tf_op jit(solution)/shard_map/ppermute | solution.py:21
  243.8 32.8 %collective-permute-start.33 = (bf16[2,240,768]{2,1,0:T(8,128)(2,1)}, bf16[2,240,768]{2,1,0:T(8,128)(2,1)}, u32[]{:S(2)}, u32[]{:S(2)}) collective-permute-start(bf16[2,240,768]{2,1,0:T(8,128)(2,1)} %get-tuple-element.529), channel_id=1, source_target_pairs={{0,4},{1,5},{2,6},{3,7},{4,0},{5,1},{6,2},{7,3},{8,12},{9,13},{10,... | collective-permute-start | bytes 2211848 | tf_op jit(solution)/shard_map/ppermute | solution.py:21
  244.4 32.2 %collective-permute-start.34 = (bf16[4,48,1536]{2,1,0:T(8,128)(2,1)}, bf16[4,48,1536]{2,1,0:T(8,128)(2,1)}, u32[]{:S(2)}, u32[]{:S(2)}) collective-permute-start(bf16[4,48,1536]{2,1,0:T(8,128)(2,1)} %get-tuple-element.530), channel_id=1, source_target_pairs={{0,2},{1,3},{2,0},{3,1},{4,6},{5,7},{6,4},{7,5},{8,10},{9,11},{10,... | collective-permute-start | bytes 1769480 | tf_op jit(solution)/shard_map/ppermute | solution.py:21
  276.6 5.7 %collective-permute-start.35 = (bf16[8,48,2304]{2,1,0:T(8,128)(2,1)}, bf16[8,48,2304]{2,1,0:T(8,128)(2,1)S(1)}, u32[]{:S(2)}, u32[]{:S(2)}) collective-permute-start(bf16[8,48,2304]{2,1,0:T(8,128)(2,1)} %get-tuple-element.542), channel_id=1, source_target_pairs={{0,1},{1,0},{2,3},{3,2},{4,5},{5,4},{6,7},{7,6},{8,9},{9,8},{10,11... | collective-permute-start | bytes 5308424 | tf_op jit(solution)/shard_map/ppermute | solution.py:21
  276.7 7.2 %collective-permute-start.36 = (bf16[2,8,48,1024]{3,2,1,0:T(8,128)(2,1)S(1)}, bf16[2,8,48,1024]{3,2,1,0:T(8,128)(2,1)S(1)}, u32[]{:S(2)}, u32[]{:S(2)}) collective-permute-start(bf16[2,8,48,1024]{3,2,1,0:T(8,128)(2,1)S(1)} %get-tuple-element.548), channel_id=1, source_target_pairs={{0,1},{1,0},{2,3},{3,2},{4,5},{5,4},{6,7},{7,6},{8,9},{9,8},{10,11... | collective-permute-start | bytes 4718600 | tf_op jit(solution)/shard_map/ppermute | solution.py:21
  282.8 22.9 %collective-permute-start.40 = (bf16[4,48,2304]{2,1,0:T(8,128)(2,1)S(1)}, bf16[4,48,2304]{2,1,0:T(8,128)(2,1)S(1)}, u32[]{:S(2)}, u32[]{:S(2)}) collective-permute-start(bf16[4,48,2304]{2,1,0:T(8,128)(2,1)S(1)} %get-tuple-element.580), channel_id=1, source_target_pairs={{0,2},{1,3},{2,0},{3,1},{4,6},{5,7},{6,4},{7,5},{8,10},{9,11},{10,... | collective-permute-start | bytes 2654216 | tf_op jit(solution)/shard_map/ppermute | solution.py:21
  284.2 20.6 %collective-permute-start.39 = (bf16[8,48,1024]{2,1,0:T(8,128)(2,1)S(1)}, bf16[8,48,1024]{2,1,0:T(8,128)(2,1)S(1)}, u32[]{:S(2)}, u32[]{:S(2)}) collective-permute-start(bf16[8,48,1024]{2,1,0:T(8,128)(2,1)S(1)} %get-tuple-element.570), channel_id=1, source_target_pairs={{0,16},{16,0},{1,17},{17,1},{2,18},{18,2},{3,19},{19,3},{4,20},{20... | collective-permute-start | bytes 2359304 | tf_op jit(solution)/shard_map/ppermute | solution.py:21
  285.8 18.9 %collective-permute-start.37 = (bf16[1,240,768]{2,1,0:T(8,128)(2,1)S(1)}, bf16[1,240,768]{2,1,0:T(8,128)(2,1)S(1)}, u32[]{:S(2)}, u32[]{:S(2)}) collective-permute-start(bf16[1,240,768]{2,1,0:T(8,128)(2,1)S(1)} %get-tuple-element.557), channel_id=1, source_target_pairs={{0,8},{1,9},{2,10},{3,11},{4,12},{5,13},{6,14},{7,15},{8,0},{9,1},... | collective-permute-start | bytes 1105928 | tf_op jit(solution)/shard_map/ppermute | solution.py:21
  287.1 14.0 %collective-permute-start.38 = (bf16[2,48,1536]{2,1,0:T(8,128)(2,1)S(1)}, bf16[2,48,1536]{2,1,0:T(8,128)(2,1)S(1)}, u32[]{:S(2)}, u32[]{:S(2)}) collective-permute-start(bf16[2,48,1536]{2,1,0:T(8,128)(2,1)S(1)} %get-tuple-element.558), channel_id=1, source_target_pairs={{0,4},{1,5},{2,6},{3,7},{4,0},{5,1},{6,2},{7,3},{8,12},{9,13},{10,... | collective-permute-start | bytes 884744 | tf_op jit(solution)/shard_map/ppermute | solution.py:21
  305.0 10.2 %collective-permute-start.41 = (bf16[4,48,1024]{2,1,0:T(8,128)(2,1)S(1)}, bf16[4,48,1024]{2,1,0:T(8,128)(2,1)S(1)}, u32[]{:S(2)}, u32[]{:S(2)}) collective-permute-start(bf16[4,48,1024]{2,1,0:T(8,128)(2,1)S(1)} %get-tuple-element.590), channel_id=1, source_target_pairs={{0,2},{1,3},{2,0},{3,1},{4,6},{5,7},{6,4},{7,5},{8,10},{9,11},{10,... | collective-permute-start | bytes 1179656 | tf_op jit(solution)/shard_map/ppermute | solution.py:21
  305.8 13.3 %collective-permute-start.42 = (bf16[2,48,2304]{2,1,0:T(8,128)(2,1)S(1)}, bf16[2,48,2304]{2,1,0:T(8,128)(2,1)S(1)}, u32[]{:S(2)}, u32[]{:S(2)}) collective-permute-start(bf16[2,48,2304]{2,1,0:T(8,128)(2,1)S(1)} %get-tuple-element.600), channel_id=1, source_target_pairs={{0,4},{1,5},{2,6},{3,7},{4,0},{5,1},{6,2},{7,3},{8,12},{9,13},{10,... | collective-permute-start | bytes 1327112 | tf_op jit(solution)/shard_map/ppermute | solution.py:21
  306.5 30.4 %collective-permute-start.46 = (bf16[240,768]{1,0:T(8,128)(2,1)S(1)}, bf16[240,768]{1,0:T(8,128)(2,1)S(1)}, u32[]{:S(2)}, u32[]{:S(2)}) collective-permute-start(bf16[240,768]{1,0:T(8,128)(2,1)S(1)} %bitcast.47), channel_id=1, source_target_pairs={{0,16},{16,0},{1,17},{17,1},{2,18},{18,2},{3,19},{19,3},{4,20},{20... | collective-permute-start | bytes 1105928 | tf_op jit(solution)/shard_map/ppermute | solution.py:21
  315.3 9.5 %collective-permute-start.43 = (bf16[2,48,1024]{2,1,0:T(8,128)(2,1)S(1)}, bf16[2,48,1024]{2,1,0:T(8,128)(2,1)S(1)}, u32[]{:S(2)}, u32[]{:S(2)}) collective-permute-start(bf16[2,48,1024]{2,1,0:T(8,128)(2,1)S(1)} %get-tuple-element.610), channel_id=1, source_target_pairs={{0,4},{1,5},{2,6},{3,7},{4,0},{5,1},{6,2},{7,3},{8,12},{9,13},{10,... | collective-permute-start | bytes 589832 | tf_op jit(solution)/shard_map/ppermute | solution.py:21
  315.7 16.4 %collective-permute-start.44 = (bf16[1,48,1536]{2,1,0:T(8,128)(2,1)S(1)}, bf16[1,48,1536]{2,1,0:T(8,128)(2,1)S(1)}, u32[]{:S(2)}, u32[]{:S(2)}) collective-permute-start(bf16[1,48,1536]{2,1,0:T(8,128)(2,1)S(1)} %get-tuple-element.620), channel_id=1, source_target_pairs={{0,8},{1,9},{2,10},{3,11},{4,12},{5,13},{6,14},{7,15},{8,0},{9,1},... | collective-permute-start | bytes 442376 | tf_op jit(solution)/shard_map/ppermute | solution.py:21
  319.2 17.7 %collective-permute-start.45 = (bf16[1,48,2304]{2,1,0:T(8,128)(2,1)S(1)}, bf16[1,48,2304]{2,1,0:T(8,128)(2,1)S(1)}, u32[]{:S(2)}, u32[]{:S(2)}) collective-permute-start(bf16[1,48,2304]{2,1,0:T(8,128)(2,1)S(1)} %get-tuple-element.629), channel_id=1, source_target_pairs={{0,8},{1,9},{2,10},{3,11},{4,12},{5,13},{6,14},{7,15},{8,0},{9,1},... | collective-permute-start | bytes 663560 | tf_op jit(solution)/shard_map/ppermute | solution.py:21
  332.2 7.0 %collective-permute-start.48 = (bf16[48,1536]{1,0:T(8,128)(2,1)S(1)}, bf16[48,1536]{1,0:T(8,128)(2,1)S(1)}, u32[]{:S(2)}, u32[]{:S(2)}) collective-permute-start(bf16[48,1536]{1,0:T(8,128)(2,1)S(1)} %bitcast.49), channel_id=1, source_target_pairs={{0,16},{16,0},{1,17},{17,1},{2,18},{18,2},{3,19},{19,3},{4,20},{20... | collective-permute-start | bytes 442376 | tf_op jit(solution)/shard_map/ppermute | solution.py:21
  333.2 5.9 %collective-permute-start.47 = (bf16[1,48,1024]{2,1,0:T(8,128)(2,1)S(1)}, bf16[1,48,1024]{2,1,0:T(8,128)(2,1)S(1)}, u32[]{:S(2)}, u32[]{:S(2)}) collective-permute-start(bf16[1,48,1024]{2,1,0:T(8,128)(2,1)S(1)} %get-tuple-element.645), channel_id=1, source_target_pairs={{0,8},{1,9},{2,10},{3,11},{4,12},{5,13},{6,14},{7,15},{8,0},{9,1},... | collective-permute-start | bytes 294920 | tf_op jit(solution)/shard_map/ppermute | solution.py:21
  339.2 7.6 %collective-permute-start.50 = (bf16[48,1024]{1,0:T(8,128)(2,1)S(1)}, bf16[48,1024]{1,0:T(8,128)(2,1)S(1)}, u32[]{:S(2)}, u32[]{:S(2)}) collective-permute-start(bf16[48,1024]{1,0:T(8,128)(2,1)S(1)} %bitcast.50), channel_id=1, source_target_pairs={{0,16},{16,0},{1,17},{17,1},{2,18},{18,2},{3,19},{19,3},{4,20},{20... | collective-permute-start | bytes 294920 | tf_op jit(solution)/shard_map/ppermute | solution.py:21
  340.8 5.9 %collective-permute-start.49 = (bf16[48,2304]{1,0:T(8,128)(2,1)S(1)}, bf16[48,2304]{1,0:T(8,128)(2,1)S(1)}, u32[]{:S(2)}, u32[]{:S(2)}) collective-permute-start(bf16[48,2304]{1,0:T(8,128)(2,1)S(1)} %bitcast.48), channel_id=1, source_target_pairs={{0,16},{16,0},{1,17},{17,1},{2,18},{18,2},{3,19},{19,3},{4,20},{20... | collective-permute-start | bytes 663560 | tf_op jit(solution)/shard_map/ppermute | solution.py:21
  (66 other events, 721.0 us)

commit v3 on v2

--- a/solution.py
+++ b/solution.py
@@ -1433,6 +1433,8 @@
     grad_qkv = attend_backward(qkv, mixed, totals, grad_mixed, starts[:2])
     grad_qkv = together(grad_qkv, down_sums, up_sums)
     grad_qkv = attend_backward(qkv, mixed, totals, grad_mixed, starts[1:], (grad_qkv,))
+    bias_columns = grad_b_up.reshape(width, up_per).astype(BF16)
+    grad_qkv, bias_columns = after(grad_qkv, bias_columns)
     grad_qkv = together(grad_qkv, down_sums, up_sums)
     half = columns // 2
     low_columns = half + 5 * width // 3
@@ -1443,7 +1445,7 @@
         branch,
         lines,
         sums,
-        grad_b_up.reshape(width, up_per).astype(BF16),
+        bias_columns,
         inverse,
         maps,
         patches,

time: 357 us -> 354 us (level)
  waiting for transfers between devices: 80.1 us -> 76.2 us
    ppermute x51, waiting for transfers between devices: 80.1 us -> 76.2 us  [swap(): return lax.ppermute(value, axis, [(i, i ^ bit) for i in range(size)])]
    unnamed x127 -> x131, local copies, waits for them, and re-layouts: 14.8 us -> 16.1 us
  transfers between devices with their start and end apart: 51 -> 51, of which waited for: 24 -> 22; matrix products, arithmetic and copies ran while one was open for 4% -> 3% of each run, Pallas kernels for 32% -> 32%
where the time goes in v3:
time: 354 us; the launch traced here: 350 us
  Pallas kernels  193 us (55%)
  waiting for transfers between devices  76.2 us (22%)
  starting transfers between devices  47.9 us (14%)
  local copies, waits for them, and re-layouts  27.4 us (8%)
  other arithmetic  3.62 us (1%)
    ppermute x51, waiting for transfers between devices, swap(): return lax.ppermute(value, axis, [(i, i ^ bit) for i in range(size)])  76.2 us
    pallas_call x1, Pallas kernels, feed_all(): pl.pallas_call(functools.partial(feed_kernel, starts, chunk), grid_spec=p...  68.8 us
    ppermute x51, starting transfers between devices, swap(): return lax.ppermute(value, axis, [(i, i ^ bit) for i in range(size)])  47.9 us
    pallas_call x2, Pallas kernels, attend_backward(): pl.pallas_call(functools.partial(attend_back_kernel, starts, chunk), grid...  30.4 us
    pallas_call x1, Pallas kernels, leave_all(): pl.pallas_call(functools.partial(leave_kernel, qkv_parts.pieces, starts,...  24 us
    pallas_call x1, Pallas kernels, attend_forward(): pl.pallas_call(functools.partial(attend_kernel, starts, chunk), grid=(pai...  19.2 us
    pallas_call x1, Pallas kernels, enter_all(): pl.pallas_call(functools.partial(enter_kernel, embed_parts.pieces, qkv_pa...  17.2 us
    unnamed x131, local copies, waits for them, and re-layouts  16.1 us
  transfers between devices with their start and end apart: 51, of which 22 were waited for; matrix products, arithmetic and copies ran while one was open for 3% of the time, Pallas kernels for 32%

profile of v3, /device:TPU:0, one launch (start us, length us, event | category | flops | bytes accessed | tf_op | source)
XLA Modules:
  0.0 349.7 jit_solution(1814749783976304373)
XLA Ops:
  1.6 4.1 %collective-permute-start = (bf16[1,48,1152]{2,1,0:T(8,128)(2,1)S(1)}, bf16[1,48,1152]{2,1,0:T(8,128)(2,1)S(1)}, u32[]{:S(2)}, u32[]{:S(2)}) collective-permute-start(bf16[1,48,1152]{2,1,0:T(8,128)(2,1)S(1)} %dynamic-slice_bitcast_fusion.refs_0_), channel_id=1, source_target_pairs={{0,8},{1,9},{2,10},{3,11},{4,12},{5,13},{6,14},{7,15},{8,0},{9,1},... | collective-permute-start | bytes 331784 | tf_op jit(solution)/shard_map/ppermute | solution.py:21
  8.2 4.6 %shard_map.418 = (bf16[48,1024]{1,0:T(8,128)(2,1)}, bf16[48,1024]{1,0:T(8,128)(2,1)}) custom-call(f32[100,1024]{1,0:T(8,128)} %refs_0_.4, f32[144,1024]{1,0:T(8,128)} %refs_1_.4, f32[256,1024]{1,0:T(8,128)} %refs_2_.4, bf16[3,48,1024]{2,1,0:T(8,128)(2,1)} %bitcast.59, bf16[48,49]{1,0:T(8,128)(2,1)} %bitcast.61, bf16[1,48]{1,0:T(2,128)(2,1)} %bitcast.62, ...), custom_call_target="tpu_custom_call" | custom-call | flops 1 | bytes 1 | tf_op jit(solution)/shard_map/pallas_call | solution.py:770
  12.9 2.9 collective-permute-start.1
  17.4 1.6 collective-permute-start.3
  19.0 4.6 %collective-permute-done.2.refs_1_ = bf16[1,48,1024]{2,1,0:T(8,128)(2,1)S(1)} collective-permute-done((bf16[1,48,1024]{2,1,0:T(8,128)(2,1)}, bf16[1,48,1024]{2,1,0:T(8,128)(2,1)S(1)}, u32[]{:S(2)}, u32[]{:S(2)}) %collective-permute-start.2) | collective-permute-done | bytes 98336 | tf_op jit(solution)/shard_map/ppermute | solution.py:21
  24.8 2.1 collective-permute-done.3.refs_1_
  26.9 1.6 collective-permute-start.7
  30.1 2.0 collective-permute-start.5
  33.1 7.8 %collective-permute-done.4.refs_1_ = bf16[2,48,1024]{2,1,0:T(8,128)(2,1)S(1)} collective-permute-done((bf16[2,48,1024]{2,1,0:T(8,128)(2,1)S(1)}, bf16[2,48,1024]{2,1,0:T(8,128)(2,1)S(1)}, u32[]{:S(2)}, u32[]{:S(2)}) %collective-permute-start.4) | collective-permute-done | bytes 196640 | tf_op jit(solution)/shard_map/ppermute | solution.py:21
  40.9 2.1 collective-permute-done.5.refs_1_
  44.3 1.5 collective-permute-start.10
  46.7 1.9 collective-permute-start.12
  48.7 6.8 %shard_map.426 = (bf16[256,512]{1,0:T(8,128)(2,1)S(1)}, bf16[400,640]{1,0:T(8,128)(2,1)S(1)}, bf16[576,768]{1,0:T(8,128)(2,1)S(1)}) custom-call(bf16[1,3,160,160]{3,2,1,0:T(8,128)(2,1)S(1)} %copy-done.48, bf16[1,3,240,240]{3,2,1,0:T(8,128)(2,1)S(1)} %copy-done.45, bf16[1,3,384,384]{3,2,1,0:T(8,128)(2,1)S(1)} %copy-done.41), custom_call_target="tpu_custom_call" | custom-call | flops 1 | bytes 1 | tf_op jit(solution)/shard_map/pallas_call | solution.py:486
  55.5 1.8 collective-permute-done.12.refs_1_
  57.4 2.2 collective-permute-done.10.refs_1_
  63.6 1.5 collective-permute-start.19
  70.0 17.2 %shard_map.433 = (f32[1232,768]{1,0:T(8,128)}, bf16[1232,768]{1,0:T(8,128)(2,1)}, bf16[1232,2304]{1,0:T(8,128)(2,1)}, f32[16,768]{1,0:T(8,128)}, f32[1232,1]{1,0:T(8,128)}, /*index=5*/bf16[768,128]{1,0:T(8,128)(2,1)}) custom-call(s32[2]{0:T(128)} %pad_add_fusion.where_ref, bf16[256,512]{1,0:T(8,128)(2,1)} %copy-done.39, bf16[400,640]{1,0:T(8,128)(2,1)} %copy-done.30, ...), custom_call_target="tpu_custom_call" | custom-call | flops 1 | bytes 1 | tf_op jit(solution)/shard_map/pallas_call | solution.py:830
  90.5 19.2 %shard_map.435 = (bf16[1232,768]{1,0:T(8,128)(2,1)}, f32[1232,128]{1,0:T(8,128)}) custom-call(bf16[1232,2304]{1,0:T(8,128)(2,1)} %get-tuple-element.470.q_ref.k_ref.v_ref, bf16[1232,2304]{1,0:T(8,128)(2,1)} %get-tuple-element.470.q_ref.k_ref.v_ref, bf16[1232,2304]{1,0:T(8,128)(2,1)} %get-tuple-element.470.q_ref.k_ref.v_ref), custom_call_target="tpu_custom_call" | custom-call | flops 1 | bytes 1 | tf_op jit(solution)/shard_map/pallas_call | solution.py:621
  109.7 6.5 %collective-permute-done.22.refs_13_ = bf16[4,192,768]{2,1,0:T(8,128)(2,1)S(1)} collective-permute-done((bf16[4,192,768]{2,1,0:T(8,128)(2,1)S(1)}, bf16[4,192,768]{2,1,0:T(8,128)(2,1)S(1)}, u32[]{:S(2)}, u32[]{:S(2)}) %collective-permute-start.22) | collective-permute-done | bytes 1179680 | tf_op jit(solution)/shard_map/ppermute | solution.py:21
  117.3 1.8 collective-permute-done.23.refs_8_
  120.0 1.7 copy.59
  126.3 68.8 %shard_map.436 = (bf16[1,256,768]{2,1,0:T(8,128)(2,1)}, bf16[1,400,768]{2,1,0:T(8,128)(2,1)}, bf16[1,576,768]{2,1,0:T(8,128)(2,1)}, bf16[2,8,48,1536]{3,2,1,0:T(...) custom-call(s32[2]{0:T(128)} %pad_add_fusion.where_ref, ...), custom_call_target="tpu_custom_call" | custom-call | flops 1 | bytes 1 | tf_op jit(solution)/shard_map/pallas_call | solution.py:1114
  195.8 1.5 copy-done.9
  197.3 6.4 %shard_map.437.refs_0_ = bf16[3,256,768]{2,1,0:T(8,128)(2,1)S(1)} custom-call(bf16[1232,2304]{1,0:T(8,128)(2,1)S(1)} %bitcast.42, bf16[1232,2304]{1,0:T(8,128)(2,1)S(1)} %bitcast.42, bf16[1232,2304]{1,0:T(8,128)(2,1)S(1)} %bitcast.42, bf16[1232,768]{1,0:T(8,128)(2,1)S(1)} %copy-done.4, bf16[1232,768]{1,0:T(8,128)(2,1)S(1)} %copy-done.9, ...), custom_call_target="tpu_custom_call" | custom-call | flops 1 | bytes 1 | tf_op jit(solution)/shard_map/pallas_call | solution.py:691
  204.7 1.7 shard_map.438
  206.6 1.5 shard_map.439
  211.7 2.6 copy-done.2
  214.3 1.5 copy-done.10
  217.1 24.0 %shard_map.440.refs_0_ = bf16[3,1232,768]{2,1,0:T(8,128)(2,1)S(1)} custom-call(bf16[1232,2304]{1,0:T(8,128)(2,1)S(1)} %copy-done.2, bf16[1232,2304]{1,0:T(8,128)(2,1)S(1)} %copy-done.2, bf16[1232,2304]{1,0:T(8,128)(2,1)S(1)} %copy-done.2, bf16[1232,768]{1,0:T(8,128)(2,1)S(1)} %copy-done.4, bf16[1232,768]{1,0:T(8,128)(2,1)S(1)} %copy-done.10, ...), custom_call_target="tpu_custom_call" | custom-call | flops 1 | bytes 1 | tf_op jit(solution)/shard_map/pallas_call | solution.py:691
  241.1 2.5 copy-done.3
  243.8 1.9 shard_map.441
  245.7 1.7 shard_map.442
  249.5 24.0 %shard_map.443 = (bf16[1232,768]{1,0:T(8,128)(2,1)}, bf16[8,48,2304]{2,1,0:T(8,128)(2,1)}, bf16[8,48,2304]{2,1,0:T(8,128)(2,1)}, bf16[2,8,48,1024]{3,2,1,0:T(8,128)(2,1)S(1)}, bf16[2,8,48,1024]{3,2,1,0:T(8,128)(2,1)S(1)}) custom-call(s32[2]{0:T(128)S(1)} %copy-done.53, bf16[3,1232,768]{2,1,0:T(8,128)(2,1)} %copy-done.3, ...), custom_call_target="tpu_custom_call" | custom-call | flops 1 | bytes 1 | tf_op jit(solution)/shard_map/pallas_call | solution.py:1280
  274.4 4.8 %collective-permute-done.35.refs_1_ = bf16[8,48,2304]{2,1,0:T(8,128)(2,1)S(1)} collective-permute-done((bf16[8,48,2304]{2,1,0:T(8,128)(2,1)}, bf16[8,48,2304]{2,1,0:T(8,128)(2,1)S(1)}, u32[]{:S(2)}, u32[]{:S(2)}) %collective-permute-start.35) | collective-permute-done | bytes 1769504 | tf_op jit(solution)/shard_map/ppermute | solution.py:21
  280.8 1.5 collective-permute-start.39
  283.8 1.6 collective-permute-start.38
  285.4 7.4 %shard_map.448 = (bf16[1,3,160,160]{3,2,1,0:T(8,128)(2,1)}, bf16[1,3,240,240]{3,2,1,0:T(8,128)(2,1)}, bf16[1,3,384,384]{3,2,1,0:T(8,128)(2,1)}) custom-call(s32[2]{0:T(128)S(1)} %copy-done.53, bf16[1232,768]{1,0:T(8,128)(2,1)S(1)} %copy-done.32, bf16[8,48,1024]{2,1,0:T(8,128)(2,1)S(1)} %copy-done.12, bf16[8,48,1024]{2,1,0:T(8,128)(2,1)S(1)} %copy-done.23, ...), custom_call_target="tpu_custom_call" | custom-call | flops 1 | bytes 1 | tf_op jit(solution)/shard_map/pallas_call | solution.py:537
  292.8 4.9 %collective-permute-done.38.refs_1_ = bf16[2,48,1536]{2,1,0:T(8,128)(2,1)S(1)} collective-permute-done((bf16[2,48,1536]{2,1,0:T(8,128)(2,1)S(1)}, bf16[2,48,1536]{2,1,0:T(8,128)(2,1)S(1)}, u32[]{:S(2)}, u32[]{:S(2)}) %collective-permute-start.38) | collective-permute-done | bytes 294944 | tf_op jit(solution)/shard_map/ppermute | solution.py:21
  297.7 3.6 %collective-permute-done.37.refs_1_ = bf16[1,240,768]{2,1,0:T(8,128)(2,1)S(1)} collective-permute-done((bf16[1,240,768]{2,1,0:T(8,128)(2,1)S(1)}, bf16[1,240,768]{2,1,0:T(8,128)(2,1)S(1)}, u32[]{:S(2)}, u32[]{:S(2)}) %collective-permute-start.37) | collective-permute-done | bytes 368672 | tf_op jit(solution)/shard_map/ppermute | solution.py:21
  304.2 7.6 %collective-permute-done.41.refs_1_ = bf16[4,48,1024]{2,1,0:T(8,128)(2,1)S(1)} collective-permute-done((bf16[4,48,1024]{2,1,0:T(8,128)(2,1)S(1)}, bf16[4,48,1024]{2,1,0:T(8,128)(2,1)S(1)}, u32[]{:S(2)}, u32[]{:S(2)}) %collective-permute-start.41) | collective-permute-done | bytes 393248 | tf_op jit(solution)/shard_map/ppermute | solution.py:21
  312.3 3.4 collective-permute-start.44
  315.9 5.5 %collective-permute-done.43.refs_1_ = bf16[2,48,1024]{2,1,0:T(8,128)(2,1)S(1)} collective-permute-done((bf16[2,48,1024]{2,1,0:T(8,128)(2,1)S(1)}, bf16[2,48,1024]{2,1,0:T(8,128)(2,1)S(1)}, u32[]{:S(2)}, u32[]{:S(2)}) %collective-permute-start.43) | collective-permute-done | bytes 196640 | tf_op jit(solution)/shard_map/ppermute | solution.py:21
  321.5 7.3 %collective-permute-done.44.refs_1_ = bf16[1,48,1536]{2,1,0:T(8,128)(2,1)S(1)} collective-permute-done((bf16[1,48,1536]{2,1,0:T(8,128)(2,1)S(1)}, bf16[1,48,1536]{2,1,0:T(8,128)(2,1)S(1)}, u32[]{:S(2)}, u32[]{:S(2)}) %collective-permute-start.44) | collective-permute-done | bytes 147488 | tf_op jit(solution)/shard_map/ppermute | solution.py:21
  329.8 3.7 %collective-permute-done.45.refs_1_ = bf16[1,48,2304]{2,1,0:T(8,128)(2,1)S(1)} collective-permute-done((bf16[1,48,2304]{2,1,0:T(8,128)(2,1)S(1)}, bf16[1,48,2304]{2,1,0:T(8,128)(2,1)S(1)}, u32[]{:S(2)}, u32[]{:S(2)}) %collective-permute-start.45) | collective-permute-done | bytes 221216 | tf_op jit(solution)/shard_map/ppermute | solution.py:21
  333.6 2.2 collective-permute-done.47.refs_1_
  335.8 1.6 collective-permute-start.50
  340.4 3.0 collective-permute-done.49
  346.5 2.1 shard_map.459
  (265 shorter events, 54.0 us)
Async XLA Ops:
  1.6 15.7 %collective-permute-start = (bf16[1,48,1152]{2,1,0:T(8,128)(2,1)S(1)}, bf16[1,48,1152]{2,1,0:T(8,128)(2,1)S(1)}, u32[]{:S(2)}, u32[]{:S(2)}) collective-permute-start(bf16[1,48,1152]{2,1,0:T(8,128)(2,1)S(1)} %dynamic-slice_bitcast_fusion.refs_0_), channel_id=1, source_target_pairs={{0,8},{1,9},{2,10},{3,11},{4,12},{5,13},{6,14},{7,15},{8,0},{9,1},... | collective-permute-start | bytes 331784 | tf_op jit(solution)/shard_map/ppermute | solution.py:21
  12.8 10.8 %collective-permute-start.2 = (bf16[1,48,1024]{2,1,0:T(8,128)(2,1)}, bf16[1,48,1024]{2,1,0:T(8,128)(2,1)S(1)}, u32[]{:S(2)}, u32[]{:S(2)}) collective-permute-start(bf16[1,48,1024]{2,1,0:T(8,128)(2,1)} %bitcast.53), channel_id=1, source_target_pairs={{0,8},{1,9},{2,10},{3,11},{4,12},{5,13},{6,14},{7,15},{8,0},{9,1},... | collective-permute-start | bytes 294920 | tf_op jit(solution)/shard_map/ppermute | solution.py:21
  12.9 11.8 %collective-permute-start.1 = (bf16[1,48,1024]{2,1,0:T(8,128)(2,1)}, bf16[1,48,1024]{2,1,0:T(8,128)(2,1)S(1)}, u32[]{:S(2)}, u32[]{:S(2)}) collective-permute-start(bf16[1,48,1024]{2,1,0:T(8,128)(2,1)} %bitcast.55), channel_id=1, source_target_pairs={{0,8},{1,9},{2,10},{3,11},{4,12},{5,13},{6,14},{7,15},{8,0},{9,1},... | collective-permute-start | bytes 294920 | tf_op jit(solution)/shard_map/ppermute | solution.py:21
  17.4 9.5 %collective-permute-start.3 = (bf16[2,48,1152]{2,1,0:T(8,128)(2,1)S(1)}, bf16[2,48,1152]{2,1,0:T(8,128)(2,1)S(1)}, u32[]{:S(2)}, u32[]{:S(2)}) collective-permute-start(bf16[2,48,1152]{2,1,0:T(8,128)(2,1)S(1)} %shard_map.419.refs_0_), channel_id=1, source_target_pairs={{0,4},{1,5},{2,6},{3,7},{4,0},{5,1},{6,2},{7,3},{8,12},{9,13},{10,... | collective-permute-start | bytes 663560 | tf_op jit(solution)/shard_map/ppermute | solution.py:21
  26.9 16.2 %collective-permute-start.7 = (bf16[4,48,1152]{2,1,0:T(8,128)(2,1)S(1)}, bf16[4,48,1152]{2,1,0:T(8,128)(2,1)S(1)}, u32[]{:S(2)}, u32[]{:S(2)}) collective-permute-start(bf16[4,48,1152]{2,1,0:T(8,128)(2,1)S(1)} %shard_map.422.refs_0_), channel_id=1, source_target_pairs={{0,16},{16,0},{1,17},{17,1},{2,18},{18,2},{3,19},{19,3},{4,20},{20... | collective-permute-start | bytes 1327112 | tf_op jit(solution)/shard_map/ppermute | solution.py:21
  28.5 14.6 %collective-permute-start.6 = (bf16[4,48,1152]{2,1,0:T(8,128)(2,1)S(1)}, bf16[4,48,1152]{2,1,0:T(8,128)(2,1)S(1)}, u32[]{:S(2)}, u32[]{:S(2)}) collective-permute-start(bf16[4,48,1152]{2,1,0:T(8,128)(2,1)S(1)} %shard_map.422.refs_0_), channel_id=1, source_target_pairs={{0,2},{1,3},{2,0},{3,1},{4,6},{5,7},{6,4},{7,5},{8,10},{9,11},{10,... | collective-permute-start | bytes 1327112 | tf_op jit(solution)/shard_map/ppermute | solution.py:21
  30.0 10.9 %collective-permute-start.4 = (bf16[2,48,1024]{2,1,0:T(8,128)(2,1)S(1)}, bf16[2,48,1024]{2,1,0:T(8,128)(2,1)S(1)}, u32[]{:S(2)}, u32[]{:S(2)}) collective-permute-start(bf16[2,48,1024]{2,1,0:T(8,128)(2,1)S(1)} %shard_map.420.refs_0_), channel_id=1, source_target_pairs={{0,4},{1,5},{2,6},{3,7},{4,0},{5,1},{6,2},{7,3},{8,12},{9,13},{10,... | collective-permute-start | bytes 589832 | tf_op jit(solution)/shard_map/ppermute | solution.py:21
  30.1 12.9 %collective-permute-start.5 = (bf16[2,48,1024]{2,1,0:T(8,128)(2,1)S(1)}, bf16[2,48,1024]{2,1,0:T(8,128)(2,1)S(1)}, u32[]{:S(2)}, u32[]{:S(2)}) collective-permute-start(bf16[2,48,1024]{2,1,0:T(8,128)(2,1)S(1)} %shard_map.421.refs_0_), channel_id=1, source_target_pairs={{0,4},{1,5},{2,6},{3,7},{4,0},{5,1},{6,2},{7,3},{8,12},{9,13},{10,... | collective-permute-start | bytes 589832 | tf_op jit(solution)/shard_map/ppermute | solution.py:21
  32.3 10.8 %collective-permute-start.8 = (bf16[1,48,1920]{2,1,0:T(8,128)(2,1)S(1)}, bf16[1,48,1920]{2,1,0:T(8,128)(2,1)S(1)}, u32[]{:S(2)}, u32[]{:S(2)}) collective-permute-start(bf16[1,48,1920]{2,1,0:T(8,128)(2,1)S(1)} %fusion.4.refs_0_), channel_id=1, source_target_pairs={{0,8},{1,9},{2,10},{3,11},{4,12},{5,13},{6,14},{7,15},{8,0},{9,1},... | collective-permute-start | bytes 552968 | tf_op jit(solution)/shard_map/ppermute | solution.py:21
  43.1 16.5 %collective-permute-start.11 = (bf16[4,48,1152]{2,1,0:T(8,128)(2,1)S(1)}, bf16[4,48,1152]{2,1,0:T(8,128)(2,1)S(1)}, u32[]{:S(2)}, u32[]{:S(2)}) collective-permute-start(bf16[4,48,1152]{2,1,0:T(8,128)(2,1)S(1)} %collective-permute-done.6.refs_1_), channel_id=1, source_target_pairs={{0,16},{16,0},{1,17},{17,1},{2,18},{18,2},{3,19},{19,3},{4,20},{20... | collective-permute-start | bytes 1327112 | tf_op jit(solution)/shard_map/ppermute | solution.py:21
  43.7 13.7 %collective-permute-start.9 = (bf16[4,48,1024]{2,1,0:T(8,128)(2,1)S(1)}, bf16[4,48,1024]{2,1,0:T(8,128)(2,1)S(1)}, u32[]{:S(2)}, u32[]{:S(2)}) collective-permute-start(bf16[4,48,1024]{2,1,0:T(8,128)(2,1)S(1)} %shard_map.423.refs_0_), channel_id=1, source_target_pairs={{0,2},{1,3},{2,0},{3,1},{4,6},{5,7},{6,4},{7,5},{8,10},{9,11},{10,... | collective-permute-start | bytes 1179656 | tf_op jit(solution)/shard_map/ppermute | solution.py:21
  44.3 15.4 %collective-permute-start.10 = (bf16[4,48,1024]{2,1,0:T(8,128)(2,1)S(1)}, bf16[4,48,1024]{2,1,0:T(8,128)(2,1)S(1)}, u32[]{:S(2)}, u32[]{:S(2)}) collective-permute-start(bf16[4,48,1024]{2,1,0:T(8,128)(2,1)S(1)} %shard_map.424.refs_0_), channel_id=1, source_target_pairs={{0,2},{1,3},{2,0},{3,1},{4,6},{5,7},{6,4},{7,5},{8,10},{9,11},{10,... | collective-permute-start | bytes 1179656 | tf_op jit(solution)/shard_map/ppermute | solution.py:21
  45.7 13.9 %collective-permute-start.13 = (bf16[2,48,1920]{2,1,0:T(8,128)(2,1)S(1)}, bf16[2,48,1920]{2,1,0:T(8,128)(2,1)S(1)}, u32[]{:S(2)}, u32[]{:S(2)}) collective-permute-start(bf16[2,48,1920]{2,1,0:T(8,128)(2,1)S(1)} %shard_map.425.refs_0_), channel_id=1, source_target_pairs={{0,4},{1,5},{2,6},{3,7},{4,0},{5,1},{6,2},{7,3},{8,12},{9,13},{10,... | collective-permute-start | bytes 1105928 | tf_op jit(solution)/shard_map/ppermute | solution.py:21
  46.7 10.7 %collective-permute-start.12 = (bf16[1,192,768]{2,1,0:T(8,128)(2,1)S(1)}, bf16[1,192,768]{2,1,0:T(8,128)(2,1)S(1)}, u32[]{:S(2)}, u32[]{:S(2)}) collective-permute-start(bf16[1,192,768]{2,1,0:T(8,128)(2,1)S(1)} %bitcast.51), channel_id=1, source_target_pairs={{0,8},{1,9},{2,10},{3,11},{4,12},{5,13},{6,14},{7,15},{8,0},{9,1},... | collective-permute-start | bytes 884744 | tf_op jit(solution)/shard_map/ppermute | solution.py:21
  63.1 6.9 %collective-permute-start.16 = (bf16[8,48,1152]{2,1,0:T(8,128)(2,1)S(1)}, bf16[8,48,1152]{2,1,0:T(8,128)(2,1)}, u32[]{:S(2)}, u32[]{:S(2)}) collective-permute-start(bf16[8,48,1152]{2,1,0:T(8,128)(2,1)S(1)} %shard_map.429.refs_8_.refs_11_), channel_id=1, source_target_pairs={{0,1},{1,0},{2,3},{3,2},{4,5},{5,4},{6,7},{7,6},{8,9},{9,8},{10,11... | collective-permute-start | bytes 2654216 | tf_op jit(solution)/shard_map/ppermute | solution.py:21
  63.2 6.8 %collective-permute-start.17 = (bf16[8,48,1152]{2,1,0:T(8,128)(2,1)S(1)}, bf16[8,48,1152]{2,1,0:T(8,128)(2,1)}, u32[]{:S(2)}, u32[]{:S(2)}) collective-permute-start(bf16[8,48,1152]{2,1,0:T(8,128)(2,1)S(1)} %shard_map.430.refs_9_.refs_12_), channel_id=1, source_target_pairs={{0,1},{1,0},{2,3},{3,2},{4,5},{5,4},{6,7},{7,6},{8,9},{9,8},{10,11... | collective-permute-start | bytes 2654216 | tf_op jit(solution)/shard_map/ppermute | solution.py:21
  63.6 23.6 %collective-permute-start.19 = (bf16[4,48,1920]{2,1,0:T(8,128)(2,1)}, bf16[4,48,1920]{2,1,0:T(8,128)(2,1)}, u32[]{:S(2)}, u32[]{:S(2)}) collective-permute-start(bf16[4,48,1920]{2,1,0:T(8,128)(2,1)} %shard_map.432.refs_4_), channel_id=1, source_target_pairs={{0,16},{16,0},{1,17},{17,1},{2,18},{18,2},{3,19},{19,3},{4,20},{20... | collective-permute-start | bytes 2211848 | tf_op jit(solution)/shard_map/ppermute | solution.py:21
  65.1 22.1 %collective-permute-start.18 = (bf16[4,48,1920]{2,1,0:T(8,128)(2,1)}, bf16[4,48,1920]{2,1,0:T(8,128)(2,1)}, u32[]{:S(2)}, u32[]{:S(2)}) collective-permute-start(bf16[4,48,1920]{2,1,0:T(8,128)(2,1)} %shard_map.432.refs_4_), channel_id=1, source_target_pairs={{0,2},{1,3},{2,0},{3,1},{4,6},{5,7},{6,4},{7,5},{8,10},{9,11},{10,... | collective-permute-start | bytes 2211848 | tf_op jit(solution)/shard_map/ppermute | solution.py:21
  68.0 19.2 %collective-permute-start.20 = (bf16[2,192,768]{2,1,0:T(8,128)(2,1)}, bf16[2,192,768]{2,1,0:T(8,128)(2,1)S(1)}, u32[]{:S(2)}, u32[]{:S(2)}) collective-permute-start(bf16[2,192,768]{2,1,0:T(8,128)(2,1)} %shard_map.431.refs_0_), channel_id=1, source_target_pairs={{0,4},{1,5},{2,6},{3,7},{4,0},{5,1},{6,2},{7,3},{8,12},{9,13},{10,... | collective-permute-start | bytes 1769480 | tf_op jit(solution)/shard_map/ppermute | solution.py:21
  88.4 27.8 %collective-permute-start.22 = (bf16[4,192,768]{2,1,0:T(8,128)(2,1)S(1)}, bf16[4,192,768]{2,1,0:T(8,128)(2,1)S(1)}, u32[]{:S(2)}, u32[]{:S(2)}) collective-permute-start(bf16[4,192,768]{2,1,0:T(8,128)(2,1)S(1)} %shard_map.434.refs_12_), channel_id=1, source_target_pairs={{0,2},{1,3},{2,0},{3,1},{4,6},{5,7},{6,4},{7,5},{8,10},{9,11},{10,... | collective-permute-start | bytes 3538952 | tf_op jit(solution)/shard_map/ppermute | solution.py:21
  89.4 20.2 %collective-permute-start.21 = (bf16[4,48,1920]{2,1,0:T(8,128)(2,1)}, bf16[4,48,1920]{2,1,0:T(8,128)(2,1)}, u32[]{:S(2)}, u32[]{:S(2)}) collective-permute-start(bf16[4,48,1920]{2,1,0:T(8,128)(2,1)} %collective-permute-done.18.refs_5_), channel_id=1, source_target_pairs={{0,16},{16,0},{1,17},{17,1},{2,18},{18,2},{3,19},{19,3},{4,20},{20... | collective-permute-start | bytes 2211848 | tf_op jit(solution)/shard_map/ppermute | solution.py:21
  116.2 9.1 %collective-permute-start.27 = (bf16[4,192,768]{2,1,0:T(8,128)(2,1)S(1)}, bf16[4,192,768]{2,1,0:T(8,128)(2,1)S(1)}, u32[]{:S(2)}, u32[]{:S(2)}) collective-permute-start(bf16[4,192,768]{2,1,0:T(8,128)(2,1)S(1)} %shard_map.434.refs_12_), channel_id=1, source_target_pairs={{0,1},{1,0},{2,3},{3,2},{4,5},{5,4},{6,7},{7,6},{8,9},{9,8},{10,11... | collective-permute-start | bytes 3538952 | tf_op jit(solution)/shard_map/ppermute | solution.py:21
  116.7 8.6 %collective-permute-start.28 = (bf16[4,192,768]{2,1,0:T(8,128)(2,1)S(1)}, bf16[4,192,768]{2,1,0:T(8,128)(2,1)}, u32[]{:S(2)}, u32[]{:S(2)}) collective-permute-start(bf16[4,192,768]{2,1,0:T(8,128)(2,1)S(1)} %collective-permute-done.22.refs_13_), channel_id=1, source_target_pairs={{0,1},{1,0},{2,3},{3,2},{4,5},{5,4},{6,7},{7,6},{8,9},{9,8},{10,11... | collective-permute-start | bytes 3538952 | tf_op jit(solution)/shard_map/ppermute | solution.py:21
  116.8 6.4 %collective-permute-start.24 = (bf16[4,48,1920]{2,1,0:T(8,128)(2,1)}, bf16[4,48,1920]{2,1,0:T(8,128)(2,1)}, u32[]{:S(2)}, u32[]{:S(2)}) collective-permute-start(bf16[4,48,1920]{2,1,0:T(8,128)(2,1)} %collective-permute-done.18.refs_5_), channel_id=1, source_target_pairs={{0,1},{1,0},{2,3},{3,2},{4,5},{5,4},{6,7},{7,6},{8,9},{9,8},{10,11... | collective-permute-start | bytes 2211848 | tf_op jit(solution)/shard_map/ppermute | solution.py:21
  117.2 7.0 %collective-permute-start.25 = (bf16[4,48,1920]{2,1,0:T(8,128)(2,1)}, bf16[4,48,1920]{2,1,0:T(8,128)(2,1)}, u32[]{:S(2)}, u32[]{:S(2)}) collective-permute-start(bf16[4,48,1920]{2,1,0:T(8,128)(2,1)} %collective-permute-done.19.refs_6_), channel_id=1, source_target_pairs={{0,1},{1,0},{2,3},{3,2},{4,5},{5,4},{6,7},{7,6},{8,9},{9,8},{10,11... | collective-permute-start | bytes 2211848 | tf_op jit(solution)/shard_map/ppermute | solution.py:21
  119.1 6.2 %collective-permute-start.26 = (bf16[4,48,1920]{2,1,0:T(8,128)(2,1)}, bf16[4,48,1920]{2,1,0:T(8,128)(2,1)}, u32[]{:S(2)}, u32[]{:S(2)}) collective-permute-start(bf16[4,48,1920]{2,1,0:T(8,128)(2,1)} %collective-permute-done.21.refs_7_), channel_id=1, source_target_pairs={{0,1},{1,0},{2,3},{3,2},{4,5},{5,4},{6,7},{7,6},{8,9},{9,8},{10,11... | collective-permute-start | bytes 2211848 | tf_op jit(solution)/shard_map/ppermute | solution.py:21
  195.2 9.5 %collective-permute-start.29 = (bf16[8,240,768]{2,1,0:T(8,128)(2,1)}, bf16[8,240,768]{2,1,0:T(8,128)(2,1)S(1)}, u32[]{:S(2)}, u32[]{:S(2)}) collective-permute-start(bf16[8,240,768]{2,1,0:T(8,128)(2,1)} %get-tuple-element.501), channel_id=1, source_target_pairs={{0,1},{1,0},{2,3},{3,2},{4,5},{5,4},{6,7},{7,6},{8,9},{9,8},{10,11... | collective-permute-start | bytes 8847368 | tf_op jit(solution)/shard_map/ppermute | solution.py:21
  195.3 9.4 %collective-permute-start.30 = (bf16[2,8,48,1536]{3,2,1,0:T(8,128)(2,1)}, bf16[2,8,48,1536]{3,2,1,0:T(8,128)(2,1)S(1)}, u32[]{:S(2)}, u32[]{:S(2)}) collective-permute-start(bf16[2,8,48,1536]{3,2,1,0:T(8,128)(2,1)} %get-tuple-element.502), channel_id=1, source_target_pairs={{0,1},{1,0},{2,3},{3,2},{4,5},{5,4},{6,7},{7,6},{8,9},{9,8},{10,11... | collective-permute-start | bytes 7077896 | tf_op jit(solution)/shard_map/ppermute | solution.py:21
  209.2 34.6 %collective-permute-start.31 = (bf16[4,240,768]{2,1,0:T(8,128)(2,1)}, bf16[4,240,768]{2,1,0:T(8,128)(2,1)}, u32[]{:S(2)}, u32[]{:S(2)}) collective-permute-start(bf16[4,240,768]{2,1,0:T(8,128)(2,1)} %get-tuple-element.513), channel_id=1, source_target_pairs={{0,2},{1,3},{2,0},{3,1},{4,6},{5,7},{6,4},{7,5},{8,10},{9,11},{10,... | collective-permute-start | bytes 4423688 | tf_op jit(solution)/shard_map/ppermute | solution.py:21
  210.1 33.4 %collective-permute-start.32 = (bf16[8,48,1536]{2,1,0:T(8,128)(2,1)}, bf16[8,48,1536]{2,1,0:T(8,128)(2,1)}, u32[]{:S(2)}, u32[]{:S(2)}) collective-permute-start(bf16[8,48,1536]{2,1,0:T(8,128)(2,1)} %get-tuple-element.514), channel_id=1, source_target_pairs={{0,16},{16,0},{1,17},{17,1},{2,18},{18,2},{3,19},{19,3},{4,20},{20... | collective-permute-start | bytes 3538952 | tf_op jit(solution)/shard_map/ppermute | solution.py:21
  247.4 26.1 %collective-permute-start.33 = (bf16[2,240,768]{2,1,0:T(8,128)(2,1)S(1)}, bf16[2,240,768]{2,1,0:T(8,128)(2,1)S(1)}, u32[]{:S(2)}, u32[]{:S(2)}) collective-permute-start(bf16[2,240,768]{2,1,0:T(8,128)(2,1)S(1)} %get-tuple-element.533), channel_id=1, source_target_pairs={{0,4},{1,5},{2,6},{3,7},{4,0},{5,1},{6,2},{7,3},{8,12},{9,13},{10,... | collective-permute-start | bytes 2211848 | tf_op jit(solution)/shard_map/ppermute | solution.py:21
  248.1 25.4 %collective-permute-start.34 = (bf16[4,48,1536]{2,1,0:T(8,128)(2,1)S(1)}, bf16[4,48,1536]{2,1,0:T(8,128)(2,1)S(1)}, u32[]{:S(2)}, u32[]{:S(2)}) collective-permute-start(bf16[4,48,1536]{2,1,0:T(8,128)(2,1)S(1)} %get-tuple-element.534), channel_id=1, source_target_pairs={{0,2},{1,3},{2,0},{3,1},{4,6},{5,7},{6,4},{7,5},{8,10},{9,11},{10,... | collective-permute-start | bytes 1769480 | tf_op jit(solution)/shard_map/ppermute | solution.py:21
  273.5 5.7 %collective-permute-start.35 = (bf16[8,48,2304]{2,1,0:T(8,128)(2,1)}, bf16[8,48,2304]{2,1,0:T(8,128)(2,1)S(1)}, u32[]{:S(2)}, u32[]{:S(2)}) collective-permute-start(bf16[8,48,2304]{2,1,0:T(8,128)(2,1)} %get-tuple-element.546), channel_id=1, source_target_pairs={{0,1},{1,0},{2,3},{3,2},{4,5},{5,4},{6,7},{7,6},{8,9},{9,8},{10,11... | collective-permute-start | bytes 5308424 | tf_op jit(solution)/shard_map/ppermute | solution.py:21
  273.6 6.9 %collective-permute-start.36 = (bf16[2,8,48,1024]{3,2,1,0:T(8,128)(2,1)S(1)}, bf16[2,8,48,1024]{3,2,1,0:T(8,128)(2,1)S(1)}, u32[]{:S(2)}, u32[]{:S(2)}) collective-permute-start(bf16[2,8,48,1024]{3,2,1,0:T(8,128)(2,1)S(1)} %get-tuple-element.552), channel_id=1, source_target_pairs={{0,1},{1,0},{2,3},{3,2},{4,5},{5,4},{6,7},{7,6},{8,9},{9,8},{10,11... | collective-permute-start | bytes 4718600 | tf_op jit(solution)/shard_map/ppermute | solution.py:21
  279.7 22.6 %collective-permute-start.40 = (bf16[4,48,2304]{2,1,0:T(8,128)(2,1)S(1)}, bf16[4,48,2304]{2,1,0:T(8,128)(2,1)S(1)}, u32[]{:S(2)}, u32[]{:S(2)}) collective-permute-start(bf16[4,48,2304]{2,1,0:T(8,128)(2,1)S(1)} %get-tuple-element.584), channel_id=1, source_target_pairs={{0,2},{1,3},{2,0},{3,1},{4,6},{5,7},{6,4},{7,5},{8,10},{9,11},{10,... | collective-permute-start | bytes 2654216 | tf_op jit(solution)/shard_map/ppermute | solution.py:21
  280.8 20.6 %collective-permute-start.39 = (bf16[8,48,1024]{2,1,0:T(8,128)(2,1)S(1)}, bf16[8,48,1024]{2,1,0:T(8,128)(2,1)S(1)}, u32[]{:S(2)}, u32[]{:S(2)}) collective-permute-start(bf16[8,48,1024]{2,1,0:T(8,128)(2,1)S(1)} %get-tuple-element.574), channel_id=1, source_target_pairs={{0,16},{16,0},{1,17},{17,1},{2,18},{18,2},{3,19},{19,3},{4,20},{20... | collective-permute-start | bytes 2359304 | tf_op jit(solution)/shard_map/ppermute | solution.py:21
  282.4 18.9 %collective-permute-start.37 = (bf16[1,240,768]{2,1,0:T(8,128)(2,1)S(1)}, bf16[1,240,768]{2,1,0:T(8,128)(2,1)S(1)}, u32[]{:S(2)}, u32[]{:S(2)}) collective-permute-start(bf16[1,240,768]{2,1,0:T(8,128)(2,1)S(1)} %get-tuple-element.561), channel_id=1, source_target_pairs={{0,8},{1,9},{2,10},{3,11},{4,12},{5,13},{6,14},{7,15},{8,0},{9,1},... | collective-permute-start | bytes 1105928 | tf_op jit(solution)/shard_map/ppermute | solution.py:21
  283.8 14.0 %collective-permute-start.38 = (bf16[2,48,1536]{2,1,0:T(8,128)(2,1)S(1)}, bf16[2,48,1536]{2,1,0:T(8,128)(2,1)S(1)}, u32[]{:S(2)}, u32[]{:S(2)}) collective-permute-start(bf16[2,48,1536]{2,1,0:T(8,128)(2,1)S(1)} %get-tuple-element.562), channel_id=1, source_target_pairs={{0,4},{1,5},{2,6},{3,7},{4,0},{5,1},{6,2},{7,3},{8,12},{9,13},{10,... | collective-permute-start | bytes 884744 | tf_op jit(solution)/shard_map/ppermute | solution.py:21
  301.6 10.2 %collective-permute-start.41 = (bf16[4,48,1024]{2,1,0:T(8,128)(2,1)S(1)}, bf16[4,48,1024]{2,1,0:T(8,128)(2,1)S(1)}, u32[]{:S(2)}, u32[]{:S(2)}) collective-permute-start(bf16[4,48,1024]{2,1,0:T(8,128)(2,1)S(1)} %get-tuple-element.594), channel_id=1, source_target_pairs={{0,2},{1,3},{2,0},{3,1},{4,6},{5,7},{6,4},{7,5},{8,10},{9,11},{10,... | collective-permute-start | bytes 1179656 | tf_op jit(solution)/shard_map/ppermute | solution.py:21
  302.4 13.3 %collective-permute-start.42 = (bf16[2,48,2304]{2,1,0:T(8,128)(2,1)S(1)}, bf16[2,48,2304]{2,1,0:T(8,128)(2,1)S(1)}, u32[]{:S(2)}, u32[]{:S(2)}) collective-permute-start(bf16[2,48,2304]{2,1,0:T(8,128)(2,1)S(1)} %get-tuple-element.604), channel_id=1, source_target_pairs={{0,4},{1,5},{2,6},{3,7},{4,0},{5,1},{6,2},{7,3},{8,12},{9,13},{10,... | collective-permute-start | bytes 1327112 | tf_op jit(solution)/shard_map/ppermute | solution.py:21
  303.4 30.1 %collective-permute-start.46 = (bf16[240,768]{1,0:T(8,128)(2,1)S(1)}, bf16[240,768]{1,0:T(8,128)(2,1)S(1)}, u32[]{:S(2)}, u32[]{:S(2)}) collective-permute-start(bf16[240,768]{1,0:T(8,128)(2,1)S(1)} %bitcast.47), channel_id=1, source_target_pairs={{0,16},{16,0},{1,17},{17,1},{2,18},{18,2},{3,19},{19,3},{4,20},{20... | collective-permute-start | bytes 1105928 | tf_op jit(solution)/shard_map/ppermute | solution.py:21
  311.9 9.5 %collective-permute-start.43 = (bf16[2,48,1024]{2,1,0:T(8,128)(2,1)S(1)}, bf16[2,48,1024]{2,1,0:T(8,128)(2,1)S(1)}, u32[]{:S(2)}, u32[]{:S(2)}) collective-permute-start(bf16[2,48,1024]{2,1,0:T(8,128)(2,1)S(1)} %get-tuple-element.614), channel_id=1, source_target_pairs={{0,4},{1,5},{2,6},{3,7},{4,0},{5,1},{6,2},{7,3},{8,12},{9,13},{10,... | collective-permute-start | bytes 589832 | tf_op jit(solution)/shard_map/ppermute | solution.py:21
  312.3 16.4 %collective-permute-start.44 = (bf16[1,48,1536]{2,1,0:T(8,128)(2,1)S(1)}, bf16[1,48,1536]{2,1,0:T(8,128)(2,1)S(1)}, u32[]{:S(2)}, u32[]{:S(2)}) collective-permute-start(bf16[1,48,1536]{2,1,0:T(8,128)(2,1)S(1)} %get-tuple-element.624), channel_id=1, source_target_pairs={{0,8},{1,9},{2,10},{3,11},{4,12},{5,13},{6,14},{7,15},{8,0},{9,1},... | collective-permute-start | bytes 442376 | tf_op jit(solution)/shard_map/ppermute | solution.py:21
  315.8 17.7 %collective-permute-start.45 = (bf16[1,48,2304]{2,1,0:T(8,128)(2,1)S(1)}, bf16[1,48,2304]{2,1,0:T(8,128)(2,1)S(1)}, u32[]{:S(2)}, u32[]{:S(2)}) collective-permute-start(bf16[1,48,2304]{2,1,0:T(8,128)(2,1)S(1)} %get-tuple-element.633), channel_id=1, source_target_pairs={{0,8},{1,9},{2,10},{3,11},{4,12},{5,13},{6,14},{7,15},{8,0},{9,1},... | collective-permute-start | bytes 663560 | tf_op jit(solution)/shard_map/ppermute | solution.py:21
  328.8 7.0 %collective-permute-start.48 = (bf16[48,1536]{1,0:T(8,128)(2,1)S(1)}, bf16[48,1536]{1,0:T(8,128)(2,1)S(1)}, u32[]{:S(2)}, u32[]{:S(2)}) collective-permute-start(bf16[48,1536]{1,0:T(8,128)(2,1)S(1)} %bitcast.49), channel_id=1, source_target_pairs={{0,16},{16,0},{1,17},{17,1},{2,18},{18,2},{3,19},{19,3},{4,20},{20... | collective-permute-start | bytes 442376 | tf_op jit(solution)/shard_map/ppermute | solution.py:21
  329.8 6.0 %collective-permute-start.47 = (bf16[1,48,1024]{2,1,0:T(8,128)(2,1)S(1)}, bf16[1,48,1024]{2,1,0:T(8,128)(2,1)S(1)}, u32[]{:S(2)}, u32[]{:S(2)}) collective-permute-start(bf16[1,48,1024]{2,1,0:T(8,128)(2,1)S(1)} %get-tuple-element.649), channel_id=1, source_target_pairs={{0,8},{1,9},{2,10},{3,11},{4,12},{5,13},{6,14},{7,15},{8,0},{9,1},... | collective-permute-start | bytes 294920 | tf_op jit(solution)/shard_map/ppermute | solution.py:21
  335.8 7.6 %collective-permute-start.50 = (bf16[48,1024]{1,0:T(8,128)(2,1)S(1)}, bf16[48,1024]{1,0:T(8,128)(2,1)S(1)}, u32[]{:S(2)}, u32[]{:S(2)}) collective-permute-start(bf16[48,1024]{1,0:T(8,128)(2,1)S(1)} %bitcast.50), channel_id=1, source_target_pairs={{0,16},{16,0},{1,17},{17,1},{2,18},{18,2},{3,19},{19,3},{4,20},{20... | collective-permute-start | bytes 294920 | tf_op jit(solution)/shard_map/ppermute | solution.py:21
  337.4 5.9 %collective-permute-start.49 = (bf16[48,2304]{1,0:T(8,128)(2,1)S(1)}, bf16[48,2304]{1,0:T(8,128)(2,1)S(1)}, u32[]{:S(2)}, u32[]{:S(2)}) collective-permute-start(bf16[48,2304]{1,0:T(8,128)(2,1)S(1)} %bitcast.48), channel_id=1, source_target_pairs={{0,16},{16,0},{1,17},{17,1},{2,18},{18,2},{3,19},{19,3},{4,20},{20... | collective-permute-start | bytes 663560 | tf_op jit(solution)/shard_map/ppermute | solution.py:21
  (68 other events, 732.0 us)
